TPU v7x, 32 devices: a whole 2x2x4 slice. The times are simulated.
32 devices in a mesh: group: 4 (over x, core), ctx: 8 (over z, y).
Axes of the slice: x: 2, y: 2, z: 4, core: 2. Of those that a mesh axis runs over, the one named last changes fastest.
Arguments:
- series: bfloat16 [8192, 768], P(('group', 'ctx')), may hold values from -6 to 6
- recon_mask: int32 [8192], P(('group', 'ctx')), may hold values 0 or 1
- mask_token: bfloat16 [768], replicated, may hold values from -4 to 4
- packing_list: int32 [128], P(('group', 'ctx')), may hold values from 0 to 3, as said below
- doc_ids: int32 [4, 2048], P('group', 'ctx'), may hold values from 0 to 3, never falling along the last dimension, each value on 1 to 1280 neighbouring positions
- norm_gain: bfloat16 [768], replicated, may hold values from 0.099609375 to 1.8984375
- w_query: bfloat16 [768, 768], replicated
- w_key: bfloat16 [768, 768], replicated
- w_value: bfloat16 [768, 768], replicated, may hold values from -0.21875 to 0.21875
- w_out: bfloat16 [768, 768], replicated, may hold values from -0.21875 to 0.21875
Outputs:
- encoded: bfloat16 [8192, 768], P(('group', 'ctx'))
Inputs may be any that keep to these rules, and one draw needn't show every extreme that they name: `packing_list`: the 4 consecutive entries of each arrival block (one device of the arrival layout) name every packed group exactly once.
All inputs are finite; a program needn't handle non-finite values. No bound on the sum of `recon_mask` on one device may be relied on, other than what follows from the above.
Results may differ from a plain program's by a relative error of at most 0.005.
Values may be sent and summed in bfloat16 or wider, within the bound.
No kernel may reach another device: no remote copies, remote signals or barrier semaphores. Data moves between devices by JAX's collectives and lax.ppermute only.
A program may use at most 128 MiB of HBM per device.

v0:
```python
import math

import jax
import jax.numpy as jnp
from jax import lax
from jax.sharding import PartitionSpec as P

HEADS = 12
HD = 64


NEGATIVE = -1e30


def rms_normed(values, gain):
    widened = values.astype(jnp.float32)
    factor = lax.rsqrt(jnp.mean(widened * widened, axis=-1, keepdims=True) + 1e-06)
    return (widened * factor * gain.astype(jnp.float32)[None, :]).astype(jnp.bfloat16)


def softmax_update(carried, query, query_doc, key_rows, value_rows, key_doc):
    maxima, totals, running = carried
    key_count = key_rows.shape[0]
    head_query = query.reshape(query.shape[0], HEADS, HD)
    head_key = key_rows.reshape(key_count, HEADS, HD)
    head_value = value_rows.reshape(key_count, HEADS, HD)
    scores = jnp.einsum(
        "qhd,khd->hqk", head_query, head_key, preferred_element_type=jnp.float32
    ) * (1.0 / math.sqrt(HD))
    allowed = (query_doc[:, None] == key_doc[None, :])[None]
    scores = jnp.where(allowed, scores, NEGATIVE)
    newmax = jnp.maximum(maxima, jnp.max(scores, axis=-1))
    expo = jnp.where(allowed, jnp.exp(scores - newmax[..., None]), 0.0)
    factor = jnp.exp(maxima - newmax)
    totals = totals * factor + jnp.sum(expo, axis=-1)
    running = running * factor[..., None] + jnp.einsum(
        "hqk,khd->hqd", expo.astype(jnp.bfloat16), head_value, preferred_element_type=jnp.float32
    )
    return (newmax, totals, running)


def visit_tiles(carried, tile_source, project, query, query_doc):
    total_rows = tile_source[0].shape[0]
    tile_rows = math.gcd(total_rows, 512)
    tile_count = total_rows // tile_rows
    stacked = tuple(
        (member.reshape((tile_count, tile_rows) + member.shape[1:]) for member in tile_source)
    )

    def one_tile(status, tile_parts):
        tile_doc = tile_parts[-1].astype(jnp.int32)
        key_rows, value_rows = project(tile_parts)
        return (softmax_update(status, query, query_doc, key_rows, value_rows, tile_doc), None)

    carried, unused = lax.scan(one_tile, carried, stacked)
    return carried


def on_device(
    series, recon_mask, mask_token, packing_list, doc_ids, norm_gain, w_query, w_key, w_value, w_out
):
    groups = lax.axis_size("group")
    row_count, model_width = series.shape
    masked = jnp.where(recon_mask[:, None] == 1, mask_token[None, :], series)
    routing = (packing_list[None, :] == jnp.arange(groups, dtype=jnp.int32)[:, None]).astype(
        jnp.bfloat16
    )
    ordered = jnp.dot(
        routing, masked.reshape(groups, -1), preferred_element_type=jnp.float32
    ).astype(jnp.bfloat16)
    packed = lax.all_to_all(ordered, "group", split_axis=0, concat_axis=0, tiled=True).reshape(
        row_count, model_width
    )
    normed = rms_normed(packed, norm_gain)
    query = jnp.dot(normed, w_query, preferred_element_type=jnp.float32).astype(jnp.bfloat16)
    query_doc = doc_ids.reshape(-1)
    doc_wire = query_doc.astype(jnp.bfloat16)
    start_carry = (
        jnp.full((HEADS, row_count), NEGATIVE, jnp.float32),
        jnp.zeros((HEADS, row_count), jnp.float32),
        jnp.zeros((HEADS, row_count, HD), jnp.float32),
    )
    keys_local = jnp.dot(normed, w_key, preferred_element_type=jnp.float32).astype(jnp.bfloat16)
    values_local = jnp.dot(normed, w_value, preferred_element_type=jnp.float32).astype(jnp.bfloat16)

    def direct(tile_parts):
        return (tile_parts[0], tile_parts[1])

    maxima, totals, running = visit_tiles(
        start_carry,
        (
            lax.all_gather(keys_local, "ctx", axis=0, tiled=True),
            lax.all_gather(values_local, "ctx", axis=0, tiled=True),
            lax.all_gather(doc_wire, "ctx", axis=0, tiled=True),
        ),
        direct,
        query,
        query_doc,
    )
    attended = (
        (running / totals[..., None])
        .transpose(1, 0, 2)
        .reshape(row_count, model_width)
        .astype(jnp.bfloat16)
    )
    mixed = jnp.dot(attended, w_out, preferred_element_type=jnp.float32)
    out_packed = (packed.astype(jnp.float32) + mixed).astype(jnp.bfloat16)
    returned = lax.all_to_all(
        out_packed.reshape(groups, -1), "group", split_axis=0, concat_axis=0, tiled=True
    )
    arrival = jnp.dot(routing.T, returned, preferred_element_type=jnp.float32).astype(jnp.bfloat16)
    return arrival.reshape(row_count, model_width)


def solution(mesh):
    in_specs = (
        P(("group", "ctx"), None),
        P(("group", "ctx")),
        P(),
        P(("group", "ctx")),
        P("group", "ctx"),
        P(),
        P(),
        P(),
        P(),
        P(),
    )
    out_specs = P(("group", "ctx"), None)
    return jax.shard_map(
        on_device, mesh=mesh, in_specs=in_specs, out_specs=out_specs, check_vma=False
    )
```

profile of v0, /device:TPU:0, one launch (start us, length us, event | category | flops | bytes accessed | tf_op | source)
XLA Modules:
  0.0 219.8 jit_solution(5513176825322404319)
XLA Ops:
  12.6 4.2 %all-to-all-start = ((bf16[4,2,24576]{2,1,0:T(2,128)(2,1)}), bf16[4,2,24576]{2,1,0:T(2,128)(2,1)S(1)}, u32[]{:S(2)}, u32[]{:S(2)}) async-start(bf16[4,2,24576]{2,1,0:T(2,128)(2,1)} %reshape.102), calls=%async_computation | async-start | bytes 786432 | tf_op jit(solution)/shard_map/all_to_all | solution.py:71
  17.5 6.8 %all-to-all-done = bf16[4,2,24576]{2,1,0:T(2,128)(2,1)S(1)} async-done(((bf16[4,2,24576]{2,1,0:T(2,128)(2,1)}), bf16[4,2,24576]{2,1,0:T(2,128)(2,1)S(1)}, u32[]{:S(2)}, u32[]{:S(2)}) %all-to-all-start) | async-done | bytes 393248 | tf_op jit(solution)/shard_map/all_to_all | solution.py:71
  24.6 2.4 %convert_reduce_fusion = f32[4,49152]{1,0:T(4,128)S(1)} fusion(bf16[4,1,49152]{2,1,0:T(2,128)(2,1)S(1)} %reshape.103), kind=kLoop, calls=%fused_computation.28 | loop fusion | flops 196608 | bytes 1179648 | tf_op jit(solution)/shard_map/convert_element_type | solution.py:107
  29.2 2.5 %convolution_convert_fusion.4 = bf16[256,768]{1,0:T(8,128)(2,1)} fusion(bf16[256,768]{1,0:T(8,128)(2,1)S(1)} %multiply_convert_fusion, bf16[768,768]{1,0:T(8,128)(2,1)} %param.19), kind=kOutput, calls=%fused_computation.27 | convolution fusion | flops 302186496 | bytes 1966080 | tf_op jit(solution)/shard_map/dot_general | solution.py:83
  31.8 21.7 %all-gather = bf16[1,2048]{1,0:T(2,128)(2,1)S(1)} all-gather(bf16[1,256]{1,0:T(2,128)(2,1)S(1)} %convert_element_type.59), channel_id=2, replica_groups=mesh['group'=4,'ctx'=8] {'ctx'}, dimensions={1}, use_global_device_ids=true | all-gather | bytes 4608 | tf_op jit(solution)/shard_map/all_gather | solution.py:94
  53.5 1.7 convolution_convert_fusion.3
  56.2 34.6 %all-gather.6.cloned.1.call-done = bf16[2048,768]{1,0:T(8,128)(2,1)} async-done(((bf16[256,768]{1,0:T(8,128)(2,1)}), bf16[2048,768]{1,0:T(8,128)(2,1)}) %all-gather.6.cloned.1.call-update) | async-done | bytes 3145744 | tf_op jit(solution)/shard_map/all_gather | solution.py:93
  90.8 61.3 %all-gather.4.cloned.1.call-done = bf16[2048,768]{1,0:T(8,128)(2,1)} async-done(((bf16[256,768]{1,0:T(8,128)(2,1)}), bf16[2048,768]{1,0:T(8,128)(2,1)}) %all-gather.4.cloned.1.call-update) | async-done | bytes 3145744 | tf_op jit(solution)/shard_map/all_gather | solution.py:92
  152.0 41.8 %while.15 = (s32[]{:T(128)}, f32[12,256]{1,0:T(8,128)S(1)}, f32[12,256]{1,0:T(8,128)}, f32[12,256,64]{1,2,0:T(8,128)}, s32[1,256]{1,0:T(1,128)S(1)}, /*index=5*/...) while((s32[]{:T(128)}, f32[12,256]{1,0:T(8,128)S(1)}, ...), condition=%wide.region_4.5_spmd.clone, body=%wide.region_1.4_spmd.clone.sunk | while | flops 423837184 | bytes 39528844 | solution.py:55
  155.9 2.3 %fusion.43 = (f32[12,256]{1,0:T(8,128)S(1)}, f32[12,512,256]{2,1,0:T(8,128)S(1)}) fusion(pred[256,512]{0,1:T(8,128)(4,1)} %broadcast_compare_fusion.3, bf16[512,12,64]{0,2,1:T(8,128)(2,1)S(1)} %bitcast.62, bf16[256,12,64]{0,2,1:T(8,128)(2,1)} %bitcast.60), kind=kOutput, calls=%fused_computation.2.clone.1 | convolution fusion | flops 206042112 | bytes 7614464 | tf_op jit(solution)/shard_map/while/body/eval_jaxpr/qhd,khd->hqk/dot_general | solution.py:27
  158.2 1.5 fusion.44
  159.8 1.8 fusion.46
  166.3 2.3 %fusion.43 = (f32[12,256]{1,0:T(8,128)S(1)}, f32[12,512,256]{2,1,0:T(8,128)S(1)}) fusion(pred[256,512]{0,1:T(8,128)(4,1)} %broadcast_compare_fusion.3, bf16[512,12,64]{0,2,1:T(8,128)(2,1)S(1)} %bitcast.62, bf16[256,12,64]{0,2,1:T(8,128)(2,1)} %bitcast.60), kind=kOutput, calls=%fused_computation.2.clone.1 | convolution fusion | flops 206042112 | bytes 7614464 | tf_op jit(solution)/shard_map/while/body/eval_jaxpr/qhd,khd->hqk/dot_general | solution.py:27
  168.7 1.5 fusion.44
  170.2 1.8 fusion.46
  176.8 2.3 %fusion.43 = (f32[12,256]{1,0:T(8,128)S(1)}, f32[12,512,256]{2,1,0:T(8,128)S(1)}) fusion(pred[256,512]{0,1:T(8,128)(4,1)} %broadcast_compare_fusion.3, bf16[512,12,64]{0,2,1:T(8,128)(2,1)S(1)} %bitcast.62, bf16[256,12,64]{0,2,1:T(8,128)(2,1)} %bitcast.60), kind=kOutput, calls=%fused_computation.2.clone.1 | convolution fusion | flops 206042112 | bytes 7614464 | tf_op jit(solution)/shard_map/while/body/eval_jaxpr/qhd,khd->hqk/dot_general | solution.py:27
  179.1 1.5 fusion.44
  180.7 1.8 fusion.46
  187.2 2.3 %fusion.43 = (f32[12,256]{1,0:T(8,128)S(1)}, f32[12,512,256]{2,1,0:T(8,128)S(1)}) fusion(pred[256,512]{0,1:T(8,128)(4,1)} %broadcast_compare_fusion.3, bf16[512,12,64]{0,2,1:T(8,128)(2,1)S(1)} %bitcast.62, bf16[256,12,64]{0,2,1:T(8,128)(2,1)} %bitcast.60), kind=kOutput, calls=%fused_computation.2.clone.1 | convolution fusion | flops 206042112 | bytes 7614464 | tf_op jit(solution)/shard_map/while/body/eval_jaxpr/qhd,khd->hqk/dot_general | solution.py:27
  189.5 1.5 fusion.44
  191.1 1.8 fusion.46
  195.0 2.0 fusion.14
  197.2 3.1 %reduce.4 = bf16[4,49152]{1,0:T(4,128)(2,1)S(1)} reduce(bf16[4,1,49152]{2,1,0:T(2,128)(2,1)S(1)} %all_to_all.19, bf16[]{:T(256)} %broadcast.74), dimensions={1}, to_apply=%all_to_all.19.reduce_sub_computation | reduce | bytes 786434 | tf_op jit(solution)/shard_map/all_to_all | solution.py:108
  200.8 10.0 %all_to_all.22 = bf16[4,2,24576]{2,1,0:T(2,128)(2,1)S(1)} all-to-all(bf16[4,2,24576]{2,1,0:T(2,128)(2,1)S(1)} %reshape.104), channel_id=1, replica_groups=mesh['group'=4,'ctx'=8] {'group'}, dimensions={0} | all-to-all | bytes 786432 | tf_op jit(solution)/shard_map/all_to_all | solution.py:108
  (143 shorter events, 33.1 us)
Async XLA Ops:
  6.5 21.3 %copy-start = (bf16[768,768]{1,0:T(8,128)(2,1)S(1)}, bf16[768,768]{1,0:T(8,128)(2,1)}, u32[]{:S(2)}) copy-start(bf16[768,768]{1,0:T(8,128)(2,1)} %param.20) | copy-start | bytes 3538948
  11.4 20.3 %copy-start.10 = (s32[1,256]{1,0:T(1,128)S(1)}, s32[1,256]{1,0:T(1,128)}, u32[]{:S(2)}) copy-start(s32[1,256]{1,0:T(1,128)} %param.16) | copy-start | bytes 3076
  12.6 11.7 %all-to-all-start = ((bf16[4,2,24576]{2,1,0:T(2,128)(2,1)}), bf16[4,2,24576]{2,1,0:T(2,128)(2,1)S(1)}, u32[]{:S(2)}, u32[]{:S(2)}) async-start(bf16[4,2,24576]{2,1,0:T(2,128)(2,1)} %reshape.102), calls=%async_computation | async-start | bytes 786432 | tf_op jit(solution)/shard_map/all_to_all | solution.py:71
  16.8 74.0 %all-gather.6.cloned.1.call-start = ((), (), s32[]{:S(2)}) async-start(), calls=%async_computation.3 | async-start | bytes 3538944 | tf_op jit(solution)/shard_map/all_gather | solution.py:93
  27.6 124.5 %copy-start.3 = (f32[256,768]{1,0:T(8,128)}, f32[256,768]{1,0:T(8,128)S(1)}, u32[]{:S(2)}) copy-start(f32[256,768]{1,0:T(8,128)S(1)} %reshape.93) | copy-start | bytes 2359300
  29.1 122.9 %all-gather.4.cloned.1.call-start = ((), (), s32[]{:S(2)}) async-start(), calls=%async_computation.2 | async-start | bytes 3538944 | tf_op jit(solution)/shard_map/all_gather | solution.py:92
  154.6 3.6 %copy-start.1 = (pred[256,512]{0,1:T(8,128)(4,1)S(1)}, pred[256,512]{0,1:T(8,128)(4,1)}, u32[]{:S(2)}) copy-start(pred[256,512]{0,1:T(8,128)(4,1)} %broadcast_compare_fusion.3) | copy-start | bytes 393220 | tf_op jit(solution)/shard_map/while
  155.9 3.8 %copy-start.6 = (f32[12,256]{1,0:T(8,128)S(1)}, f32[12,256]{1,0:T(8,128)}, u32[]{:S(2)}) copy-start(f32[12,256]{1,0:T(8,128)} %get-tuple-element.216) | copy-start | bytes 36868 | tf_op jit(solution)/shard_map/while
  155.9 3.9 %copy-start.2 = (bf16[1,512,768]{1,2,0:T(8,128)(2,1)S(1)}, bf16[1,512,768]{1,2,0:T(8,128)(2,1)}, u32[]{:S(2)}) copy-start(bf16[1,512,768]{1,2,0:T(8,128)(2,1)} %copy.39) | copy-start | bytes 2359300 | tf_op jit(solution)/shard_map/while
  155.9 3.9 %copy-start.4 = (f32[12,256,64]{1,2,0:T(8,128)S(1)}, f32[12,256,64]{1,2,0:T(8,128)}, u32[]{:S(2)}) copy-start(f32[12,256,64]{1,2,0:T(8,128)} %get-tuple-element.217) | copy-start | bytes 2359300 | tf_op jit(solution)/shard_map/while
  165.1 3.6 %copy-start.1 = (pred[256,512]{0,1:T(8,128)(4,1)S(1)}, pred[256,512]{0,1:T(8,128)(4,1)}, u32[]{:S(2)}) copy-start(pred[256,512]{0,1:T(8,128)(4,1)} %broadcast_compare_fusion.3) | copy-start | bytes 393220 | tf_op jit(solution)/shard_map/while
  166.3 3.8 %copy-start.6 = (f32[12,256]{1,0:T(8,128)S(1)}, f32[12,256]{1,0:T(8,128)}, u32[]{:S(2)}) copy-start(f32[12,256]{1,0:T(8,128)} %get-tuple-element.216) | copy-start | bytes 36868 | tf_op jit(solution)/shard_map/while
  166.3 3.9 %copy-start.2 = (bf16[1,512,768]{1,2,0:T(8,128)(2,1)S(1)}, bf16[1,512,768]{1,2,0:T(8,128)(2,1)}, u32[]{:S(2)}) copy-start(bf16[1,512,768]{1,2,0:T(8,128)(2,1)} %copy.39) | copy-start | bytes 2359300 | tf_op jit(solution)/shard_map/while
  166.3 3.9 %copy-start.4 = (f32[12,256,64]{1,2,0:T(8,128)S(1)}, f32[12,256,64]{1,2,0:T(8,128)}, u32[]{:S(2)}) copy-start(f32[12,256,64]{1,2,0:T(8,128)} %get-tuple-element.217) | copy-start | bytes 2359300 | tf_op jit(solution)/shard_map/while
  175.5 3.6 %copy-start.1 = (pred[256,512]{0,1:T(8,128)(4,1)S(1)}, pred[256,512]{0,1:T(8,128)(4,1)}, u32[]{:S(2)}) copy-start(pred[256,512]{0,1:T(8,128)(4,1)} %broadcast_compare_fusion.3) | copy-start | bytes 393220 | tf_op jit(solution)/shard_map/while
  176.8 3.8 %copy-start.6 = (f32[12,256]{1,0:T(8,128)S(1)}, f32[12,256]{1,0:T(8,128)}, u32[]{:S(2)}) copy-start(f32[12,256]{1,0:T(8,128)} %get-tuple-element.216) | copy-start | bytes 36868 | tf_op jit(solution)/shard_map/while
  176.8 3.9 %copy-start.2 = (bf16[1,512,768]{1,2,0:T(8,128)(2,1)S(1)}, bf16[1,512,768]{1,2,0:T(8,128)(2,1)}, u32[]{:S(2)}) copy-start(bf16[1,512,768]{1,2,0:T(8,128)(2,1)} %copy.39) | copy-start | bytes 2359300 | tf_op jit(solution)/shard_map/while
  176.8 3.9 %copy-start.4 = (f32[12,256,64]{1,2,0:T(8,128)S(1)}, f32[12,256,64]{1,2,0:T(8,128)}, u32[]{:S(2)}) copy-start(f32[12,256,64]{1,2,0:T(8,128)} %get-tuple-element.217) | copy-start | bytes 2359300 | tf_op jit(solution)/shard_map/while
  180.7 2.7 %copy-start.9 = (bf16[4,512]{1,0:T(4,128)(2,1)S(1)}, bf16[4,512]{1,0:T(4,128)(2,1)}, u32[]{:S(2)}) copy-start(bf16[4,512]{1,0:T(4,128)(2,1)} %copy-done.8) | copy-start | bytes 12292 | tf_op jit(solution)/shard_map/while
  186.0 3.6 %copy-start.1 = (pred[256,512]{0,1:T(8,128)(4,1)S(1)}, pred[256,512]{0,1:T(8,128)(4,1)}, u32[]{:S(2)}) copy-start(pred[256,512]{0,1:T(8,128)(4,1)} %broadcast_compare_fusion.3) | copy-start | bytes 393220 | tf_op jit(solution)/shard_map/while
  187.2 3.8 %copy-start.6 = (f32[12,256]{1,0:T(8,128)S(1)}, f32[12,256]{1,0:T(8,128)}, u32[]{:S(2)}) copy-start(f32[12,256]{1,0:T(8,128)} %get-tuple-element.216) | copy-start | bytes 36868 | tf_op jit(solution)/shard_map/while
  187.2 3.9 %copy-start.2 = (bf16[1,512,768]{1,2,0:T(8,128)(2,1)S(1)}, bf16[1,512,768]{1,2,0:T(8,128)(2,1)}, u32[]{:S(2)}) copy-start(bf16[1,512,768]{1,2,0:T(8,128)(2,1)} %copy.39) | copy-start | bytes 2359300 | tf_op jit(solution)/shard_map/while
  187.2 3.9 %copy-start.4 = (f32[12,256,64]{1,2,0:T(8,128)S(1)}, f32[12,256,64]{1,2,0:T(8,128)}, u32[]{:S(2)}) copy-start(f32[12,256,64]{1,2,0:T(8,128)} %get-tuple-element.217) | copy-start | bytes 2359300 | tf_op jit(solution)/shard_map/while
  193.8 17.4 %copy-start.12 = (s32[4]{0:T(128)S(1)}, s32[4]{0:T(128)}, u32[]{:S(2)}) copy-start(s32[4]{0:T(128)} %param.15) | copy-start | bytes 52
  (19 other events, 39.0 us)
Sparse Core Ops, SparseCore 0:
  29.3 61.4 all-gather.5
  92.9 59.0 all-gather.3
where the time goes:
time: 220 us
  waiting for transfers between devices  103 us (47%)
  blocking collectives  31.7 us (14%)
  matrix products  25.6 us (12%)
  local copies, waits for them, and re-layouts  21.5 us (10%)
  other arithmetic  20 us (9%)
  between operations  13.6 us (6%)
  starting transfers between devices  4.25 us (2%)
    all_gather x1, waiting for transfers between devices, on_device(): lax.all_gather(keys_local, 'ctx', axis=0, tiled=True)  61.3 us
    all_gather x1, waiting for transfers between devices, on_device(): lax.all_gather(values_local, 'ctx', axis=0, tiled=True)  34.6 us
    all_gather x1, blocking collectives, on_device(): lax.all_gather(doc_wire, 'ctx', axis=0, tiled=True)  21.7 us
    dynamic_slice x12, local copies, waits for them, and re-layouts, visit_tiles(): carried, unused = lax.scan(one_tile, carried, stacked)  12 us
    all_to_all x1, blocking collectives, on_device(): lax.all_to_all(out_packed.reshape(groups, -1), 'group', split_axis=0, con...  9.98 us
    dot_general x4, matrix products, softmax_update(): jnp.einsum('qhd,khd->hqk', head_query, head_key, preferred_element_type=j...  9.21 us
    dot_general x4, matrix products, softmax_update(): jnp.einsum('hqk,khd->hqd', expo.astype(jnp.bfloat16), head_value, preferr...  7.19 us
    all_to_all x1, waiting for transfers between devices, on_device(): lax.all_to_all(ordered, 'group', split_axis=0, concat_axis=0, tiled=True)  6.76 us
  transfers between devices with their start and end apart: 3, of which 3 were waited for; matrix products, arithmetic and copies ran while one was open for 3% of the time, Pallas kernels for 0%

commit v1 on v0

v1 whole, which is shorter than its diff:
```python
import functools
import math

import jax
import jax.numpy as jnp
from jax import lax
from jax.experimental import pallas as pl
from jax.experimental.pallas import tpu as pltpu
from jax.sharding import PartitionSpec as P

HEADS = 12
HD = 64
STEP_HEADS = 4
STEP_COLS = STEP_HEADS * HD
STATE_ROWS = HD + 16
NEGATIVE = -1e30
VMEM_LIMIT = 32 * 1024 * 1024


def whole(shape):
    return pl.BlockSpec(shape, lambda *step: (0,) * len(shape))


def smem():
    return pl.BlockSpec(memory_space=pltpu.SMEM)


def params():
    return pltpu.CompilerParams(vmem_limit_bytes=VMEM_LIMIT)


def piece_of(listing_ref, group, groups):
    place = jnp.int32(0)
    for k in range(groups):
        place = place + jnp.where(listing_ref[k] == group, jnp.int32(k), jnp.int32(0))
    return place


def route_kernel(groups, listing_ref, series_ref, mask_ref, token_ref, *rest):
    out_refs, column_ref = rest[:-1], rest[-1]
    rows, width = series_ref.shape
    piece = rows // groups
    for part in range(rows // 128):
        line = mask_ref[part : part + 1, :].astype(jnp.float32)
        column_ref[part * 128 : (part + 1) * 128, :] = jnp.broadcast_to(line, (128, 128)).T
    own = lax.axis_index("group")
    token = token_ref[...].astype(jnp.float32)
    for r in range(groups):
        place = piece_of(listing_ref, lax.bitwise_xor(own, jnp.int32(r)), groups)
        first = pl.multiple_of(place * piece, piece)
        hidden = column_ref[pl.ds(first, piece), :] > 0.5
        arrived = series_ref[pl.ds(first, piece), :].astype(jnp.float32)
        for lane in range(0, width, 128):
            out_refs[r][:, lane : lane + 128] = jnp.where(
                hidden, token[:, lane : lane + 128], arrived[:, lane : lane + 128]
            ).astype(jnp.bfloat16)


def route(packing_list, series, recon_mask, mask_token, groups):
    rows, width = series.shape
    piece = rows // groups
    return pl.pallas_call(
        functools.partial(route_kernel, groups),
        out_shape=[jax.ShapeDtypeStruct((piece, width), jnp.bfloat16)] * groups,
        in_specs=[smem(), whole((rows, width)), whole((rows // 128, 128)), whole((1, width))],
        out_specs=[whole((piece, width))] * groups,
        grid=(1,),
        scratch_shapes=[pltpu.VMEM((rows, 128), jnp.float32)],
        compiler_params=params(),
        name="route",
    )(packing_list, series, recon_mask.reshape(rows // 128, 128), mask_token.reshape(1, width))


def norm_kernel(count, with_borders, *refs):
    piece_refs, gain_ref = refs[:count], refs[count]
    out_ref = refs[-1]
    piece = piece_refs[0].shape[0]
    gain = gain_ref[...].astype(jnp.float32)
    for i, ref in enumerate(piece_refs):
        widened = ref[...].astype(jnp.float32)
        factor = lax.rsqrt(jnp.mean(widened * widened, axis=-1, keepdims=True) + 1e-06)
        out_ref[i * piece : (i + 1) * piece, :] = (widened * factor * gain).astype(jnp.bfloat16)
    if with_borders:
        docs = refs[count + 1][...]
        width = out_ref.shape[1]
        row = lax.broadcasted_iota(jnp.int32, (8, width), 0)
        lines = jnp.zeros((8, width), jnp.float32)
        for d in (1, 2, 3):
            below = jnp.sum(jnp.where(docs < d, 1.0, 0.0), axis=-1, keepdims=True)
            lines = jnp.where(row == d, below, lines)
        out_ref[count * piece :, :] = lines.astype(jnp.bfloat16)


def norm(pieces, gain, docs=None):
    piece, width = pieces[0].shape
    count = len(pieces)
    rows = count * piece + (8 if docs is not None else 0)
    operands = list(pieces) + [gain.reshape(1, width)]
    if docs is not None:
        operands.append(docs)
    return pl.pallas_call(
        functools.partial(norm_kernel, count, docs is not None),
        out_shape=jax.ShapeDtypeStruct((rows, width), jnp.bfloat16),
        in_specs=[whole(member.shape) for member in operands],
        out_specs=whole((rows, width)),
        grid=(1,),
        compiler_params=params(),
        name="norm",
    )(*operands)


def doc_numbers(borders, place):
    docs = jnp.zeros(place.shape, jnp.float32)
    for d in (1, 2, 3):
        docs = docs + jnp.where(place >= borders[d : d + 1, :], 1.0, 0.0)
    return docs


def places_of(count, piece, groups, shape, axis):
    own = lax.axis_index("group")
    held = lax.broadcasted_iota(jnp.int32, shape, axis)
    source = lax.bitwise_xor(held // piece, own)
    return (source * piece + held % piece).astype(jnp.float32)


def attend(x, caps, key_weight, value_weight, queries_ref, state, first):
    keys = jnp.dot(x, key_weight, preferred_element_type=jnp.float32).astype(jnp.bfloat16)
    values = jnp.dot(x, value_weight, preferred_element_type=jnp.float32).T.astype(jnp.bfloat16)
    ones = jnp.ones((16, x.shape[0]), jnp.bfloat16)
    after = []
    for h in range(STEP_HEADS):
        pair = h // 2 * 128
        scores = jnp.dot(
            keys[:, pair : pair + 128], queries_ref[h], preferred_element_type=jnp.float32
        )
        scores = jnp.minimum(scores, caps)
        top = jnp.max(scores, axis=0, keepdims=True)
        if not first:
            top = jnp.maximum(top, state[h][1])
        weights = jnp.exp(scores - top).astype(jnp.bfloat16)
        widened = jnp.concatenate([values[h * HD : (h + 1) * HD], ones], axis=0)
        sums = jnp.dot(widened, weights, preferred_element_type=jnp.float32)
        if not first:
            sums = sums + state[h][0] * jnp.exp(state[h][1] - top)
        after.append((sums, top))
    return after


def load_state(state_ref):
    return [
        (state_ref[h], state_ref[h, HD + 8 : HD + 9, :]) for h in range(STEP_HEADS)
    ]


def store_state(state_ref, state):
    for h in range(STEP_HEADS):
        sums, top = state[h]
        state_ref[h, : HD + 8, :] = sums[: HD + 8]
        state_ref[h, HD + 8 :, :] = jnp.broadcast_to(top, (8, top.shape[1]))


def caps_of(borders, query_docs, piece, groups, rows):
    place = places_of(rows, piece, groups, (rows, rows), 0)
    return jnp.where(doc_numbers(borders, place) == query_docs, jnp.float32(3e38), NEGATIVE)


def own_kernel(
    piece, groups, a_ref, b_ref, wq_ref, wk_ref, wv_ref, queries_ref, docs_ref, state_ref, caps_ref
):
    half = b_ref.shape[0]
    rows = 2 * half
    x = jnp.concatenate([a_ref[:half, :], b_ref[...]], axis=0)

    @pl.when(pl.program_id(0) == 0)
    def first_step():
        borders = a_ref[half:, :rows].astype(jnp.float32)
        place = places_of(rows, piece, groups, (8, rows), 1)
        docs = jnp.zeros((8, rows), jnp.float32)
        for d in (1, 2, 3):
            docs = docs + jnp.where(place >= borders[d : d + 1, :], 1.0, 0.0)
        docs_ref[...] = docs
        caps_ref[...] = caps_of(borders, docs[0:1, :], piece, groups, rows)

    queries = jnp.dot(x, wq_ref[...], preferred_element_type=jnp.float32)
    queries = (queries.astype(jnp.bfloat16).astype(jnp.float32) * (1.0 / math.sqrt(HD))).T
    queries = queries.astype(jnp.bfloat16)
    blank = jnp.zeros((HD, rows), jnp.bfloat16)
    for h in range(STEP_HEADS):
        own = queries[h * HD : (h + 1) * HD]
        queries_ref[h] = jnp.concatenate([own, blank] if h % 2 == 0 else [blank, own], axis=0)
    store_state(
        state_ref, attend(x, caps_ref[...], wk_ref[...], wv_ref[...], queries_ref, None, True)
    )


def fold(piece, groups, sources, docs_ref, caps_ref, wk_ref, wv_ref, queries_ref, state):
    half = sources[0][1].shape[0]
    rows = 2 * half
    for i, (a_ref, b_ref) in enumerate(sources):

        @pl.when(pl.program_id(0) == 0)
        def first_step():
            borders = a_ref[half:, :rows].astype(jnp.float32)
            caps_ref[i] = caps_of(borders, docs_ref[0:1, :], piece, groups, rows)

        x = jnp.concatenate([a_ref[:half, :], b_ref[...]], axis=0)
        state = attend(x, caps_ref[i], wk_ref[...], wv_ref[...], queries_ref, state, False)
    return state


def chunk_kernel(
    piece, groups, count, queries_ref, docs_ref, wk_ref, wv_ref, state_in_ref, *rest
):
    source_refs, state_ref, caps_ref = rest[: 2 * count], rest[2 * count], rest[2 * count + 1]
    sources = [(source_refs[2 * i], source_refs[2 * i + 1]) for i in range(count)]
    state = fold(
        piece, groups, sources, docs_ref, caps_ref, wk_ref, wv_ref, queries_ref, load_state(state_in_ref)
    )
    store_state(state_ref, state)


def last_kernel(
    piece, groups, queries_ref, docs_ref, wk_ref, wv_ref, state_in_ref, a_ref, b_ref, wo_ref, *rest
):
    piece_refs, out_refs = rest[:groups], rest[groups : 2 * groups]
    caps_ref, total_ref = rest[2 * groups], rest[2 * groups + 1]
    state = fold(
        piece, groups, [(a_ref, b_ref)], docs_ref, caps_ref, wk_ref, wv_ref, queries_ref, load_state(state_in_ref)
    )
    attended = jnp.concatenate(
        [(sums[:HD] / sums[HD : HD + 1]) for sums, top in state], axis=0
    ).T.astype(jnp.bfloat16)
    mixed = jnp.dot(attended, wo_ref[...], preferred_element_type=jnp.float32)
    step, last = pl.program_id(0), pl.num_programs(0) - 1

    @pl.when(step == 0)
    def start():
        total_ref[...] = mixed

    @pl.when(jnp.logical_and(step > 0, step < last))
    def middle():
        total_ref[...] += mixed

    @pl.when(step == last)
    def finish():
        summed = total_ref[...] + mixed
        for r in range(groups):
            out_refs[r][...] = (
                piece_refs[r][...].astype(jnp.float32) + summed[r * piece : (r + 1) * piece]
            ).astype(jnp.bfloat16)


def column_block(width):
    return pl.BlockSpec((width, STEP_COLS), lambda step: (0, step))


def queries_block(rows):
    return pl.BlockSpec((STEP_HEADS, 2 * HD, rows), lambda step: (step, 0, 0))


def state_block(rows):
    return pl.BlockSpec((STEP_HEADS, STATE_ROWS, rows), lambda step: (step, 0, 0))


def own_call(a, b, w_query, w_key, w_value, piece, groups):
    rows, width = 2 * b.shape[0], b.shape[1]
    return pl.pallas_call(
        functools.partial(own_kernel, piece, groups),
        out_shape=[
            jax.ShapeDtypeStruct((HEADS, 2 * HD, rows), jnp.bfloat16),
            jax.ShapeDtypeStruct((8, rows), jnp.float32),
            jax.ShapeDtypeStruct((HEADS, STATE_ROWS, rows), jnp.float32),
        ],
        in_specs=[whole(a.shape), whole(b.shape)] + [column_block(width)] * 3,
        out_specs=[queries_block(rows), whole((8, rows)), state_block(rows)],
        grid=(HEADS // STEP_HEADS,),
        scratch_shapes=[pltpu.VMEM((rows, rows), jnp.float32)],
        compiler_params=params(),
        name="own_rows",
    )(a, b, w_query, w_key, w_value)


def chunk_call(queries, docs, w_key, w_value, state, sources, piece, groups):
    rows, width = queries.shape[2], w_key.shape[0]
    flat = [member for source in sources for member in source]
    return pl.pallas_call(
        functools.partial(chunk_kernel, piece, groups, len(sources)),
        out_shape=jax.ShapeDtypeStruct(state.shape, jnp.float32),
        in_specs=[queries_block(rows), whole(docs.shape), column_block(width), column_block(width), state_block(rows)]
        + [whole(member.shape) for member in flat],
        out_specs=state_block(rows),
        grid=(HEADS // STEP_HEADS,),
        scratch_shapes=[pltpu.VMEM((len(sources), rows, rows), jnp.float32)],
        input_output_aliases={4: 0},
        compiler_params=params(),
        name="received_rows",
    )(queries, docs, w_key, w_value, state, *flat)


def last_call(queries, docs, w_key, w_value, state, a, b, w_out, pieces, piece, groups):
    rows, width = queries.shape[2], w_key.shape[0]
    return pl.pallas_call(
        functools.partial(last_kernel, piece, groups),
        out_shape=[jax.ShapeDtypeStruct((piece, width), jnp.bfloat16)] * groups,
        in_specs=[queries_block(rows), whole(docs.shape), column_block(width), column_block(width), state_block(rows)]
        + [whole(a.shape), whole(b.shape), pl.BlockSpec((STEP_COLS, width), lambda step: (step, 0))]
        + [whole((piece, width))] * groups,
        out_specs=[whole((piece, width))] * groups,
        grid=(HEADS // STEP_HEADS,),
        scratch_shapes=[
            pltpu.VMEM((1, rows, rows), jnp.float32),
            pltpu.VMEM((rows, width), jnp.float32),
        ],
        compiler_params=params(),
        name="last_rows",
    )(queries, docs, w_key, w_value, state, a, b, w_out, *pieces)


def arrange_kernel(groups, listing_ref, *refs):
    piece_refs, out_ref = refs[:groups], refs[groups]
    piece = piece_refs[0].shape[0]
    own = lax.axis_index("group")
    for r in range(groups):
        place = piece_of(listing_ref, lax.bitwise_xor(own, jnp.int32(r)), groups)
        out_ref[pl.ds(pl.multiple_of(place * piece, piece), piece), :] = piece_refs[r][...]


def arrange(packing_list, pieces):
    groups, (piece, width) = len(pieces), pieces[0].shape
    return pl.pallas_call(
        functools.partial(arrange_kernel, groups),
        out_shape=jax.ShapeDtypeStruct((groups * piece, width), jnp.bfloat16),
        in_specs=[smem()] + [whole((piece, width))] * groups,
        out_specs=whole((groups * piece, width)),
        grid=(1,),
        compiler_params=params(),
        name="arrange",
    )(packing_list, *pieces)


def exchange(pieces):
    groups = len(pieces)
    return [pieces[0]] + [
        lax.ppermute(pieces[r], "group", [(i, i ^ r) for i in range(groups)])
        for r in range(1, groups)
    ]


def on_device(
    series, recon_mask, mask_token, packing_list, doc_ids, norm_gain, w_query, w_key, w_value, w_out
):
    groups, shards = lax.axis_size("group"), lax.axis_size("ctx")
    rows, width = series.shape
    piece = rows // groups
    ring = list(range(0, shards, 2)) + list(range(shards - 1, 0, -2))
    onward = [(ring[i], ring[(i + 1) % shards]) for i in range(shards)]
    backward = [(there, here) for here, there in onward]

    pieces = exchange(route(packing_list, series, recon_mask, mask_token, groups))
    a = norm(pieces[: groups // 2], norm_gain, doc_ids)
    b = norm(pieces[groups // 2 :], norm_gain)
    queries, docs, state = own_call(a, b, w_query, w_key, w_value, piece, groups)
    before, after = (a, b), (a, b)
    for step in range(1, shards // 2):
        before = tuple(lax.ppermute(member, "ctx", onward) for member in before)
        after = tuple(lax.ppermute(member, "ctx", backward) for member in after)
        state = chunk_call(
            queries, docs, w_key, w_value, state, (before, after), piece, groups
        )
    far_a = lax.ppermute(before[0], "ctx", onward)
    far_b = lax.ppermute(after[1], "ctx", backward)
    done = last_call(
        queries, docs, w_key, w_value, state, far_a, far_b, w_out, pieces, piece, groups
    )
    return arrange(packing_list, exchange(done))


def solution(mesh):
    in_specs = (
        P(("group", "ctx"), None),
        P(("group", "ctx")),
        P(),
        P(("group", "ctx")),
        P("group", "ctx"),
        P(),
        P(),
        P(),
        P(),
        P(),
    )
    out_specs = P(("group", "ctx"), None)
    return jax.shard_map(
        on_device, mesh=mesh, in_specs=in_specs, out_specs=out_specs, check_vma=False
    )
```

time: 220 us -> 89.7 us (0.41)
  waiting for transfers between devices: 103 us -> 15.4 us
  Pallas kernels: 0 us -> 41.8 us
  blocking collectives: 31.7 us -> 0 us
  matrix products: 25.6 us -> 0 us
  starting transfers between devices: 4.25 us -> 25 us
  other arithmetic: 20 us -> 0 us
  local copies, waits for them, and re-layouts: 21.5 us -> 7.03 us
  between operations: 13.6 us -> 0.15 us
    all_gather x2 -> x0, waiting for transfers between devices: 95.8 us -> none  [the longest x1 61.3 us: on_device(): lax.all_gather(keys_local, 'ctx', axis=0, tiled=True)]
    pallas_call x0 -> x9, Pallas kernels: none -> 41.8 us  [the longest x3 28.1 us: chunk_call(): pl.pallas_call(functools.partial(chunk_kernel, piece, groups, len(sources...]
    dot_general x14 -> x0, matrix products: 25.6 us -> none  [the longest x4 9.21 us: softmax_update(): jnp.einsum('qhd,khd->hqk', head_query, head_key, preferred_element_type=j...]
    ppermute x0 -> x20, starting transfers between devices: none -> 25 us  [the longest x6 9.31 us: on_device(): after = tuple((lax.ppermute(member, 'ctx', backward) for member in after))]
    all_gather x1 -> x0, blocking collectives: 21.7 us -> none  [on_device(): lax.all_gather(doc_wire, 'ctx', axis=0, tiled=True)]
    ppermute x0 -> x20, waiting for transfers between devices: none -> 15.4 us  [the longest x6 6.79 us: exchange(): lax.ppermute(pieces[r], 'group', [(i, i ^ r) for i in range(groups)])]
    dynamic_slice x12 -> x0, local copies, waits for them, and re-layouts: 12 us -> none  [visit_tiles(): carried, unused = lax.scan(one_tile, carried, stacked)]
    all_to_all x1 -> x0, blocking collectives: 9.98 us -> none  [on_device(): lax.all_to_all(out_packed.reshape(groups, -1), 'group', split_axis=0, con...]
  transfers between devices with their start and end apart: 3 -> 20, of which waited for: 3 -> 10; matrix products, arithmetic and copies ran while one was open for 3% -> 1% of each run, Pallas kernels for 0% -> 38%
where the time goes in v1:
time: 89.7 us; the launch traced here: 89.4 us
  Pallas kernels  41.8 us (47%)
  starting transfers between devices  25 us (28%)
  waiting for transfers between devices  15.4 us (17%)
  local copies, waits for them, and re-layouts  7.03 us (8%)
    pallas_call x3, Pallas kernels, chunk_call(): pl.pallas_call(functools.partial(chunk_kernel, piece, groups, len(sources...  28.1 us
    ppermute x6, starting transfers between devices, on_device(): after = tuple((lax.ppermute(member, 'ctx', backward) for member in after))  9.31 us
    ppermute x6, starting transfers between devices, on_device(): before = tuple((lax.ppermute(member, 'ctx', onward) for member in before))  8.75 us
    ppermute x6, waiting for transfers between devices, exchange(): lax.ppermute(pieces[r], 'group', [(i, i ^ r) for i in range(groups)])  6.79 us
    ppermute x6, waiting for transfers between devices, on_device(): after = tuple((lax.ppermute(member, 'ctx', backward) for member in after))  6.55 us
    pallas_call x1, Pallas kernels, last_call(): pl.pallas_call(functools.partial(last_kernel, piece, groups), out_shape=[...  6.11 us
    unnamed x18, local copies, waits for them, and re-layouts  5.56 us
    pallas_call x1, Pallas kernels, own_call(): pl.pallas_call(functools.partial(own_kernel, piece, groups), out_shape=[j...  5.28 us
  transfers between devices with their start and end apart: 20, of which 10 were waited for; matrix products, arithmetic and copies ran while one was open for 1% of the time, Pallas kernels for 38%

profile of v1, /device:TPU:0, one launch (start us, length us, event | category | flops | bytes accessed | tf_op | source)
XLA Modules:
  0.0 89.4 jit_solution(15258655299381571072)
XLA Ops:
  4.4 2.6 %collective-permute-start.1 = (bf16[64,768]{1,0:T(8,128)(2,1)S(1)}, bf16[64,768]{1,0:T(8,128)(2,1)S(1)}, u32[]{:S(2)}, u32[]{:S(2)}) collective-permute-start(bf16[64,768]{1,0:T(8,128)(2,1)S(1)} %get-tuple-element.18), channel_id=1, source_target_pairs={{0,16},{8,24},{16,0},{24,8},{1,17},{9,25},{17,1},{25,9},{2,18},{10... | collective-permute-start | bytes 294920 | tf_op jit(solution)/shard_map/ppermute | solution.py:344
  8.5 1.9 %collective-permute-start.3 = (bf16[136,768]{1,0:T(8,128)(2,1)S(1)}, bf16[136,768]{1,0:T(8,128)(2,1)S(1)}, u32[]{:S(2)}, u32[]{:S(2)}) collective-permute-start(bf16[136,768]{1,0:T(8,128)(2,1)S(1)} %norm.2.a_ref), channel_id=1, source_target_pairs={{0,2},{2,4},{4,6},{6,7},{7,5},{5,3},{3,1},{1,0},{8,10},{10,12},{12... | collective-permute-start | bytes 626696 | tf_op jit(solution)/shard_map/ppermute | solution.py:365
  10.6 1.6 %collective-permute-done.2.refs_1_.rest_3_ = bf16[64,768]{1,0:T(8,128)(2,1)S(1)} collective-permute-done((bf16[64,768]{1,0:T(8,128)(2,1)S(1)}, bf16[64,768]{1,0:T(8,128)(2,1)S(1)}, u32[]{:S(2)}, u32[]{:S(2)}) %collective-permute-start.2) | collective-permute-done | bytes 98336 | tf_op jit(solution)/shard_map/ppermute | solution.py:344
  12.3 1.6 %collective-permute-start.6 = (bf16[128,768]{1,0:T(8,128)(2,1)S(1)}, bf16[128,768]{1,0:T(8,128)(2,1)S(1)}, u32[]{:S(2)}, u32[]{:S(2)}) collective-permute-start(bf16[128,768]{1,0:T(8,128)(2,1)S(1)} %norm.3.b_ref), channel_id=1, source_target_pairs={{2,0},{4,2},{6,4},{7,6},{5,7},{3,5},{1,3},{0,1},{10,8},{12,10},{14... | collective-permute-start | bytes 589832 | tf_op jit(solution)/shard_map/ppermute | solution.py:366
  13.9 1.6 %collective-permute-start.5 = (bf16[136,768]{1,0:T(8,128)(2,1)S(1)}, bf16[136,768]{1,0:T(8,128)(2,1)S(1)}, u32[]{:S(2)}, u32[]{:S(2)}) collective-permute-start(bf16[136,768]{1,0:T(8,128)(2,1)S(1)} %norm.2.a_ref), channel_id=1, source_target_pairs={{2,0},{4,2},{6,4},{7,6},{5,7},{3,5},{1,3},{0,1},{10,8},{12,10},{14... | collective-permute-start | bytes 626696 | tf_op jit(solution)/shard_map/ppermute | solution.py:366
  16.0 1.8 %collective-permute-start.7 = (bf16[136,768]{1,0:T(8,128)(2,1)S(1)}, bf16[136,768]{1,0:T(8,128)(2,1)S(1)}, u32[]{:S(2)}, u32[]{:S(2)}) collective-permute-start(bf16[136,768]{1,0:T(8,128)(2,1)S(1)} %collective-permute-done.3.rest_0_), channel_id=1, source_target_pairs={{0,2},{2,4},{4,6},{6,7},{7,5},{5,3},{3,1},{1,0},{8,10},{10,12},{12... | collective-permute-start | bytes 626696 | tf_op jit(solution)/shard_map/ppermute | solution.py:365
  17.8 1.6 %collective-permute-start.4 = (bf16[128,768]{1,0:T(8,128)(2,1)S(1)}, bf16[128,768]{1,0:T(8,128)(2,1)S(1)}, u32[]{:S(2)}, u32[]{:S(2)}) collective-permute-start(bf16[128,768]{1,0:T(8,128)(2,1)S(1)} %norm.3.b_ref), channel_id=1, source_target_pairs={{0,2},{2,4},{4,6},{6,7},{7,5},{5,3},{3,1},{1,0},{8,10},{10,12},{12... | collective-permute-start | bytes 589832 | tf_op jit(solution)/shard_map/ppermute | solution.py:365
  20.1 1.6 %collective-permute-start.10 = (bf16[128,768]{1,0:T(8,128)(2,1)S(1)}, bf16[128,768]{1,0:T(8,128)(2,1)S(1)}, u32[]{:S(2)}, u32[]{:S(2)}) collective-permute-start(bf16[128,768]{1,0:T(8,128)(2,1)S(1)} %collective-permute-done.6.rest_3_), channel_id=1, source_target_pairs={{2,0},{4,2},{6,4},{7,6},{5,7},{3,5},{1,3},{0,1},{10,8},{12,10},{14... | collective-permute-start | bytes 589832 | tf_op jit(solution)/shard_map/ppermute | solution.py:366
  21.6 2.9 %collective-permute-done.5.rest_2_ = bf16[136,768]{1,0:T(8,128)(2,1)S(1)} collective-permute-done((bf16[136,768]{1,0:T(8,128)(2,1)S(1)}, bf16[136,768]{1,0:T(8,128)(2,1)S(1)}, u32[]{:S(2)}, u32[]{:S(2)}) %collective-permute-start.5) | collective-permute-done | bytes 208928 | tf_op jit(solution)/shard_map/ppermute | solution.py:366
  24.5 1.6 %collective-permute-start.9 = (bf16[136,768]{1,0:T(8,128)(2,1)S(1)}, bf16[136,768]{1,0:T(8,128)(2,1)S(1)}, u32[]{:S(2)}, u32[]{:S(2)}) collective-permute-start(bf16[136,768]{1,0:T(8,128)(2,1)S(1)} %collective-permute-done.5.rest_2_), channel_id=1, source_target_pairs={{2,0},{4,2},{6,4},{7,6},{5,7},{3,5},{1,3},{0,1},{10,8},{12,10},{14... | collective-permute-start | bytes 626696 | tf_op jit(solution)/shard_map/ppermute | solution.py:366
  26.8 2.1 %collective-permute-start.8 = (bf16[128,768]{1,0:T(8,128)(2,1)S(1)}, bf16[128,768]{1,0:T(8,128)(2,1)S(1)}, u32[]{:S(2)}, u32[]{:S(2)}) collective-permute-start(bf16[128,768]{1,0:T(8,128)(2,1)S(1)} %collective-permute-done.4.rest_1_), channel_id=1, source_target_pairs={{0,2},{2,4},{4,6},{6,7},{7,5},{5,3},{3,1},{1,0},{8,10},{10,12},{12... | collective-permute-start | bytes 589832 | tf_op jit(solution)/shard_map/ppermute | solution.py:365
  28.9 1.4 %collective-permute-start.14 = (bf16[128,768]{1,0:T(8,128)(2,1)S(1)}, bf16[128,768]{1,0:T(8,128)(2,1)S(1)}, u32[]{:S(2)}, u32[]{:S(2)}) collective-permute-start(bf16[128,768]{1,0:T(8,128)(2,1)S(1)} %collective-permute-done.10.rest_3_), channel_id=1, source_target_pairs={{2,0},{4,2},{6,4},{7,6},{5,7},{3,5},{1,3},{0,1},{10,8},{12,10},{14... | collective-permute-start | bytes 589832 | tf_op jit(solution)/shard_map/ppermute | solution.py:366
  30.3 2.9 %collective-permute-done.9.rest_2_ = bf16[136,768]{1,0:T(8,128)(2,1)S(1)} collective-permute-done((bf16[136,768]{1,0:T(8,128)(2,1)S(1)}, bf16[136,768]{1,0:T(8,128)(2,1)S(1)}, u32[]{:S(2)}, u32[]{:S(2)}) %collective-permute-start.9) | collective-permute-done | bytes 208928 | tf_op jit(solution)/shard_map/ppermute | solution.py:366
  33.2 1.6 %collective-permute-start.13 = (bf16[136,768]{1,0:T(8,128)(2,1)S(1)}, bf16[136,768]{1,0:T(8,128)(2,1)S(1)}, u32[]{:S(2)}, u32[]{:S(2)}) collective-permute-start(bf16[136,768]{1,0:T(8,128)(2,1)S(1)} %collective-permute-done.9.rest_2_), channel_id=1, source_target_pairs={{2,0},{4,2},{6,4},{7,6},{5,7},{3,5},{1,3},{0,1},{10,8},{12,10},{14... | collective-permute-start | bytes 626696 | tf_op jit(solution)/shard_map/ppermute | solution.py:366
  35.3 1.3 %collective-permute-done.8.rest_1_ = bf16[128,768]{1,0:T(8,128)(2,1)S(1)} collective-permute-done((bf16[128,768]{1,0:T(8,128)(2,1)S(1)}, bf16[128,768]{1,0:T(8,128)(2,1)S(1)}, u32[]{:S(2)}, u32[]{:S(2)}) %collective-permute-start.8) | collective-permute-done | bytes 196640 | tf_op jit(solution)/shard_map/ppermute | solution.py:365
  37.6 1.4 %collective-permute-start.16 = (bf16[128,768]{1,0:T(8,128)(2,1)S(1)}, bf16[128,768]{1,0:T(8,128)(2,1)S(1)}, u32[]{:S(2)}, u32[]{:S(2)}) collective-permute-start(bf16[128,768]{1,0:T(8,128)(2,1)S(1)} %collective-permute-done.14.rest_3_), channel_id=1, source_target_pairs={{2,0},{4,2},{6,4},{7,6},{5,7},{3,5},{1,3},{0,1},{10,8},{12,10},{14... | collective-permute-start | bytes 589832 | tf_op jit(solution)/shard_map/ppermute | solution.py:371
  41.5 5.3 %own_rows.1 = (bf16[12,128,256]{2,1,0:T(8,128)(2,1)S(1)}, f32[8,256]{1,0:T(8,128)S(1)}, f32[12,80,256]{2,1,0:T(8,128)S(1)}) custom-call(bf16[136,768]{1,0:T(8,128)(2,1)S(1)} %norm.2.a_ref, bf16[128,768]{1,0:T(8,128)(2,1)S(1)} %norm.3.b_ref, bf16[768,768]{1,0:T(8,128)(2,1)S(1)} %copy-done.3, bf16[768,768]{1,0:T(8,128)(2,1)S(1)} %copy-done, ...), custom_call_target="tpu_custom_call" | custom-call | tf_op jit(solution)/shard_map/own_rows/pallas_call | solution.py:267
  46.8 9.4 %received_rows.3.state_in_ref = f32[12,80,256]{2,1,0:T(8,128)S(1)} custom-call(bf16[12,128,256]{2,1,0:T(8,128)(2,1)S(1)} %get-tuple-element.20.queries_ref, f32[8,256]{1,0:T(8,128)S(1)} %get-tuple-element.21.docs_ref, bf16[768,768]{1,0:T(8,128)(2,1)S(1)} %copy-done, bf16[768,768]{1,0:T(8,128)(2,1)S(1)} %copy-done.2, ...), custom_call_target="tpu_custom_call", output_to_operand_aliasing={{}: (4, {})} | custom-call | tf_op jit(solution)/shard_map/received_rows/pallas_call | solution.py:286
  56.2 9.4 %received_rows.4.state_in_ref = f32[12,80,256]{2,1,0:T(8,128)S(1)} custom-call(bf16[12,128,256]{2,1,0:T(8,128)(2,1)S(1)} %get-tuple-element.20.queries_ref, f32[8,256]{1,0:T(8,128)S(1)} %get-tuple-element.21.docs_ref, bf16[768,768]{1,0:T(8,128)(2,1)S(1)} %copy-done, bf16[768,768]{1,0:T(8,128)(2,1)S(1)} %copy-done.2, ...), custom_call_target="tpu_custom_call", output_to_operand_aliasing={{}: (4, {})} | custom-call | tf_op jit(solution)/shard_map/received_rows/pallas_call | solution.py:286
  65.6 9.4 %received_rows.5.state_in_ref = f32[12,80,256]{2,1,0:T(8,128)S(1)} custom-call(bf16[12,128,256]{2,1,0:T(8,128)(2,1)S(1)} %get-tuple-element.20.queries_ref, f32[8,256]{1,0:T(8,128)S(1)} %get-tuple-element.21.docs_ref, bf16[768,768]{1,0:T(8,128)(2,1)S(1)} %copy-done, bf16[768,768]{1,0:T(8,128)(2,1)S(1)} %copy-done.2, ...), custom_call_target="tpu_custom_call", output_to_operand_aliasing={{}: (4, {})} | custom-call | tf_op jit(solution)/shard_map/received_rows/pallas_call | solution.py:286
  75.1 6.1 %last_rows.1 = (bf16[64,768]{1,0:T(8,128)(2,1)S(1)}, bf16[64,768]{1,0:T(8,128)(2,1)S(1)}, bf16[64,768]{1,0:T(8,128)(2,1)S(1)}, bf16[64,768]{1,0:T(8,128)(2,1)S(1)}) custom-call(bf16[12,128,256]{2,1,0:T(8,128)(2,1)S(1)} %get-tuple-element.20.queries_ref, f32[8,256]{1,0:T(8,128)S(1)} %get-tuple-element.21.docs_ref, bf16[768,768]{1,0:T(8,128)(2,1)S(1)} %copy-done, ...), custom_call_target="tpu_custom_call" | custom-call | tf_op jit(solution)/shard_map/last_rows/pallas_call | solution.py:302
  81.3 1.6 %collective-permute-start.18 = (bf16[64,768]{1,0:T(8,128)(2,1)S(1)}, bf16[64,768]{1,0:T(8,128)(2,1)S(1)}, u32[]{:S(2)}, u32[]{:S(2)}) collective-permute-start(bf16[64,768]{1,0:T(8,128)(2,1)S(1)} %get-tuple-element.25), channel_id=1, source_target_pairs={{0,16},{8,24},{16,0},{24,8},{1,17},{9,25},{17,1},{25,9},{2,18},{10... | collective-permute-start | bytes 294920 | tf_op jit(solution)/shard_map/ppermute | solution.py:344
  83.1 3.8 %collective-permute-done.18.refs_2_ = bf16[64,768]{1,0:T(8,128)(2,1)S(1)} collective-permute-done((bf16[64,768]{1,0:T(8,128)(2,1)S(1)}, bf16[64,768]{1,0:T(8,128)(2,1)S(1)}, u32[]{:S(2)}, u32[]{:S(2)}) %collective-permute-start.18) | collective-permute-done | bytes 98336 | tf_op jit(solution)/shard_map/ppermute | solution.py:344
  88.1 1.3 %arrange.1 = bf16[256,768]{1,0:T(8,128)(2,1)} custom-call(s32[4]{0:T(128)S(1)} %copy-done.6, bf16[64,768]{1,0:T(8,128)(2,1)S(1)} %get-tuple-element.23.refs_0_, bf16[64,768]{1,0:T(8,128)(2,1)S(1)} %collective-permute-done.17.refs_1_, bf16[64,768]{1,0:T(8,128)(2,1)S(1)} %collective-permute-done.18.refs_2_, bf16[64,768]{1,0:T(8,128)(2,1)S(1)} %collective-permute-done.19.refs_3_), custom_call_target="tpu_custom_call" | custom-call | tf_op jit(solution)/shard_map/arrange/pallas_call | solution.py:330
  (45 shorter events, 13.7 us)
Async XLA Ops:
  0.0 39.0 %copy-start = (bf16[768,768]{1,0:T(8,128)(2,1)S(1)}, bf16[768,768]{1,0:T(8,128)(2,1)}, u32[]{:S(2)}) copy-start(bf16[768,768]{1,0:T(8,128)(2,1)} %wk_ref.9) | copy-start | bytes 3538948
  3.8 3.8 %collective-permute-start = (bf16[64,768]{1,0:T(8,128)(2,1)S(1)}, bf16[64,768]{1,0:T(8,128)(2,1)S(1)}, u32[]{:S(2)}, u32[]{:S(2)}) collective-permute-start(bf16[64,768]{1,0:T(8,128)(2,1)S(1)} %get-tuple-element.17), channel_id=1, source_target_pairs={{0,8},{8,0},{16,24},{24,16},{1,9},{9,1},{17,25},{25,17},{2,10},{10... | collective-permute-start | bytes 294920 | tf_op jit(solution)/shard_map/ppermute | solution.py:344
  4.4 6.2 %collective-permute-start.1 = (bf16[64,768]{1,0:T(8,128)(2,1)S(1)}, bf16[64,768]{1,0:T(8,128)(2,1)S(1)}, u32[]{:S(2)}, u32[]{:S(2)}) collective-permute-start(bf16[64,768]{1,0:T(8,128)(2,1)S(1)} %get-tuple-element.18), channel_id=1, source_target_pairs={{0,16},{8,24},{16,0},{24,8},{1,17},{9,25},{17,1},{25,9},{2,18},{10... | collective-permute-start | bytes 294920 | tf_op jit(solution)/shard_map/ppermute | solution.py:344
  6.9 5.2 %collective-permute-start.2 = (bf16[64,768]{1,0:T(8,128)(2,1)S(1)}, bf16[64,768]{1,0:T(8,128)(2,1)S(1)}, u32[]{:S(2)}, u32[]{:S(2)}) collective-permute-start(bf16[64,768]{1,0:T(8,128)(2,1)S(1)} %get-tuple-element.19), channel_id=1, source_target_pairs={{0,24},{8,16},{16,8},{24,0},{1,25},{9,17},{17,9},{25,1},{2,26},{10... | collective-permute-start | bytes 294920 | tf_op jit(solution)/shard_map/ppermute | solution.py:344
  8.5 7.5 %collective-permute-start.3 = (bf16[136,768]{1,0:T(8,128)(2,1)S(1)}, bf16[136,768]{1,0:T(8,128)(2,1)S(1)}, u32[]{:S(2)}, u32[]{:S(2)}) collective-permute-start(bf16[136,768]{1,0:T(8,128)(2,1)S(1)} %norm.2.a_ref), channel_id=1, source_target_pairs={{0,2},{2,4},{4,6},{6,7},{7,5},{5,3},{3,1},{1,0},{8,10},{10,12},{12... | collective-permute-start | bytes 626696 | tf_op jit(solution)/shard_map/ppermute | solution.py:365
  12.3 7.8 %collective-permute-start.6 = (bf16[128,768]{1,0:T(8,128)(2,1)S(1)}, bf16[128,768]{1,0:T(8,128)(2,1)S(1)}, u32[]{:S(2)}, u32[]{:S(2)}) collective-permute-start(bf16[128,768]{1,0:T(8,128)(2,1)S(1)} %norm.3.b_ref), channel_id=1, source_target_pairs={{2,0},{4,2},{6,4},{7,6},{5,7},{3,5},{1,3},{0,1},{10,8},{12,10},{14... | collective-permute-start | bytes 589832 | tf_op jit(solution)/shard_map/ppermute | solution.py:366
  13.9 10.6 %collective-permute-start.5 = (bf16[136,768]{1,0:T(8,128)(2,1)S(1)}, bf16[136,768]{1,0:T(8,128)(2,1)S(1)}, u32[]{:S(2)}, u32[]{:S(2)}) collective-permute-start(bf16[136,768]{1,0:T(8,128)(2,1)S(1)} %norm.2.a_ref), channel_id=1, source_target_pairs={{2,0},{4,2},{6,4},{7,6},{5,7},{3,5},{1,3},{0,1},{10,8},{12,10},{14... | collective-permute-start | bytes 626696 | tf_op jit(solution)/shard_map/ppermute | solution.py:366
  16.0 10.1 %collective-permute-start.7 = (bf16[136,768]{1,0:T(8,128)(2,1)S(1)}, bf16[136,768]{1,0:T(8,128)(2,1)S(1)}, u32[]{:S(2)}, u32[]{:S(2)}) collective-permute-start(bf16[136,768]{1,0:T(8,128)(2,1)S(1)} %collective-permute-done.3.rest_0_), channel_id=1, source_target_pairs={{0,2},{2,4},{4,6},{6,7},{7,5},{5,3},{3,1},{1,0},{8,10},{10,12},{12... | collective-permute-start | bytes 626696 | tf_op jit(solution)/shard_map/ppermute | solution.py:365
  17.8 9.0 %collective-permute-start.4 = (bf16[128,768]{1,0:T(8,128)(2,1)S(1)}, bf16[128,768]{1,0:T(8,128)(2,1)S(1)}, u32[]{:S(2)}, u32[]{:S(2)}) collective-permute-start(bf16[128,768]{1,0:T(8,128)(2,1)S(1)} %norm.3.b_ref), channel_id=1, source_target_pairs={{0,2},{2,4},{4,6},{6,7},{7,5},{5,3},{3,1},{1,0},{8,10},{10,12},{12... | collective-permute-start | bytes 589832 | tf_op jit(solution)/shard_map/ppermute | solution.py:365
  20.1 8.8 %collective-permute-start.10 = (bf16[128,768]{1,0:T(8,128)(2,1)S(1)}, bf16[128,768]{1,0:T(8,128)(2,1)S(1)}, u32[]{:S(2)}, u32[]{:S(2)}) collective-permute-start(bf16[128,768]{1,0:T(8,128)(2,1)S(1)} %collective-permute-done.6.rest_3_), channel_id=1, source_target_pairs={{2,0},{4,2},{6,4},{7,6},{5,7},{3,5},{1,3},{0,1},{10,8},{12,10},{14... | collective-permute-start | bytes 589832 | tf_op jit(solution)/shard_map/ppermute | solution.py:366
  24.5 8.7 %collective-permute-start.9 = (bf16[136,768]{1,0:T(8,128)(2,1)S(1)}, bf16[136,768]{1,0:T(8,128)(2,1)S(1)}, u32[]{:S(2)}, u32[]{:S(2)}) collective-permute-start(bf16[136,768]{1,0:T(8,128)(2,1)S(1)} %collective-permute-done.5.rest_2_), channel_id=1, source_target_pairs={{2,0},{4,2},{6,4},{7,6},{5,7},{3,5},{1,3},{0,1},{10,8},{12,10},{14... | collective-permute-start | bytes 626696 | tf_op jit(solution)/shard_map/ppermute | solution.py:366
  26.1 8.7 %collective-permute-start.11 = (bf16[136,768]{1,0:T(8,128)(2,1)S(1)}, bf16[136,768]{1,0:T(8,128)(2,1)S(1)}, u32[]{:S(2)}, u32[]{:S(2)}) collective-permute-start(bf16[136,768]{1,0:T(8,128)(2,1)S(1)} %collective-permute-done.7.rest_0_), channel_id=1, source_target_pairs={{0,2},{2,4},{4,6},{6,7},{7,5},{5,3},{3,1},{1,0},{8,10},{10,12},{12... | collective-permute-start | bytes 626696 | tf_op jit(solution)/shard_map/ppermute | solution.py:365
  26.8 9.8 %collective-permute-start.8 = (bf16[128,768]{1,0:T(8,128)(2,1)S(1)}, bf16[128,768]{1,0:T(8,128)(2,1)S(1)}, u32[]{:S(2)}, u32[]{:S(2)}) collective-permute-start(bf16[128,768]{1,0:T(8,128)(2,1)S(1)} %collective-permute-done.4.rest_1_), channel_id=1, source_target_pairs={{0,2},{2,4},{4,6},{6,7},{7,5},{5,3},{3,1},{1,0},{8,10},{10,12},{12... | collective-permute-start | bytes 589832 | tf_op jit(solution)/shard_map/ppermute | solution.py:365
  28.9 8.7 %collective-permute-start.14 = (bf16[128,768]{1,0:T(8,128)(2,1)S(1)}, bf16[128,768]{1,0:T(8,128)(2,1)S(1)}, u32[]{:S(2)}, u32[]{:S(2)}) collective-permute-start(bf16[128,768]{1,0:T(8,128)(2,1)S(1)} %collective-permute-done.10.rest_3_), channel_id=1, source_target_pairs={{2,0},{4,2},{6,4},{7,6},{5,7},{3,5},{1,3},{0,1},{10,8},{12,10},{14... | collective-permute-start | bytes 589832 | tf_op jit(solution)/shard_map/ppermute | solution.py:366
  33.2 32.4 %collective-permute-start.13 = (bf16[136,768]{1,0:T(8,128)(2,1)S(1)}, bf16[136,768]{1,0:T(8,128)(2,1)S(1)}, u32[]{:S(2)}, u32[]{:S(2)}) collective-permute-start(bf16[136,768]{1,0:T(8,128)(2,1)S(1)} %collective-permute-done.9.rest_2_), channel_id=1, source_target_pairs={{2,0},{4,2},{6,4},{7,6},{5,7},{3,5},{1,3},{0,1},{10,8},{12,10},{14... | collective-permute-start | bytes 626696 | tf_op jit(solution)/shard_map/ppermute | solution.py:366
  34.8 40.2 %collective-permute-start.15 = (bf16[136,768]{1,0:T(8,128)(2,1)S(1)}, bf16[136,768]{1,0:T(8,128)(2,1)S(1)}, u32[]{:S(2)}, u32[]{:S(2)}) collective-permute-start(bf16[136,768]{1,0:T(8,128)(2,1)S(1)} %collective-permute-done.11.rest_0_), channel_id=1, source_target_pairs={{0,2},{2,4},{4,6},{6,7},{7,5},{5,3},{3,1},{1,0},{8,10},{10,12},{12... | collective-permute-start | bytes 626696 | tf_op jit(solution)/shard_map/ppermute | solution.py:370
  36.6 29.0 %collective-permute-start.12 = (bf16[128,768]{1,0:T(8,128)(2,1)S(1)}, bf16[128,768]{1,0:T(8,128)(2,1)S(1)}, u32[]{:S(2)}, u32[]{:S(2)}) collective-permute-start(bf16[128,768]{1,0:T(8,128)(2,1)S(1)} %collective-permute-done.8.rest_1_), channel_id=1, source_target_pairs={{0,2},{2,4},{4,6},{6,7},{7,5},{5,3},{3,1},{1,0},{8,10},{10,12},{12... | collective-permute-start | bytes 589832 | tf_op jit(solution)/shard_map/ppermute | solution.py:365
  37.6 37.4 %collective-permute-start.16 = (bf16[128,768]{1,0:T(8,128)(2,1)S(1)}, bf16[128,768]{1,0:T(8,128)(2,1)S(1)}, u32[]{:S(2)}, u32[]{:S(2)}) collective-permute-start(bf16[128,768]{1,0:T(8,128)(2,1)S(1)} %collective-permute-done.14.rest_3_), channel_id=1, source_target_pairs={{2,0},{4,2},{6,4},{7,6},{5,7},{3,5},{1,3},{0,1},{10,8},{12,10},{14... | collective-permute-start | bytes 589832 | tf_op jit(solution)/shard_map/ppermute | solution.py:371
  39.0 1.3 %copy-start.1 = (bf16[768,768]{1,0:T(8,128)(2,1)S(1)}, bf16[768,768]{1,0:T(8,128)(2,1)}, u32[]{:S(2)}) copy-start(bf16[768,768]{1,0:T(8,128)(2,1)} %wv_ref.9) | copy-start | bytes 3538948
  41.5 5.3 %copy-start.2 = (bf16[768,768]{1,0:T(8,128)(2,1)S(1)}, bf16[768,768]{1,0:T(8,128)(2,1)}, u32[]{:S(2)}) copy-start(bf16[768,768]{1,0:T(8,128)(2,1)} %wv_ref.9) | copy-start | bytes 3538948
  65.6 9.4 %copy-start.4 = (bf16[768,768]{1,0:T(8,128)(2,1)S(1)}, bf16[768,768]{1,0:T(8,128)(2,1)}, u32[]{:S(2)}) copy-start(bf16[768,768]{1,0:T(8,128)(2,1)} %wo_ref.1) | copy-start | bytes 3538948
  81.2 1.9 %collective-permute-start.17 = (bf16[64,768]{1,0:T(8,128)(2,1)S(1)}, bf16[64,768]{1,0:T(8,128)(2,1)S(1)}, u32[]{:S(2)}, u32[]{:S(2)}) collective-permute-start(bf16[64,768]{1,0:T(8,128)(2,1)S(1)} %get-tuple-element.24), channel_id=1, source_target_pairs={{0,8},{8,0},{16,24},{24,16},{1,9},{9,1},{17,25},{25,17},{2,10},{10... | collective-permute-start | bytes 294920 | tf_op jit(solution)/shard_map/ppermute | solution.py:344
  81.3 5.7 %collective-permute-start.18 = (bf16[64,768]{1,0:T(8,128)(2,1)S(1)}, bf16[64,768]{1,0:T(8,128)(2,1)S(1)}, u32[]{:S(2)}, u32[]{:S(2)}) collective-permute-start(bf16[64,768]{1,0:T(8,128)(2,1)S(1)} %get-tuple-element.25), channel_id=1, source_target_pairs={{0,16},{8,24},{16,0},{24,8},{1,17},{9,25},{17,1},{25,9},{2,18},{10... | collective-permute-start | bytes 294920 | tf_op jit(solution)/shard_map/ppermute | solution.py:344
  82.8 5.3 %collective-permute-start.19 = (bf16[64,768]{1,0:T(8,128)(2,1)S(1)}, bf16[64,768]{1,0:T(8,128)(2,1)S(1)}, u32[]{:S(2)}, u32[]{:S(2)}) collective-permute-start(bf16[64,768]{1,0:T(8,128)(2,1)S(1)} %get-tuple-element.26), channel_id=1, source_target_pairs={{0,24},{8,16},{16,8},{24,0},{1,25},{9,17},{17,9},{25,1},{2,26},{10... | collective-permute-start | bytes 294920 | tf_op jit(solution)/shard_map/ppermute | solution.py:344
  (5 other events, 4.3 us)

commit v2 on v1

v2 whole, which is shorter than its diff:
```python
import functools
import math

import jax
import jax.numpy as jnp
from jax import lax
from jax.experimental import pallas as pl
from jax.experimental.pallas import tpu as pltpu
from jax.sharding import PartitionSpec as P

HEADS = 12
HD = 64
STEP_HEADS = 4
STEP_COLS = STEP_HEADS * HD
STATE_ROWS = HD + 16
BIG = 3.3895313892515355e38
LARGEST = 1e30
LOG2E = 1.4426950408889634
HALVES = True
VMEM_LIMIT = 32 * 1024 * 1024


def whole(shape):
    return pl.BlockSpec(shape, lambda *step: (0,) * len(shape))


def smem():
    return pl.BlockSpec(memory_space=pltpu.SMEM)


def params():
    return pltpu.CompilerParams(vmem_limit_bytes=VMEM_LIMIT)


def piece_of(listing_ref, group, groups):
    place = jnp.int32(0)
    for k in range(groups):
        place = place + jnp.where(listing_ref[k] == group, jnp.int32(k), jnp.int32(0))
    return place


def route_kernel(groups, listing_ref, series_ref, mask_ref, token_ref, *rest):
    out_refs, column_ref = rest[:-1], rest[-1]
    rows, width = series_ref.shape
    piece = rows // groups
    for part in range(rows // 128):
        line = mask_ref[part : part + 1, :].astype(jnp.float32)
        column_ref[part * 128 : (part + 1) * 128, :] = jnp.broadcast_to(line, (128, 128)).T
    own = lax.axis_index("group")
    token = token_ref[...].astype(jnp.float32)
    for r in range(groups):
        place = piece_of(listing_ref, lax.bitwise_xor(own, jnp.int32(r)), groups)
        first = pl.multiple_of(place * piece, piece)
        hidden = column_ref[pl.ds(first, piece), :] > 0.5
        arrived = series_ref[pl.ds(first, piece), :].astype(jnp.float32)
        for lane in range(0, width, 128):
            out_refs[r][:, lane : lane + 128] = jnp.where(
                hidden, token[:, lane : lane + 128], arrived[:, lane : lane + 128]
            ).astype(jnp.bfloat16)


def route(packing_list, series, recon_mask, mask_token, groups):
    rows, width = series.shape
    piece = rows // groups
    return pl.pallas_call(
        functools.partial(route_kernel, groups),
        out_shape=[jax.ShapeDtypeStruct((piece, width), jnp.bfloat16)] * groups,
        in_specs=[smem(), whole((rows, width)), whole((rows // 128, 128)), whole((1, width))],
        out_specs=[whole((piece, width))] * groups,
        grid=(1,),
        scratch_shapes=[pltpu.VMEM((rows, 128), jnp.float32)],
        compiler_params=params(),
        name="route",
    )(packing_list, series, recon_mask.reshape(rows // 128, 128), mask_token.reshape(1, width))


def norm_kernel(count, with_borders, *refs):
    piece_refs, gain_ref = refs[:count], refs[count]
    out_ref = refs[-1]
    piece = piece_refs[0].shape[0]
    gain = gain_ref[...].astype(jnp.float32)
    for i, ref in enumerate(piece_refs):
        widened = ref[...].astype(jnp.float32)
        factor = lax.rsqrt(jnp.mean(widened * widened, axis=-1, keepdims=True) + 1e-06)
        out_ref[i * piece : (i + 1) * piece, :] = (widened * factor * gain).astype(jnp.bfloat16)
    if with_borders:
        docs = refs[count + 1][...]
        width = out_ref.shape[1]
        row = lax.broadcasted_iota(jnp.int32, (8, width), 0)
        lines = jnp.zeros((8, width), jnp.float32)
        for d in (1, 2, 3):
            below = jnp.sum(jnp.where(docs < d, 1.0, 0.0), axis=-1, keepdims=True)
            lines = jnp.where(row == d, below, lines)
        out_ref[count * piece :, :] = lines.astype(jnp.bfloat16)


def norm(pieces, gain, docs=None):
    piece, width = pieces[0].shape
    count = len(pieces)
    rows = count * piece + (8 if docs is not None else 0)
    operands = list(pieces) + [gain.reshape(1, width)]
    if docs is not None:
        operands.append(docs)
    return pl.pallas_call(
        functools.partial(norm_kernel, count, docs is not None),
        out_shape=jax.ShapeDtypeStruct((rows, width), jnp.bfloat16),
        in_specs=[whole(member.shape) for member in operands],
        out_specs=whole((rows, width)),
        grid=(1,),
        compiler_params=params(),
        name="norm",
    )(*operands)


def borders_of(ref, first):
    return ref[first : first + 8, :].astype(jnp.float32)


def places_of(count, piece, shape, axis):
    own = lax.axis_index("group")
    held = lax.broadcasted_iota(jnp.int32, shape, axis)
    source = lax.bitwise_xor(held // piece, own)
    return (source * piece + held % piece).astype(jnp.float32)


def doc_numbers(borders, place):
    docs = jnp.zeros(place.shape, jnp.float32)
    for d in (1, 2, 3):
        docs = docs + jnp.where(place >= borders[d : d + 1, : place.shape[1]], 1.0, 0.0)
    return docs


def key_extras(borders, rows, piece):
    docs = doc_numbers(borders, places_of(rows, piece, (rows, 128), 0))
    column = lax.rem(lax.broadcasted_iota(jnp.int32, (rows, 128), 1), HD)
    named = jnp.where(docs == column.astype(jnp.float32), 1.0, 0.0)
    flags = jnp.where(column < 7, 1.0, 0.0)
    return jnp.where(column < 4, named, flags).astype(jnp.bfloat16)


def load_rows(parts):
    return jnp.concatenate([ref[first : first + count, :] for ref, first, count in parts], axis=0)


def scores_of(keys, extras, queries):
    low = lax.broadcasted_iota(jnp.int32, extras.shape, 1) < HD
    scores = []
    for h in range(STEP_HEADS):
        pair = keys[:, h // 2 * 128 : h // 2 * 128 + 128]
        mixed = jnp.where(low, pair, extras) if h % 2 == 0 else jnp.where(low, extras, pair)
        scores.append(jnp.dot(mixed, queries[h], preferred_element_type=jnp.float32))
    return scores


def with_ones(values, h):
    ones = jnp.ones((16, values.shape[1]), jnp.bfloat16)
    return jnp.concatenate([values[h * HD : (h + 1) * HD], ones], axis=0)


def project(x, weight_ref, j):
    columns = weight_ref[:, j * STEP_COLS : (j + 1) * STEP_COLS]
    return jnp.dot(x, columns, preferred_element_type=jnp.float32)


def own_kernel(piece, parts, borders_at, *refs):
    row_refs, (wq_ref, wk_ref, wv_ref, queries_ref, state_ref) = refs[:-5], refs[-5:]
    x = load_rows([(row_refs[i], first, count) for i, first, count in parts])
    rows = x.shape[0]
    borders = borders_of(row_refs[borders_at[0]], borders_at[1])
    docs = doc_numbers(borders, places_of(rows, piece, (8, rows), 1))
    row = lax.broadcasted_iota(jnp.int32, (HD, rows), 0)
    differs = jnp.where(docs[0:1, :] == row.astype(jnp.float32), 0.0, -BIG)
    mask_rows = jnp.where(row < 4, differs, 0.0)
    extras = key_extras(borders, rows, piece)
    for j in range(HEADS // STEP_HEADS):
        queries = project(x, wq_ref, j).astype(jnp.bfloat16).astype(jnp.float32)
        queries = (queries * (1.0 / math.sqrt(HD))).T.astype(jnp.bfloat16)
        keys = project(x, wk_ref, j).astype(jnp.bfloat16)
        values = project(x, wv_ref, j).T.astype(jnp.bfloat16)

        def stacked(h, rest):
            own = queries[h * HD : (h + 1) * HD]
            return jnp.concatenate([own, rest] if h % 2 == 0 else [rest, own], axis=0)

        plain = mask_rows.astype(jnp.bfloat16)
        scores = scores_of(keys, extras, [stacked(h, plain) for h in range(STEP_HEADS)])
        tops = [jnp.max(member, axis=0, keepdims=True) for member in scores]
        weights = [
            jnp.exp2((member - top) * LOG2E).astype(jnp.bfloat16)
            for member, top in zip(scores, tops)
        ]
        sums = [
            jnp.dot(with_ones(values, h), weights[h], preferred_element_type=jnp.float32)
            for h in range(STEP_HEADS)
        ]
        for h in range(STEP_HEADS):
            upper = tops[h].astype(jnp.bfloat16).astype(jnp.float32)
            middle = (tops[h] - upper).astype(jnp.bfloat16).astype(jnp.float32)
            lower = tops[h] - upper - middle
            rest = jnp.where(row == 4, -upper, mask_rows)
            rest = jnp.where(row == 5, -middle, rest)
            rest = jnp.where(row == 6, -lower, rest)
            queries_ref[j * STEP_HEADS + h] = stacked(h, rest.astype(jnp.bfloat16))
            state_ref[j * STEP_HEADS + h, : HD + 8, :] = sums[h][: HD + 8]
            state_ref[j * STEP_HEADS + h, HD + 8 :, :] = jnp.zeros((8, rows), jnp.float32)


def fold(piece, sources, queries_ref, wk_ref, wv_ref, state_ref, finish):
    x = jnp.concatenate([load_rows(parts) for parts, _, _ in sources], axis=0)
    extras = jnp.concatenate(
        [
            key_extras(borders_of(ref, first), sum(count for _, _, count in parts), piece)
            for parts, ref, first in sources
        ],
        axis=0,
    )
    for j in range(HEADS // STEP_HEADS):
        heads = [j * STEP_HEADS + h for h in range(STEP_HEADS)]
        keys = project(x, wk_ref, j).astype(jnp.bfloat16)
        values = project(x, wv_ref, j).T.astype(jnp.bfloat16)
        scores = scores_of(keys, extras, [queries_ref[head] for head in heads])
        weights = [jnp.exp2(member * LOG2E).astype(jnp.bfloat16) for member in scores]
        sums = [
            state_ref[head, : HD + 8, :]
            + jnp.dot(with_ones(values, h), weights[h], preferred_element_type=jnp.float32)[: HD + 8]
            for h, head in enumerate(heads)
        ]
        largest = functools.reduce(jnp.maximum, [member[HD : HD + 8] for member in sums])
        excess = functools.reduce(jnp.maximum, [state_ref[head, HD + 8 :, :] for head in heads])
        usual = jnp.logical_and(jnp.max(largest) < LARGEST, jnp.max(excess) <= 0.0)

        @pl.when(usual)
        def plain():
            finish(j, sums, None)

        @pl.when(jnp.logical_not(usual))
        def again():
            scores = scores_of(keys, extras, [queries_ref[head] for head in heads])
            tops, sums = [], []
            for h, head in enumerate(heads):
                before = state_ref[head, HD + 8 : HD + 9, :]
                top = jnp.maximum(before, jnp.max(scores[h], axis=0, keepdims=True))
                weights = jnp.exp2((scores[h] - top) * LOG2E).astype(jnp.bfloat16)
                added = jnp.dot(with_ones(values, h), weights, preferred_element_type=jnp.float32)
                factor = jnp.exp2((before - top) * LOG2E)
                sums.append(state_ref[head, : HD + 8, :] * factor + added[: HD + 8])
                tops.append(jnp.broadcast_to(top, (8, top.shape[1])))
            finish(j, sums, tops)


def named_sources(row_refs, layout):
    return [
        ([(row_refs[i], first, count) for i, first, count in parts], row_refs[at], first_border)
        for parts, (at, first_border) in layout
    ]


def chunk_kernel(piece, layout, queries_ref, wk_ref, wv_ref, old_ref, *rest):
    row_refs, state_ref = rest[:-1], rest[-1]

    def finish(j, sums, tops):
        for h in range(STEP_HEADS):
            head = j * STEP_HEADS + h
            state_ref[head, : HD + 8, :] = sums[h]
            if tops is None:
                state_ref[head, HD + 8 :, :] = jnp.zeros((8, sums[h].shape[1]), jnp.float32)
            else:
                state_ref[head, HD + 8 :, :] = tops[h]

    fold(piece, named_sources(row_refs, layout), queries_ref, wk_ref, wv_ref, old_ref, finish)


def last_kernel(groups, piece, layout, queries_ref, wk_ref, wv_ref, old_ref, wo_ref, *rest):
    row_refs = rest[: -2 * groups - 1]
    piece_refs, out_refs = rest[-2 * groups - 1 : -groups - 1], rest[-groups - 1 : -1]
    attended_ref = rest[-1]

    def finish(j, sums, tops):
        for h in range(STEP_HEADS):
            first = (j * STEP_HEADS + h) * HD
            attended_ref[first : first + HD, :] = sums[h][:HD] / sums[h][HD : HD + 1]

    fold(piece, named_sources(row_refs, layout), queries_ref, wk_ref, wv_ref, old_ref, finish)
    attended = attended_ref[...].T.astype(jnp.bfloat16)
    mixed = jnp.dot(attended, wo_ref[...], preferred_element_type=jnp.float32)
    for r in range(groups):
        out_refs[r][...] = (
            piece_refs[r][...].astype(jnp.float32) + mixed[r * piece : (r + 1) * piece]
        ).astype(jnp.bfloat16)


def vmem(count):
    return [pl.BlockSpec(memory_space=pltpu.VMEM)] * count


def cost(us):
    return pl.CostEstimate(flops=int(us * 1.1e9), bytes_accessed=0, transcendentals=0)


def own_call(members, layout, w_query, w_key, w_value, piece, rows):
    parts, borders_at = layout
    return pl.pallas_call(
        functools.partial(own_kernel, piece, parts, borders_at),
        out_shape=[
            jax.ShapeDtypeStruct((HEADS, 2 * HD, rows), jnp.bfloat16),
            jax.ShapeDtypeStruct((HEADS, STATE_ROWS, rows), jnp.float32),
        ],
        in_specs=vmem(len(members) + 3),
        out_specs=vmem(2),
        compiler_params=params(),
        cost_estimate=cost(3.0),
        name="own_rows",
    )(*members, w_query, w_key, w_value)


def chunk_call(queries, w_key, w_value, state, members, layout, piece):
    return pl.pallas_call(
        functools.partial(chunk_kernel, piece, layout),
        out_shape=jax.ShapeDtypeStruct(state.shape, jnp.float32),
        in_specs=vmem(4 + len(members)),
        out_specs=vmem(1)[0],
        compiler_params=params(),
        cost_estimate=cost(3.5),
        name="received_rows",
    )(queries, w_key, w_value, state, *members)


def last_call(queries, w_key, w_value, state, w_out, members, layout, pieces, piece):
    groups, width = len(pieces), w_key.shape[0]
    rows = queries.shape[2]
    return pl.pallas_call(
        functools.partial(last_kernel, groups, piece, layout),
        out_shape=[jax.ShapeDtypeStruct((piece, width), jnp.bfloat16)] * groups,
        in_specs=vmem(5 + len(members) + groups),
        out_specs=vmem(groups),
        scratch_shapes=[pltpu.VMEM((HEADS * HD, rows), jnp.float32)],
        compiler_params=params(),
        cost_estimate=cost(3.0),
        name="last_rows",
    )(queries, w_key, w_value, state, w_out, *members, *pieces)


def arrange_kernel(groups, listing_ref, *refs):
    piece_refs, out_ref = refs[:groups], refs[groups]
    piece = piece_refs[0].shape[0]
    own = lax.axis_index("group")
    for r in range(groups):
        place = piece_of(listing_ref, lax.bitwise_xor(own, jnp.int32(r)), groups)
        out_ref[pl.ds(pl.multiple_of(place * piece, piece), piece), :] = piece_refs[r][...]


def arrange(packing_list, pieces):
    groups, (piece, width) = len(pieces), pieces[0].shape
    return pl.pallas_call(
        functools.partial(arrange_kernel, groups),
        out_shape=jax.ShapeDtypeStruct((groups * piece, width), jnp.bfloat16),
        in_specs=[smem()] + [whole((piece, width))] * groups,
        out_specs=whole((groups * piece, width)),
        grid=(1,),
        compiler_params=params(),
        name="arrange",
    )(packing_list, *pieces)


def exchange(pieces):
    groups = len(pieces)
    return [pieces[0]] + [
        lax.ppermute(pieces[r], "group", [(i, i ^ r) for i in range(groups)])
        for r in range(1, groups)
    ]


def on_device(
    series, recon_mask, mask_token, packing_list, doc_ids, norm_gain, w_query, w_key, w_value, w_out
):
    groups, shards = lax.axis_size("group"), lax.axis_size("ctx")
    rows, width = series.shape
    piece = rows // groups
    ring = list(range(0, shards, 2)) + list(range(shards - 1, 0, -2))
    onward = [(ring[i], ring[(i + 1) % shards]) for i in range(shards)]
    backward = [(there, here) for here, there in onward]

    pieces = exchange(route(packing_list, series, recon_mask, mask_token, groups))
    half = rows // 2
    if HALVES:
        own = (
            norm(pieces[: groups // 2], norm_gain, doc_ids),
            norm(pieces[groups // 2 :], norm_gain),
        )
        parts = [(0, 0, half), (1, 0, half)]
        own_layout = (parts, (0, half))
        pair_layout = (own_layout, ([(2, 0, half), (3, 0, half)], (2, half)))
        far_layout = (own_layout,)
    else:
        own = (norm(pieces, norm_gain, doc_ids),)
        own_layout = ([(0, 0, rows)], (0, rows))
        pair_layout = (own_layout, ([(1, 0, rows)], (1, rows)))
        far_layout = (([(0, 0, half), (1, 0, half)], (1, half)),)
    queries, state = own_call(own, own_layout, w_query, w_key, w_value, piece, rows)
    before, after = own, own
    for step in range(1, shards // 2):
        before = tuple(lax.ppermute(member, "ctx", onward) for member in before)
        after = tuple(lax.ppermute(member, "ctx", backward) for member in after)
        state = chunk_call(queries, w_key, w_value, state, before + after, pair_layout, piece)
    if HALVES:
        far = (
            lax.ppermute(before[0], "ctx", onward),
            lax.ppermute(after[1], "ctx", backward),
        )
    else:
        far = (
            lax.ppermute(before[0][:half], "ctx", onward),
            lax.ppermute(after[0][half:], "ctx", backward),
        )
    done = last_call(queries, w_key, w_value, state, w_out, far, far_layout, pieces, piece)
    return arrange(packing_list, exchange(done))


def solution(mesh):
    in_specs = (
        P(("group", "ctx"), None),
        P(("group", "ctx")),
        P(),
        P(("group", "ctx")),
        P("group", "ctx"),
        P(),
        P(),
        P(),
        P(),
        P(),
    )
    out_specs = P(("group", "ctx"), None)
    return jax.shard_map(
        on_device, mesh=mesh, in_specs=in_specs, out_specs=out_specs, check_vma=False
    )
```

time: 89.7 us -> 62.2 us (0.69)
  Pallas kernels: 41.8 us -> 19.1 us
  starting transfers between devices: 25 us -> 19.7 us
  local copies, waits for them, and re-layouts: 7.03 us -> 8.21 us
    pallas_call x5, Pallas kernels: 39.5 us -> 16.8 us  [the longest x3 10.8 us: chunk_call(): pl.pallas_call(functools.partial(chunk_kernel, piece, layout), out_shape=...]
    ppermute x6, waiting for transfers between devices: 6.55 us -> 0.11 us  [on_device(): after = tuple((lax.ppermute(member, 'ctx', backward) for member in after))]
    ppermute x6, starting transfers between devices: 9.31 us -> 6.09 us  [on_device(): after = tuple((lax.ppermute(member, 'ctx', backward) for member in after))]
    ppermute x6, starting transfers between devices: 8.75 us -> 6.42 us  [on_device(): before = tuple((lax.ppermute(member, 'ctx', onward) for member in before))]
    ppermute x6, waiting for transfers between devices: 6.79 us -> 9.02 us  [exchange(): lax.ppermute(pieces[r], 'group', [(i, i ^ r) for i in range(groups)])]
    ppermute x6, waiting for transfers between devices: 2.07 us -> 3.89 us  [on_device(): before = tuple((lax.ppermute(member, 'ctx', onward) for member in before))]
    ppermute x2, waiting for transfers between devices: 0.01 us -> 1.67 us  [the longest x1 1.67 us: on_device(): lax.ppermute(before[0], 'ctx', onward)]
    unnamed x18 -> x22, local copies, waits for them, and re-layouts: 5.56 us -> 6.84 us
  transfers between devices with their start and end apart: 20 -> 20, of which waited for: 10 -> 7; matrix products, arithmetic and copies ran while one was open for 1% -> 1% of each run, Pallas kernels for 38% -> 22%
where the time goes in v2:
time: 62.2 us; the launch traced here: 61.9 us
  starting transfers between devices  19.7 us (32%)
  Pallas kernels  19.1 us (31%)
  waiting for transfers between devices  14.7 us (24%)
  local copies, waits for them, and re-layouts  8.21 us (13%)
    pallas_call x3, Pallas kernels, chunk_call(): pl.pallas_call(functools.partial(chunk_kernel, piece, layout), out_shape=...  10.8 us
    ppermute x6, waiting for transfers between devices, exchange(): lax.ppermute(pieces[r], 'group', [(i, i ^ r) for i in range(groups)])  9.02 us
    unnamed x22, local copies, waits for them, and re-layouts  6.84 us
    ppermute x6, starting transfers between devices, on_device(): before = tuple((lax.ppermute(member, 'ctx', onward) for member in before))  6.42 us
    ppermute x6, starting transfers between devices, on_device(): after = tuple((lax.ppermute(member, 'ctx', backward) for member in after))  6.09 us
    ppermute x6, starting transfers between devices, exchange(): lax.ppermute(pieces[r], 'group', [(i, i ^ r) for i in range(groups)])  5.13 us
    ppermute x6, waiting for transfers between devices, on_device(): before = tuple((lax.ppermute(member, 'ctx', onward) for member in before))  3.89 us
    pallas_call x1, Pallas kernels, last_call(): pl.pallas_call(functools.partial(last_kernel, groups, piece, layout), out...  3.26 us
  transfers between devices with their start and end apart: 20, of which 7 were waited for; matrix products, arithmetic and copies ran while one was open for 1% of the time, Pallas kernels for 22%

profile of v2, /device:TPU:0, one launch (start us, length us, event | category | flops | bytes accessed | tf_op | source)
XLA Modules:
  0.0 61.9 jit_solution(16407516009111658454)
XLA Ops:
  0.7 1.0 %copy-done = bf16[256,768]{1,0:T(8,128)(2,1)S(1)} copy-done((bf16[256,768]{1,0:T(8,128)(2,1)S(1)}, bf16[256,768]{1,0:T(8,128)(2,1)}, u32[]{:S(2)}) %copy-start) | copy-done | bytes 393240
  3.7 3.0 %collective-permute-start.1 = (bf16[64,768]{1,0:T(8,128)(2,1)S(1)}, bf16[64,768]{1,0:T(8,128)(2,1)S(1)}, u32[]{:S(2)}, u32[]{:S(2)}) collective-permute-start(bf16[64,768]{1,0:T(8,128)(2,1)S(1)} %get-tuple-element.17), channel_id=1, source_target_pairs={{0,16},{8,24},{16,0},{24,8},{1,17},{9,25},{17,1},{25,9},{2,18},{10... | collective-permute-start | bytes 294920 | tf_op jit(solution)/shard_map/ppermute | solution.py:368
  7.6 2.2 %collective-permute-done.1.refs_0_.rest_4_ = bf16[64,768]{1,0:T(8,128)(2,1)S(1)} collective-permute-done((bf16[64,768]{1,0:T(8,128)(2,1)S(1)}, bf16[64,768]{1,0:T(8,128)(2,1)S(1)}, u32[]{:S(2)}, u32[]{:S(2)}) %collective-permute-start.1) | collective-permute-done | bytes 98336 | tf_op jit(solution)/shard_map/ppermute | solution.py:368
  9.8 1.8 %collective-permute-done.2.refs_1_.rest_5_ = bf16[64,768]{1,0:T(8,128)(2,1)S(1)} collective-permute-done((bf16[64,768]{1,0:T(8,128)(2,1)S(1)}, bf16[64,768]{1,0:T(8,128)(2,1)S(1)}, u32[]{:S(2)}, u32[]{:S(2)}) %collective-permute-start.2) | collective-permute-done | bytes 98336 | tf_op jit(solution)/shard_map/ppermute | solution.py:368
  11.8 1.8 %collective-permute-start.4 = (bf16[128,768]{1,0:T(8,128)(2,1)S(1)}, bf16[128,768]{1,0:T(8,128)(2,1)S(1)}, u32[]{:S(2)}, u32[]{:S(2)}) collective-permute-start(bf16[128,768]{1,0:T(8,128)(2,1)S(1)} %norm.3.refs_1_), channel_id=1, source_target_pairs={{0,2},{2,4},{4,6},{6,7},{7,5},{5,3},{3,1},{1,0},{8,10},{10,12},{12... | collective-permute-start | bytes 589832 | tf_op jit(solution)/shard_map/ppermute | solution.py:402
  14.7 1.8 %collective-permute-start.3 = (bf16[136,768]{1,0:T(8,128)(2,1)S(1)}, bf16[136,768]{1,0:T(8,128)(2,1)S(1)}, u32[]{:S(2)}, u32[]{:S(2)}) collective-permute-start(bf16[136,768]{1,0:T(8,128)(2,1)S(1)} %norm.2.refs_0_), channel_id=1, source_target_pairs={{0,2},{2,4},{4,6},{6,7},{7,5},{5,3},{3,1},{1,0},{8,10},{10,12},{12... | collective-permute-start | bytes 626696 | tf_op jit(solution)/shard_map/ppermute | solution.py:402
  16.8 1.3 %copy-done.5 = bf16[768,768]{1,0:T(8,128)(2,1)S(1)} copy-done((bf16[768,768]{1,0:T(8,128)(2,1)S(1)}, bf16[768,768]{1,0:T(8,128)(2,1)}, u32[]{:S(2)}) %copy-start.5) | copy-done | bytes 1179672
  18.0 1.3 %copy-done.6 = bf16[768,768]{1,0:T(8,128)(2,1)S(1)} copy-done((bf16[768,768]{1,0:T(8,128)(2,1)S(1)}, bf16[768,768]{1,0:T(8,128)(2,1)}, u32[]{:S(2)}) %copy-start.6) | copy-done | bytes 1179672
  19.3 1.3 %copy-done.8 = bf16[768,768]{1,0:T(8,128)(2,1)S(1)} copy-done((bf16[768,768]{1,0:T(8,128)(2,1)S(1)}, bf16[768,768]{1,0:T(8,128)(2,1)}, u32[]{:S(2)}) %copy-start.8) | copy-done | bytes 1179672
  20.6 2.7 %own_rows.1 = (bf16[12,128,256]{2,1,0:T(8,128)(2,1)S(1)}, f32[12,80,256]{2,1,0:T(8,128)S(1)}) custom-call(bf16[136,768]{1,0:T(8,128)(2,1)S(1)} %norm.2.refs_0_, bf16[128,768]{1,0:T(8,128)(2,1)S(1)} %norm.3.refs_1_, bf16[768,768]{1,0:T(8,128)(2,1)S(1)} %copy-done.5, bf16[768,768]{1,0:T(8,128)(2,1)S(1)} %copy-done.6, bf16[768,768]{1,0:T(8,128)(2,1)S(1)} %copy-done.8), custom_call_target="tpu_custom_call" | custom-call | flops 3300000000 | tf_op jit(solution)/shard_map/own_rows/pallas_call | solution.py:302
  23.3 1.8 %collective-permute-start.10 = (bf16[128,768]{1,0:T(8,128)(2,1)S(1)}, bf16[128,768]{1,0:T(8,128)(2,1)S(1)}, u32[]{:S(2)}, u32[]{:S(2)}) collective-permute-start(bf16[128,768]{1,0:T(8,128)(2,1)S(1)} %collective-permute-done.6.rest_3_), channel_id=1, source_target_pairs={{2,0},{4,2},{6,4},{7,6},{5,7},{3,5},{1,3},{0,1},{10,8},{12,10},{14... | collective-permute-start | bytes 589832 | tf_op jit(solution)/shard_map/ppermute | solution.py:403
  25.4 1.8 %collective-permute-start.7 = (bf16[136,768]{1,0:T(8,128)(2,1)S(1)}, bf16[136,768]{1,0:T(8,128)(2,1)S(1)}, u32[]{:S(2)}, u32[]{:S(2)}) collective-permute-start(bf16[136,768]{1,0:T(8,128)(2,1)S(1)} %collective-permute-done.3.rest_0_), channel_id=1, source_target_pairs={{0,2},{2,4},{4,6},{6,7},{7,5},{5,3},{3,1},{1,0},{8,10},{10,12},{12... | collective-permute-start | bytes 626696 | tf_op jit(solution)/shard_map/ppermute | solution.py:402
  27.4 3.6 %received_rows.3.old_ref = f32[12,80,256]{2,1,0:T(8,128)S(1)} custom-call(bf16[12,128,256]{2,1,0:T(8,128)(2,1)S(1)} %get-tuple-element.19.queries_ref, bf16[768,768]{1,0:T(8,128)(2,1)S(1)} %copy-done.7, bf16[768,768]{1,0:T(8,128)(2,1)S(1)} %copy-done.9, f32[12,80,256]{2,1,0:T(8,128)S(1)} %get-tuple-element.20.old_ref, ...), custom_call_target="tpu_custom_call" | custom-call | flops 3849999872 | tf_op jit(solution)/shard_map/received_rows/pallas_call | solution.py:317
  31.0 1.9 %collective-permute-start.14 = (bf16[128,768]{1,0:T(8,128)(2,1)S(1)}, bf16[128,768]{1,0:T(8,128)(2,1)S(1)}, u32[]{:S(2)}, u32[]{:S(2)}) collective-permute-start(bf16[128,768]{1,0:T(8,128)(2,1)S(1)} %collective-permute-done.10.rest_3_), channel_id=1, source_target_pairs={{2,0},{4,2},{6,4},{7,6},{5,7},{3,5},{1,3},{0,1},{10,8},{12,10},{14... | collective-permute-start | bytes 589832 | tf_op jit(solution)/shard_map/ppermute | solution.py:403
  33.2 3.9 %collective-permute-done.7.rest_0_ = bf16[136,768]{1,0:T(8,128)(2,1)S(1)} collective-permute-done((bf16[136,768]{1,0:T(8,128)(2,1)S(1)}, bf16[136,768]{1,0:T(8,128)(2,1)S(1)}, u32[]{:S(2)}, u32[]{:S(2)}) %collective-permute-start.7) | collective-permute-done | bytes 208928 | tf_op jit(solution)/shard_map/ppermute | solution.py:402
  37.5 1.6 %collective-permute-start.13 = (bf16[136,768]{1,0:T(8,128)(2,1)S(1)}, bf16[136,768]{1,0:T(8,128)(2,1)S(1)}, u32[]{:S(2)}, u32[]{:S(2)}) collective-permute-start(bf16[136,768]{1,0:T(8,128)(2,1)S(1)} %collective-permute-done.9.rest_2_), channel_id=1, source_target_pairs={{2,0},{4,2},{6,4},{7,6},{5,7},{3,5},{1,3},{0,1},{10,8},{12,10},{14... | collective-permute-start | bytes 626696 | tf_op jit(solution)/shard_map/ppermute | solution.py:403
  39.1 3.7 %received_rows.4.old_ref = f32[12,80,256]{2,1,0:T(8,128)S(1)} custom-call(bf16[12,128,256]{2,1,0:T(8,128)(2,1)S(1)} %get-tuple-element.19.queries_ref, bf16[768,768]{1,0:T(8,128)(2,1)S(1)} %copy-done.7, bf16[768,768]{1,0:T(8,128)(2,1)S(1)} %copy-done.9, f32[12,80,256]{2,1,0:T(8,128)S(1)} %received_rows.3.old_ref, ...), custom_call_target="tpu_custom_call" | custom-call | flops 3849999872 | tf_op jit(solution)/shard_map/received_rows/pallas_call | solution.py:317
  42.9 1.6 %collective-permute-start.16 = (bf16[128,768]{1,0:T(8,128)(2,1)S(1)}, bf16[128,768]{1,0:T(8,128)(2,1)S(1)}, u32[]{:S(2)}, u32[]{:S(2)}) collective-permute-start(bf16[128,768]{1,0:T(8,128)(2,1)S(1)} %collective-permute-done.14.rest_3_), channel_id=1, source_target_pairs={{2,0},{4,2},{6,4},{7,6},{5,7},{3,5},{1,3},{0,1},{10,8},{12,10},{14... | collective-permute-start | bytes 589832 | tf_op jit(solution)/shard_map/ppermute | solution.py:408
  45.1 3.6 %received_rows.5.old_ref = f32[12,80,256]{2,1,0:T(8,128)S(1)} custom-call(bf16[12,128,256]{2,1,0:T(8,128)(2,1)S(1)} %get-tuple-element.19.queries_ref, bf16[768,768]{1,0:T(8,128)(2,1)S(1)} %copy-done.7, bf16[768,768]{1,0:T(8,128)(2,1)S(1)} %copy-done.9, f32[12,80,256]{2,1,0:T(8,128)S(1)} %received_rows.4.old_ref, ...), custom_call_target="tpu_custom_call" | custom-call | flops 3849999872 | tf_op jit(solution)/shard_map/received_rows/pallas_call | solution.py:317
  48.7 1.7 %collective-permute-done.15.rest_0_ = bf16[136,768]{1,0:T(8,128)(2,1)S(1)} collective-permute-done((bf16[136,768]{1,0:T(8,128)(2,1)S(1)}, bf16[136,768]{1,0:T(8,128)(2,1)S(1)}, u32[]{:S(2)}, u32[]{:S(2)}) %collective-permute-start.15) | collective-permute-done | bytes 208928 | tf_op jit(solution)/shard_map/ppermute | solution.py:407
  50.3 3.3 %last_rows.1 = (bf16[64,768]{1,0:T(8,128)(2,1)S(1)}, bf16[64,768]{1,0:T(8,128)(2,1)S(1)}, bf16[64,768]{1,0:T(8,128)(2,1)S(1)}, bf16[64,768]{1,0:T(8,128)(2,1)S(1)}) custom-call(bf16[12,128,256]{2,1,0:T(8,128)(2,1)S(1)} %get-tuple-element.19.queries_ref, bf16[768,768]{1,0:T(8,128)(2,1)S(1)} %copy-done.7, bf16[768,768]{1,0:T(8,128)(2,1)S(1)} %copy-done.9, ...), custom_call_target="tpu_custom_call" | custom-call | flops 3300000000 | tf_op jit(solution)/shard_map/last_rows/pallas_call | solution.py:331
  55.5 3.8 %collective-permute-done.18.refs_2_ = bf16[64,768]{1,0:T(8,128)(2,1)S(1)} collective-permute-done((bf16[64,768]{1,0:T(8,128)(2,1)S(1)}, bf16[64,768]{1,0:T(8,128)(2,1)S(1)}, u32[]{:S(2)}, u32[]{:S(2)}) %collective-permute-start.18) | collective-permute-done | bytes 98336 | tf_op jit(solution)/shard_map/ppermute | solution.py:368
  59.3 1.2 %collective-permute-done.19.refs_3_ = bf16[64,768]{1,0:T(8,128)(2,1)S(1)} collective-permute-done((bf16[64,768]{1,0:T(8,128)(2,1)S(1)}, bf16[64,768]{1,0:T(8,128)(2,1)S(1)}, u32[]{:S(2)}, u32[]{:S(2)}) %collective-permute-start.19) | collective-permute-done | bytes 98336 | tf_op jit(solution)/shard_map/ppermute | solution.py:368
  60.5 1.3 %arrange.1 = bf16[256,768]{1,0:T(8,128)(2,1)} custom-call(s32[4]{0:T(128)S(1)} %copy-done.2, bf16[64,768]{1,0:T(8,128)(2,1)S(1)} %get-tuple-element.21.refs_0_, bf16[64,768]{1,0:T(8,128)(2,1)S(1)} %collective-permute-done.17.refs_1_, bf16[64,768]{1,0:T(8,128)(2,1)S(1)} %collective-permute-done.18.refs_2_, bf16[64,768]{1,0:T(8,128)(2,1)S(1)} %collective-permute-done.19.refs_3_), custom_call_target="tpu_custom_call" | custom-call | tf_op jit(solution)/shard_map/arrange/pallas_call | solution.py:354
  (49 shorter events, 9.0 us)
Async XLA Ops:
  3.7 6.1 %collective-permute-start.1 = (bf16[64,768]{1,0:T(8,128)(2,1)S(1)}, bf16[64,768]{1,0:T(8,128)(2,1)S(1)}, u32[]{:S(2)}, u32[]{:S(2)}) collective-permute-start(bf16[64,768]{1,0:T(8,128)(2,1)S(1)} %get-tuple-element.17), channel_id=1, source_target_pairs={{0,16},{8,24},{16,0},{24,8},{1,17},{9,25},{17,1},{25,9},{2,18},{10... | collective-permute-start | bytes 294920 | tf_op jit(solution)/shard_map/ppermute | solution.py:368
  6.7 4.9 %collective-permute-start.2 = (bf16[64,768]{1,0:T(8,128)(2,1)S(1)}, bf16[64,768]{1,0:T(8,128)(2,1)S(1)}, u32[]{:S(2)}, u32[]{:S(2)}) collective-permute-start(bf16[64,768]{1,0:T(8,128)(2,1)S(1)} %get-tuple-element.18), channel_id=1, source_target_pairs={{0,24},{8,16},{16,8},{24,0},{1,25},{9,17},{17,9},{25,1},{2,26},{10... | collective-permute-start | bytes 294920 | tf_op jit(solution)/shard_map/ppermute | solution.py:368
  6.7 7.1 %collective-permute-start = (bf16[64,768]{1,0:T(8,128)(2,1)S(1)}, bf16[64,768]{1,0:T(8,128)(2,1)S(1)}, u32[]{:S(2)}, u32[]{:S(2)}) collective-permute-start(bf16[64,768]{1,0:T(8,128)(2,1)S(1)} %get-tuple-element.16), channel_id=1, source_target_pairs={{0,8},{8,0},{16,24},{24,16},{1,9},{9,1},{17,25},{25,17},{2,10},{10... | collective-permute-start | bytes 294920 | tf_op jit(solution)/shard_map/ppermute | solution.py:368
  11.8 13.3 %collective-permute-start.4 = (bf16[128,768]{1,0:T(8,128)(2,1)S(1)}, bf16[128,768]{1,0:T(8,128)(2,1)S(1)}, u32[]{:S(2)}, u32[]{:S(2)}) collective-permute-start(bf16[128,768]{1,0:T(8,128)(2,1)S(1)} %norm.3.refs_1_), channel_id=1, source_target_pairs={{0,2},{2,4},{4,6},{6,7},{7,5},{5,3},{3,1},{1,0},{8,10},{10,12},{12... | collective-permute-start | bytes 589832 | tf_op jit(solution)/shard_map/ppermute | solution.py:402
  13.6 9.7 %collective-permute-start.6 = (bf16[128,768]{1,0:T(8,128)(2,1)S(1)}, bf16[128,768]{1,0:T(8,128)(2,1)S(1)}, u32[]{:S(2)}, u32[]{:S(2)}) collective-permute-start(bf16[128,768]{1,0:T(8,128)(2,1)S(1)} %norm.3.refs_1_), channel_id=1, source_target_pairs={{2,0},{4,2},{6,4},{7,6},{5,7},{3,5},{1,3},{0,1},{10,8},{12,10},{14... | collective-permute-start | bytes 589832 | tf_op jit(solution)/shard_map/ppermute | solution.py:403
  14.7 10.7 %collective-permute-start.3 = (bf16[136,768]{1,0:T(8,128)(2,1)S(1)}, bf16[136,768]{1,0:T(8,128)(2,1)S(1)}, u32[]{:S(2)}, u32[]{:S(2)}) collective-permute-start(bf16[136,768]{1,0:T(8,128)(2,1)S(1)} %norm.2.refs_0_), channel_id=1, source_target_pairs={{0,2},{2,4},{4,6},{6,7},{7,5},{5,3},{3,1},{1,0},{8,10},{10,12},{12... | collective-permute-start | bytes 626696 | tf_op jit(solution)/shard_map/ppermute | solution.py:402
  16.5 10.6 %collective-permute-start.5 = (bf16[136,768]{1,0:T(8,128)(2,1)S(1)}, bf16[136,768]{1,0:T(8,128)(2,1)S(1)}, u32[]{:S(2)}, u32[]{:S(2)}) collective-permute-start(bf16[136,768]{1,0:T(8,128)(2,1)S(1)} %norm.2.refs_0_), channel_id=1, source_target_pairs={{2,0},{4,2},{6,4},{7,6},{5,7},{3,5},{1,3},{0,1},{10,8},{12,10},{14... | collective-permute-start | bytes 626696 | tf_op jit(solution)/shard_map/ppermute | solution.py:403
  20.6 6.8 %copy-start.7 = (bf16[768,768]{1,0:T(8,128)(2,1)S(1)}, bf16[768,768]{1,0:T(8,128)(2,1)}, u32[]{:S(2)}) copy-start(bf16[768,768]{1,0:T(8,128)(2,1)} %wk_ref.7) | copy-start | bytes 3538948
  20.6 6.8 %copy-start.9 = (bf16[768,768]{1,0:T(8,128)(2,1)S(1)}, bf16[768,768]{1,0:T(8,128)(2,1)}, u32[]{:S(2)}) copy-start(bf16[768,768]{1,0:T(8,128)(2,1)} %wv_ref.7) | copy-start | bytes 3538948
  23.3 7.7 %collective-permute-start.10 = (bf16[128,768]{1,0:T(8,128)(2,1)S(1)}, bf16[128,768]{1,0:T(8,128)(2,1)S(1)}, u32[]{:S(2)}, u32[]{:S(2)}) collective-permute-start(bf16[128,768]{1,0:T(8,128)(2,1)S(1)} %collective-permute-done.6.rest_3_), channel_id=1, source_target_pairs={{2,0},{4,2},{6,4},{7,6},{5,7},{3,5},{1,3},{0,1},{10,8},{12,10},{14... | collective-permute-start | bytes 589832 | tf_op jit(solution)/shard_map/ppermute | solution.py:403
  25.0 7.8 %collective-permute-start.8 = (bf16[128,768]{1,0:T(8,128)(2,1)S(1)}, bf16[128,768]{1,0:T(8,128)(2,1)S(1)}, u32[]{:S(2)}, u32[]{:S(2)}) collective-permute-start(bf16[128,768]{1,0:T(8,128)(2,1)S(1)} %collective-permute-done.4.rest_1_), channel_id=1, source_target_pairs={{0,2},{2,4},{4,6},{6,7},{7,5},{5,3},{3,1},{1,0},{8,10},{10,12},{12... | collective-permute-start | bytes 589832 | tf_op jit(solution)/shard_map/ppermute | solution.py:402
  25.4 11.7 %collective-permute-start.7 = (bf16[136,768]{1,0:T(8,128)(2,1)S(1)}, bf16[136,768]{1,0:T(8,128)(2,1)S(1)}, u32[]{:S(2)}, u32[]{:S(2)}) collective-permute-start(bf16[136,768]{1,0:T(8,128)(2,1)S(1)} %collective-permute-done.3.rest_0_), channel_id=1, source_target_pairs={{0,2},{2,4},{4,6},{6,7},{7,5},{5,3},{3,1},{1,0},{8,10},{10,12},{12... | collective-permute-start | bytes 626696 | tf_op jit(solution)/shard_map/ppermute | solution.py:402
  27.1 10.4 %collective-permute-start.9 = (bf16[136,768]{1,0:T(8,128)(2,1)S(1)}, bf16[136,768]{1,0:T(8,128)(2,1)S(1)}, u32[]{:S(2)}, u32[]{:S(2)}) collective-permute-start(bf16[136,768]{1,0:T(8,128)(2,1)S(1)} %collective-permute-done.5.rest_2_), channel_id=1, source_target_pairs={{2,0},{4,2},{6,4},{7,6},{5,7},{3,5},{1,3},{0,1},{10,8},{12,10},{14... | collective-permute-start | bytes 626696 | tf_op jit(solution)/shard_map/ppermute | solution.py:403
  31.0 11.9 %collective-permute-start.14 = (bf16[128,768]{1,0:T(8,128)(2,1)S(1)}, bf16[128,768]{1,0:T(8,128)(2,1)S(1)}, u32[]{:S(2)}, u32[]{:S(2)}) collective-permute-start(bf16[128,768]{1,0:T(8,128)(2,1)S(1)} %collective-permute-done.10.rest_3_), channel_id=1, source_target_pairs={{2,0},{4,2},{6,4},{7,6},{5,7},{3,5},{1,3},{0,1},{10,8},{12,10},{14... | collective-permute-start | bytes 589832 | tf_op jit(solution)/shard_map/ppermute | solution.py:403
  32.9 12.1 %collective-permute-start.12 = (bf16[128,768]{1,0:T(8,128)(2,1)S(1)}, bf16[128,768]{1,0:T(8,128)(2,1)S(1)}, u32[]{:S(2)}, u32[]{:S(2)}) collective-permute-start(bf16[128,768]{1,0:T(8,128)(2,1)S(1)} %collective-permute-done.8.rest_1_), channel_id=1, source_target_pairs={{0,2},{2,4},{4,6},{6,7},{7,5},{5,3},{3,1},{1,0},{8,10},{10,12},{12... | collective-permute-start | bytes 589832 | tf_op jit(solution)/shard_map/ppermute | solution.py:402
  37.1 7.4 %collective-permute-start.11 = (bf16[136,768]{1,0:T(8,128)(2,1)S(1)}, bf16[136,768]{1,0:T(8,128)(2,1)S(1)}, u32[]{:S(2)}, u32[]{:S(2)}) collective-permute-start(bf16[136,768]{1,0:T(8,128)(2,1)S(1)} %collective-permute-done.7.rest_0_), channel_id=1, source_target_pairs={{0,2},{2,4},{4,6},{6,7},{7,5},{5,3},{3,1},{1,0},{8,10},{10,12},{12... | collective-permute-start | bytes 626696 | tf_op jit(solution)/shard_map/ppermute | solution.py:402
  37.5 7.6 %collective-permute-start.13 = (bf16[136,768]{1,0:T(8,128)(2,1)S(1)}, bf16[136,768]{1,0:T(8,128)(2,1)S(1)}, u32[]{:S(2)}, u32[]{:S(2)}) collective-permute-start(bf16[136,768]{1,0:T(8,128)(2,1)S(1)} %collective-permute-done.9.rest_2_), channel_id=1, source_target_pairs={{2,0},{4,2},{6,4},{7,6},{5,7},{3,5},{1,3},{0,1},{10,8},{12,10},{14... | collective-permute-start | bytes 626696 | tf_op jit(solution)/shard_map/ppermute | solution.py:403
  42.9 7.5 %copy-start.10 = (bf16[768,768]{1,0:T(8,128)(2,1)S(1)}, bf16[768,768]{1,0:T(8,128)(2,1)}, u32[]{:S(2)}) copy-start(bf16[768,768]{1,0:T(8,128)(2,1)} %wo_ref.1) | copy-start | bytes 3538948
  42.9 5.8 %collective-permute-start.16 = (bf16[128,768]{1,0:T(8,128)(2,1)S(1)}, bf16[128,768]{1,0:T(8,128)(2,1)S(1)}, u32[]{:S(2)}, u32[]{:S(2)}) collective-permute-start(bf16[128,768]{1,0:T(8,128)(2,1)S(1)} %collective-permute-done.14.rest_3_), channel_id=1, source_target_pairs={{2,0},{4,2},{6,4},{7,6},{5,7},{3,5},{1,3},{0,1},{10,8},{12,10},{14... | collective-permute-start | bytes 589832 | tf_op jit(solution)/shard_map/ppermute | solution.py:408
  44.5 5.8 %collective-permute-start.15 = (bf16[136,768]{1,0:T(8,128)(2,1)S(1)}, bf16[136,768]{1,0:T(8,128)(2,1)S(1)}, u32[]{:S(2)}, u32[]{:S(2)}) collective-permute-start(bf16[136,768]{1,0:T(8,128)(2,1)S(1)} %collective-permute-done.11.rest_0_), channel_id=1, source_target_pairs={{0,2},{2,4},{4,6},{6,7},{7,5},{5,3},{3,1},{1,0},{8,10},{10,12},{12... | collective-permute-start | bytes 626696 | tf_op jit(solution)/shard_map/ppermute | solution.py:407
  48.6 11.9 %copy-start.2 = (s32[4]{0:T(128)S(1)}, s32[4]{0:T(128)}, u32[]{:S(2)}) copy-start(s32[4]{0:T(128)} %listing_ref.3) | copy-start | bytes 52
  53.6 1.9 %collective-permute-start.17 = (bf16[64,768]{1,0:T(8,128)(2,1)S(1)}, bf16[64,768]{1,0:T(8,128)(2,1)S(1)}, u32[]{:S(2)}, u32[]{:S(2)}) collective-permute-start(bf16[64,768]{1,0:T(8,128)(2,1)S(1)} %get-tuple-element.22), channel_id=1, source_target_pairs={{0,8},{8,0},{16,24},{24,16},{1,9},{9,1},{17,25},{25,17},{2,10},{10... | collective-permute-start | bytes 294920 | tf_op jit(solution)/shard_map/ppermute | solution.py:368
  53.7 5.7 %collective-permute-start.18 = (bf16[64,768]{1,0:T(8,128)(2,1)S(1)}, bf16[64,768]{1,0:T(8,128)(2,1)S(1)}, u32[]{:S(2)}, u32[]{:S(2)}) collective-permute-start(bf16[64,768]{1,0:T(8,128)(2,1)S(1)} %get-tuple-element.23), channel_id=1, source_target_pairs={{0,16},{8,24},{16,0},{24,8},{1,17},{9,25},{17,1},{25,9},{2,18},{10... | collective-permute-start | bytes 294920 | tf_op jit(solution)/shard_map/ppermute | solution.py:368
  54.6 6.0 %collective-permute-start.19 = (bf16[64,768]{1,0:T(8,128)(2,1)S(1)}, bf16[64,768]{1,0:T(8,128)(2,1)S(1)}, u32[]{:S(2)}, u32[]{:S(2)}) collective-permute-start(bf16[64,768]{1,0:T(8,128)(2,1)S(1)} %get-tuple-element.24), channel_id=1, source_target_pairs={{0,24},{8,16},{16,8},{24,0},{1,25},{9,17},{17,9},{25,1},{2,26},{10... | collective-permute-start | bytes 294920 | tf_op jit(solution)/shard_map/ppermute | solution.py:368
  (7 other events, 6.8 us)

commit v3 on v2

--- a/solution.py
+++ b/solution.py
@@ -16,20 +16,28 @@
 BIG = 3.3895313892515355e38
 LARGEST = 1e30
 LOG2E = 1.4426950408889634
-HALVES = True
 VMEM_LIMIT = 32 * 1024 * 1024
-
-
-def whole(shape):
-    return pl.BlockSpec(shape, lambda *step: (0,) * len(shape))
+LARGE = 56 * 1024 * 1024
+
+
+def vmem(count):
+    return [pl.BlockSpec(memory_space=pltpu.VMEM)] * count
+
+
+def anywhere(count):
+    return [pl.BlockSpec(memory_space=pl.ANY)] * count
 
 
 def smem():
     return pl.BlockSpec(memory_space=pltpu.SMEM)
 
 
-def params():
-    return pltpu.CompilerParams(vmem_limit_bytes=VMEM_LIMIT)
+def params(limit=VMEM_LIMIT):
+    return pltpu.CompilerParams(vmem_limit_bytes=limit)
+
+
+def cost(us):
+    return pl.CostEstimate(flops=int(us * 1.1e9), bytes_accessed=0, transcendentals=0)
 
 
 def piece_of(listing_ref, group, groups):
@@ -40,19 +48,37 @@
 
 
 def route_kernel(groups, listing_ref, series_ref, mask_ref, token_ref, *rest):
-    out_refs, column_ref = rest[:-1], rest[-1]
-    rows, width = series_ref.shape
-    piece = rows // groups
-    for part in range(rows // 128):
-        line = mask_ref[part : part + 1, :].astype(jnp.float32)
-        column_ref[part * 128 : (part + 1) * 128, :] = jnp.broadcast_to(line, (128, 128)).T
+    out_refs, (held_ref, lines_ref, word_ref, column_ref, sems) = rest[:groups], rest[groups:]
+    piece, width = out_refs[0].shape
     own = lax.axis_index("group")
-    token = token_ref[...].astype(jnp.float32)
+    copies = [
+        pltpu.make_async_copy(mask_ref, lines_ref, sems.at[groups]),
+        pltpu.make_async_copy(token_ref, word_ref, sems.at[groups + 1]),
+    ]
+    firsts = []
     for r in range(groups):
         place = piece_of(listing_ref, lax.bitwise_xor(own, jnp.int32(r)), groups)
         first = pl.multiple_of(place * piece, piece)
-        hidden = column_ref[pl.ds(first, piece), :] > 0.5
-        arrived = series_ref[pl.ds(first, piece), :].astype(jnp.float32)
+        firsts.append(first)
+        copies.append(
+            pltpu.make_async_copy(
+                series_ref.at[pl.ds(first, piece), :],
+                held_ref.at[r * piece : (r + 1) * piece, :],
+                sems.at[r],
+            )
+        )
+    for copy in copies:
+        copy.start()
+    copies[0].wait()
+    for part in range(lines_ref.shape[0]):
+        line = lines_ref[part : part + 1, :].astype(jnp.float32)
+        column_ref[part * 128 : (part + 1) * 128, :] = jnp.broadcast_to(line, (128, 128)).T
+    copies[1].wait()
+    token = word_ref[...].astype(jnp.float32).reshape(1, width)
+    for r in range(groups):
+        copies[2 + r].wait()
+        hidden = column_ref[pl.ds(firsts[r], piece), :] > 0.5
+        arrived = held_ref[r * piece : (r + 1) * piece, :].astype(jnp.float32)
         for lane in range(0, width, 128):
             out_refs[r][:, lane : lane + 128] = jnp.where(
                 hidden, token[:, lane : lane + 128], arrived[:, lane : lane + 128]
@@ -65,27 +91,66 @@
     return pl.pallas_call(
         functools.partial(route_kernel, groups),
         out_shape=[jax.ShapeDtypeStruct((piece, width), jnp.bfloat16)] * groups,
-        in_specs=[smem(), whole((rows, width)), whole((rows // 128, 128)), whole((1, width))],
-        out_specs=[whole((piece, width))] * groups,
-        grid=(1,),
-        scratch_shapes=[pltpu.VMEM((rows, 128), jnp.float32)],
-        compiler_params=params(),
+        in_specs=[smem()] + anywhere(3),
+        out_specs=vmem(groups),
+        scratch_shapes=[
+            pltpu.VMEM((rows, width), jnp.bfloat16),
+            pltpu.VMEM((rows // 128, 128), jnp.int32),
+            pltpu.VMEM((width,), jnp.bfloat16),
+            pltpu.VMEM((rows, 128), jnp.float32),
+            pltpu.SemaphoreType.DMA((groups + 2,)),
+        ],
+        compiler_params=params(LARGE),
+        cost_estimate=cost(1.5),
         name="route",
-    )(packing_list, series, recon_mask.reshape(rows // 128, 128), mask_token.reshape(1, width))
+    )(packing_list, series, recon_mask.reshape(rows // 128, 128), mask_token)
+
+
+def stage_kernel(count, turned, *refs):
+    from_refs, to_refs = refs[:count], refs[count + 1 : 2 * count + 1]
+    scratch, sems = refs[2 * count + 1 : -1], refs[-1]
+    copies = []
+    for i in range(count):
+        target = scratch[0] if i == turned else to_refs[i]
+        copies.append(pltpu.make_async_copy(from_refs[i], target, sems.at[i]))
+    for copy in copies:
+        copy.start()
+    for copy in copies:
+        copy.wait()
+    if turned is not None:
+        width = to_refs[turned].shape[0]
+        for lane in range(0, width, 256):
+            to_refs[turned][lane : lane + 256, :] = (
+                scratch[0][:, lane : lane + 256].astype(jnp.float32).T.astype(jnp.bfloat16)
+            )
+
+
+def stage(weights, turned, behind, us):
+    count = len(weights)
+    scratch = [pltpu.VMEM(weights[turned].shape, jnp.bfloat16)] if turned is not None else []
+    return pl.pallas_call(
+        functools.partial(stage_kernel, count, turned),
+        out_shape=[jax.ShapeDtypeStruct(member.shape, member.dtype) for member in weights],
+        in_specs=anywhere(count + 1),
+        out_specs=vmem(count),
+        scratch_shapes=scratch + [pltpu.SemaphoreType.DMA((count,))],
+        compiler_params=params(),
+        cost_estimate=cost(us),
+        name="stage",
+    )(*weights, behind)
 
 
 def norm_kernel(count, with_borders, *refs):
     piece_refs, gain_ref = refs[:count], refs[count]
     out_ref = refs[-1]
-    piece = piece_refs[0].shape[0]
-    gain = gain_ref[...].astype(jnp.float32)
+    piece, width = piece_refs[0].shape
+    gain = gain_ref[...].astype(jnp.float32).reshape(1, width)
     for i, ref in enumerate(piece_refs):
         widened = ref[...].astype(jnp.float32)
         factor = lax.rsqrt(jnp.mean(widened * widened, axis=-1, keepdims=True) + 1e-06)
         out_ref[i * piece : (i + 1) * piece, :] = (widened * factor * gain).astype(jnp.bfloat16)
     if with_borders:
         docs = refs[count + 1][...]
-        width = out_ref.shape[1]
         row = lax.broadcasted_iota(jnp.int32, (8, width), 0)
         lines = jnp.zeros((8, width), jnp.float32)
         for d in (1, 2, 3):
@@ -94,22 +159,20 @@
         out_ref[count * piece :, :] = lines.astype(jnp.bfloat16)
 
 
-def norm(pieces, gain, docs=None):
+def norm(pieces, gain, docs=None, behind=()):
     piece, width = pieces[0].shape
     count = len(pieces)
     rows = count * piece + (8 if docs is not None else 0)
-    operands = list(pieces) + [gain.reshape(1, width)]
-    if docs is not None:
-        operands.append(docs)
+    operands = list(pieces) + [gain] + ([docs] if docs is not None else [])
     return pl.pallas_call(
         functools.partial(norm_kernel, count, docs is not None),
         out_shape=jax.ShapeDtypeStruct((rows, width), jnp.bfloat16),
-        in_specs=[whole(member.shape) for member in operands],
-        out_specs=whole((rows, width)),
-        grid=(1,),
-        compiler_params=params(),
+        in_specs=vmem(len(operands)) + anywhere(len(behind)),
+        out_specs=vmem(1)[0],
+        compiler_params=params(),
+        cost_estimate=cost(0.3),
         name="norm",
-    )(*operands)
+    )(*operands, *behind)
 
 
 def borders_of(ref, first):
@@ -160,6 +223,15 @@
 def project(x, weight_ref, j):
     columns = weight_ref[:, j * STEP_COLS : (j + 1) * STEP_COLS]
     return jnp.dot(x, columns, preferred_element_type=jnp.float32)
+
+
+def project_turned(x, weight_ref, j):
+    return lax.dot_general(
+        weight_ref[j * STEP_COLS : (j + 1) * STEP_COLS, :],
+        x,
+        (((1,), (1,)), ((), ())),
+        preferred_element_type=jnp.float32,
+    ).astype(jnp.bfloat16)
 
 
 def own_kernel(piece, parts, borders_at, *refs):
@@ -176,7 +248,7 @@
         queries = project(x, wq_ref, j).astype(jnp.bfloat16).astype(jnp.float32)
         queries = (queries * (1.0 / math.sqrt(HD))).T.astype(jnp.bfloat16)
         keys = project(x, wk_ref, j).astype(jnp.bfloat16)
-        values = project(x, wv_ref, j).T.astype(jnp.bfloat16)
+        values = project_turned(x, wv_ref, j)
 
         def stacked(h, rest):
             own = queries[h * HD : (h + 1) * HD]
@@ -214,10 +286,11 @@
         ],
         axis=0,
     )
+    largest, excess = [], []
     for j in range(HEADS // STEP_HEADS):
         heads = [j * STEP_HEADS + h for h in range(STEP_HEADS)]
         keys = project(x, wk_ref, j).astype(jnp.bfloat16)
-        values = project(x, wv_ref, j).T.astype(jnp.bfloat16)
+        values = project_turned(x, wv_ref, j)
         scores = scores_of(keys, extras, [queries_ref[head] for head in heads])
         weights = [jnp.exp2(member * LOG2E).astype(jnp.bfloat16) for member in scores]
         sums = [
@@ -225,27 +298,32 @@
             + jnp.dot(with_ones(values, h), weights[h], preferred_element_type=jnp.float32)[: HD + 8]
             for h, head in enumerate(heads)
         ]
-        largest = functools.reduce(jnp.maximum, [member[HD : HD + 8] for member in sums])
-        excess = functools.reduce(jnp.maximum, [state_ref[head, HD + 8 :, :] for head in heads])
-        usual = jnp.logical_and(jnp.max(largest) < LARGEST, jnp.max(excess) <= 0.0)
-
-        @pl.when(usual)
-        def plain():
-            finish(j, sums, None)
-
-        @pl.when(jnp.logical_not(usual))
-        def again():
+        for h, head in enumerate(heads):
+            finish(head, sums[h], None)
+            largest.append(sums[h][HD : HD + 8])
+            excess.append(state_ref[head, HD + 8 :, :])
+    largest = functools.reduce(jnp.maximum, largest)
+    excess = functools.reduce(jnp.maximum, excess)
+    usual = jnp.logical_and(largest < LARGEST, excess <= 0.0)
+
+    @pl.when(jnp.min(jnp.where(usual, 1.0, 0.0)) < 0.5)
+    def again():
+        for j in range(HEADS // STEP_HEADS):
+            heads = [j * STEP_HEADS + h for h in range(STEP_HEADS)]
+            keys = project(x, wk_ref, j).astype(jnp.bfloat16)
+            values = project_turned(x, wv_ref, j)
             scores = scores_of(keys, extras, [queries_ref[head] for head in heads])
-            tops, sums = [], []
             for h, head in enumerate(heads):
                 before = state_ref[head, HD + 8 : HD + 9, :]
                 top = jnp.maximum(before, jnp.max(scores[h], axis=0, keepdims=True))
                 weights = jnp.exp2((scores[h] - top) * LOG2E).astype(jnp.bfloat16)
                 added = jnp.dot(with_ones(values, h), weights, preferred_element_type=jnp.float32)
                 factor = jnp.exp2((before - top) * LOG2E)
-                sums.append(state_ref[head, : HD + 8, :] * factor + added[: HD + 8])
-                tops.append(jnp.broadcast_to(top, (8, top.shape[1])))
-            finish(j, sums, tops)
+                finish(
+                    head,
+                    state_ref[head, : HD + 8, :] * factor + added[: HD + 8],
+                    jnp.broadcast_to(top, (8, top.shape[1])),
+                )
 
 
 def named_sources(row_refs, layout):
@@ -258,14 +336,9 @@
 def chunk_kernel(piece, layout, queries_ref, wk_ref, wv_ref, old_ref, *rest):
     row_refs, state_ref = rest[:-1], rest[-1]
 
-    def finish(j, sums, tops):
-        for h in range(STEP_HEADS):
-            head = j * STEP_HEADS + h
-            state_ref[head, : HD + 8, :] = sums[h]
-            if tops is None:
-                state_ref[head, HD + 8 :, :] = jnp.zeros((8, sums[h].shape[1]), jnp.float32)
-            else:
-                state_ref[head, HD + 8 :, :] = tops[h]
+    def finish(head, sums, top):
+        state_ref[head, : HD + 8, :] = sums
+        state_ref[head, HD + 8 :, :] = jnp.zeros((8, sums.shape[1]), jnp.float32) if top is None else top
 
     fold(piece, named_sources(row_refs, layout), queries_ref, wk_ref, wv_ref, old_ref, finish)
 
@@ -275,10 +348,8 @@
     piece_refs, out_refs = rest[-2 * groups - 1 : -groups - 1], rest[-groups - 1 : -1]
     attended_ref = rest[-1]
 
-    def finish(j, sums, tops):
-        for h in range(STEP_HEADS):
-            first = (j * STEP_HEADS + h) * HD
-            attended_ref[first : first + HD, :] = sums[h][:HD] / sums[h][HD : HD + 1]
+    def finish(head, sums, top):
+        attended_ref[head * HD : (head + 1) * HD, :] = sums[:HD] / sums[HD : HD + 1]
 
     fold(piece, named_sources(row_refs, layout), queries_ref, wk_ref, wv_ref, old_ref, finish)
     attended = attended_ref[...].T.astype(jnp.bfloat16)
@@ -289,14 +360,6 @@
         ).astype(jnp.bfloat16)
 
 
-def vmem(count):
-    return [pl.BlockSpec(memory_space=pltpu.VMEM)] * count
-
-
-def cost(us):
-    return pl.CostEstimate(flops=int(us * 1.1e9), bytes_accessed=0, transcendentals=0)
-
-
 def own_call(members, layout, w_query, w_key, w_value, piece, rows):
     parts, borders_at = layout
     return pl.pallas_call(
@@ -354,10 +417,10 @@
     return pl.pallas_call(
         functools.partial(arrange_kernel, groups),
         out_shape=jax.ShapeDtypeStruct((groups * piece, width), jnp.bfloat16),
-        in_specs=[smem()] + [whole((piece, width))] * groups,
-        out_specs=whole((groups * piece, width)),
-        grid=(1,),
-        compiler_params=params(),
+        in_specs=[smem()] + vmem(groups),
+        out_specs=vmem(1)[0],
+        compiler_params=params(),
+        cost_estimate=cost(1.3),
         name="arrange",
     )(packing_list, *pieces)
 
@@ -380,38 +443,27 @@
     onward = [(ring[i], ring[(i + 1) % shards]) for i in range(shards)]
     backward = [(there, here) for here, there in onward]
 
-    pieces = exchange(route(packing_list, series, recon_mask, mask_token, groups))
     half = rows // 2
-    if HALVES:
-        own = (
-            norm(pieces[: groups // 2], norm_gain, doc_ids),
-            norm(pieces[groups // 2 :], norm_gain),
-        )
-        parts = [(0, 0, half), (1, 0, half)]
-        own_layout = (parts, (0, half))
-        pair_layout = (own_layout, ([(2, 0, half), (3, 0, half)], (2, half)))
-        far_layout = (own_layout,)
-    else:
-        own = (norm(pieces, norm_gain, doc_ids),)
-        own_layout = ([(0, 0, rows)], (0, rows))
-        pair_layout = (own_layout, ([(1, 0, rows)], (1, rows)))
-        far_layout = (([(0, 0, half), (1, 0, half)], (1, half)),)
+    sent = route(packing_list, series, recon_mask, mask_token, groups)
+    w_query, w_key = stage((w_query, w_key), None, sent[0], 2.0)
+    pieces = exchange(sent)
+    a = norm(pieces[: groups // 2], norm_gain, doc_ids, (w_query,))
+    w_value, w_out = stage((w_value, w_out), 0, a, 2.0)
+    b = norm(pieces[groups // 2 :], norm_gain, None, (a, w_value))
+    own = (a, b)
+    own_layout = ([(0, 0, half), (1, 0, half)], (0, half))
+    pair_layout = (own_layout, ([(2, 0, half), (3, 0, half)], (2, half)))
+    far_layout = (own_layout,)
     queries, state = own_call(own, own_layout, w_query, w_key, w_value, piece, rows)
     before, after = own, own
     for step in range(1, shards // 2):
         before = tuple(lax.ppermute(member, "ctx", onward) for member in before)
         after = tuple(lax.ppermute(member, "ctx", backward) for member in after)
         state = chunk_call(queries, w_key, w_value, state, before + after, pair_layout, piece)
-    if HALVES:
-        far = (
-            lax.ppermute(before[0], "ctx", onward),
-            lax.ppermute(after[1], "ctx", backward),
-        )
-    else:
-        far = (
-            lax.ppermute(before[0][:half], "ctx", onward),
-            lax.ppermute(after[0][half:], "ctx", backward),
-        )
+    far = (
+        lax.ppermute(before[0], "ctx", onward),
+        lax.ppermute(after[1], "ctx", backward),
+    )
     done = last_call(queries, w_key, w_value, state, w_out, far, far_layout, pieces, piece)
     return arrange(packing_list, exchange(done))
 

time: 62.2 us -> 57.1 us (0.918)
  local copies, waits for them, and re-layouts: 8.21 us -> 2.12 us
  Pallas kernels: 19.1 us -> 20 us
    ppermute x6, waiting for transfers between devices: 0.11 us -> 4.92 us  [on_device(): after = tuple((lax.ppermute(member, 'ctx', backward) for member in after))]
    unnamed x22 -> x18, local copies, waits for them, and re-layouts: 6.84 us -> 2.12 us
    ppermute x6, starting transfers between devices: 6.42 us -> 10.3 us  [on_device(): before = tuple((lax.ppermute(member, 'ctx', onward) for member in before))]
    ppermute x6, starting transfers between devices: 6.09 us -> 2.32 us  [on_device(): after = tuple((lax.ppermute(member, 'ctx', backward) for member in after))]
    ppermute x6, waiting for transfers between devices: 9.02 us -> 6.74 us  [exchange(): lax.ppermute(pieces[r], 'group', [(i, i ^ r) for i in range(groups)])]
    pallas_call x1, Pallas kernels: 0.71 us -> 2.64 us  [route(): pl.pallas_call(functools.partial(route_kernel, groups), out_shape=[jax.Sh...]
    pallas_call x3, Pallas kernels: 10.8 us -> 9.13 us  [chunk_call(): pl.pallas_call(functools.partial(chunk_kernel, piece, layout), out_shape=...]
    ppermute x1, waiting for transfers between devices: 1.67 us -> 0.07 us  [on_device(): lax.ppermute(before[0], 'ctx', onward)]
  transfers between devices with their start and end apart: 20 -> 20, of which waited for: 7 -> 12; matrix products, arithmetic and copies ran while one was open for 1% -> 0% of each run, Pallas kernels for 22% -> 23%
where the time goes in v3:
time: 57.1 us; the launch traced here: 56.8 us
  starting transfers between devices  20.3 us (36%)
  Pallas kernels  20 us (35%)
  waiting for transfers between devices  14.2 us (25%)
  local copies, waits for them, and re-layouts  2.12 us (4%)
    ppermute x6, starting transfers between devices, on_device(): before = tuple((lax.ppermute(member, 'ctx', onward) for member in before))  10.3 us
    pallas_call x3, Pallas kernels, chunk_call(): pl.pallas_call(functools.partial(chunk_kernel, piece, layout), out_shape=...  9.13 us
    ppermute x6, waiting for transfers between devices, exchange(): lax.ppermute(pieces[r], 'group', [(i, i ^ r) for i in range(groups)])  6.74 us
    ppermute x6, starting transfers between devices, exchange(): lax.ppermute(pieces[r], 'group', [(i, i ^ r) for i in range(groups)])  5.08 us
    ppermute x6, waiting for transfers between devices, on_device(): after = tuple((lax.ppermute(member, 'ctx', backward) for member in after))  4.92 us
    pallas_call x1, Pallas kernels, own_call(): pl.pallas_call(functools.partial(own_kernel, piece, parts, borders_at), o...  2.71 us
    pallas_call x1, Pallas kernels, route(): pl.pallas_call(functools.partial(route_kernel, groups), out_shape=[jax.Sh...  2.64 us
    pallas_call x1, Pallas kernels, last_call(): pl.pallas_call(functools.partial(last_kernel, groups, piece, layout), out...  2.57 us
  transfers between devices with their start and end apart: 20, of which 12 were waited for; matrix products, arithmetic and copies ran while one was open for 0% of the time, Pallas kernels for 23%

profile of v3, /device:TPU:0, one launch (start us, length us, event | category | flops | bytes accessed | tf_op | source)
XLA Modules:
  0.0 56.8 jit_solution(17460895757751551881)
XLA Ops:
  0.0 2.6 %route.1 = (bf16[64,768]{1,0:T(8,128)(2,1)}, bf16[64,768]{1,0:T(8,128)(2,1)}, bf16[64,768]{1,0:T(8,128)(2,1)}, bf16[64,768]{1,0:T(8,128)(2,1)}) custom-call(s32[4]{0:T(128)} %listing_ref.3, bf16[256,768]{1,0:T(8,128)(2,1)} %series_ref.1, s32[2,128]{1,0:T(2,128)} %bitcast.1, bf16[768]{0:T(1024)(128)(2,1)} %token_ref.1), custom_call_target="tpu_custom_call" | custom-call | flops 1650000000 | tf_op jit(solution)/shard_map/route/pallas_call | solution.py:91
  3.2 2.6 %collective-permute-start.1 = (bf16[64,768]{1,0:T(8,128)(2,1)}, bf16[64,768]{1,0:T(8,128)(2,1)S(1)}, u32[]{:S(2)}, u32[]{:S(2)}) collective-permute-start(bf16[64,768]{1,0:T(8,128)(2,1)} %get-tuple-element.22), channel_id=1, source_target_pairs={{0,16},{8,24},{16,0},{24,8},{1,17},{9,25},{17,1},{25,9},{2,18},{10... | collective-permute-start | bytes 294920 | tf_op jit(solution)/shard_map/ppermute | solution.py:431
  5.8 0.9 %copy-done = bf16[64,768]{1,0:T(8,128)(2,1)S(1)} copy-done((bf16[64,768]{1,0:T(8,128)(2,1)S(1)}, bf16[64,768]{1,0:T(8,128)(2,1)}, u32[]{:S(2)}) %copy-start) | copy-done | bytes 98328
  8.6 0.9 %stage.3 = (bf16[768,768]{1,0:T(8,128)(2,1)S(1)}, bf16[768,768]{1,0:T(8,128)(2,1)S(1)}) custom-call(bf16[768,768]{1,0:T(8,128)(2,1)S(1)} %copy-done.6, bf16[768,768]{1,0:T(8,128)(2,1)S(1)} %copy-done.7, bf16[136,768]{1,0:T(8,128)(2,1)S(1)} %norm.2.refs_2_.refs_3_.refs_0_), custom_call_target="tpu_custom_call" | custom-call | flops 2200000000 | tf_op jit(solution)/shard_map/stage/pallas_call | solution.py:131
  9.6 1.6 %collective-permute-done.2.refs_1_.rest_5_ = bf16[64,768]{1,0:T(8,128)(2,1)S(1)} collective-permute-done((bf16[64,768]{1,0:T(8,128)(2,1)}, bf16[64,768]{1,0:T(8,128)(2,1)S(1)}, u32[]{:S(2)}, u32[]{:S(2)}) %collective-permute-start.2) | collective-permute-done | bytes 98336 | tf_op jit(solution)/shard_map/ppermute | solution.py:431
  11.3 1.7 %collective-permute-start.4 = (bf16[128,768]{1,0:T(8,128)(2,1)S(1)}, bf16[128,768]{1,0:T(8,128)(2,1)S(1)}, u32[]{:S(2)}, u32[]{:S(2)}) collective-permute-start(bf16[128,768]{1,0:T(8,128)(2,1)S(1)} %norm.3.refs_1_), channel_id=1, source_target_pairs={{0,2},{2,4},{4,6},{6,7},{7,5},{5,3},{3,1},{1,0},{8,10},{10,12},{12... | collective-permute-start | bytes 589832 | tf_op jit(solution)/shard_map/ppermute | solution.py:460
  13.4 1.7 %collective-permute-start.3 = (bf16[136,768]{1,0:T(8,128)(2,1)S(1)}, bf16[136,768]{1,0:T(8,128)(2,1)S(1)}, u32[]{:S(2)}, u32[]{:S(2)}) collective-permute-start(bf16[136,768]{1,0:T(8,128)(2,1)S(1)} %norm.2.refs_2_.refs_3_.refs_0_), channel_id=1, source_target_pairs={{0,2},{2,4},{4,6},{6,7},{7,5},{5,3},{3,1},{1,0},{8,10},{10,12},{12... | collective-permute-start | bytes 626696 | tf_op jit(solution)/shard_map/ppermute | solution.py:460
  15.4 2.7 %own_rows.1 = (bf16[12,128,256]{2,1,0:T(8,128)(2,1)S(1)}, f32[12,80,256]{2,1,0:T(8,128)S(1)}) custom-call(bf16[136,768]{1,0:T(8,128)(2,1)S(1)} %norm.2.refs_2_.refs_3_.refs_0_, bf16[128,768]{1,0:T(8,128)(2,1)S(1)} %norm.3.refs_1_, bf16[768,768]{1,0:T(8,128)(2,1)S(1)} %get-tuple-element.21.refs_4_.refs_2_, ...), custom_call_target="tpu_custom_call" | custom-call | flops 3300000000 | tf_op jit(solution)/shard_map/own_rows/pallas_call | solution.py:365
  18.1 2.6 %collective-permute-done.6.rest_3_ = bf16[128,768]{1,0:T(8,128)(2,1)S(1)} collective-permute-done((bf16[128,768]{1,0:T(8,128)(2,1)S(1)}, bf16[128,768]{1,0:T(8,128)(2,1)S(1)}, u32[]{:S(2)}, u32[]{:S(2)}) %collective-permute-start.6) | collective-permute-done | bytes 196640 | tf_op jit(solution)/shard_map/ppermute | solution.py:461
  21.2 1.6 %collective-permute-start.8 = (bf16[128,768]{1,0:T(8,128)(2,1)S(1)}, bf16[128,768]{1,0:T(8,128)(2,1)S(1)}, u32[]{:S(2)}, u32[]{:S(2)}) collective-permute-start(bf16[128,768]{1,0:T(8,128)(2,1)S(1)} %collective-permute-done.4.rest_1_), channel_id=1, source_target_pairs={{0,2},{2,4},{4,6},{6,7},{7,5},{5,3},{3,1},{1,0},{8,10},{10,12},{12... | collective-permute-start | bytes 589832 | tf_op jit(solution)/shard_map/ppermute | solution.py:460
  23.6 1.6 %collective-permute-start.7 = (bf16[136,768]{1,0:T(8,128)(2,1)S(1)}, bf16[136,768]{1,0:T(8,128)(2,1)S(1)}, u32[]{:S(2)}, u32[]{:S(2)}) collective-permute-start(bf16[136,768]{1,0:T(8,128)(2,1)S(1)} %collective-permute-done.3.rest_0_), channel_id=1, source_target_pairs={{0,2},{2,4},{4,6},{6,7},{7,5},{5,3},{3,1},{1,0},{8,10},{10,12},{12... | collective-permute-start | bytes 626696 | tf_op jit(solution)/shard_map/ppermute | solution.py:460
  25.7 3.0 %received_rows.3.old_ref = f32[12,80,256]{2,1,0:T(8,128)S(1)} custom-call(bf16[12,128,256]{2,1,0:T(8,128)(2,1)S(1)} %get-tuple-element.26.queries_ref, bf16[768,768]{1,0:T(8,128)(2,1)S(1)} %get-tuple-element.25.refs_3_.wk_ref, bf16[768,768]{1,0:T(8,128)(2,1)S(1)} %get-tuple-element.24.refs_4_.wv_ref, f32[12,80,256]{2,1,0:T(8,128)S(1)} %get-tuple-element.27.old_ref, ...), custom_call_target="tpu_custom_call" | custom-call | flops 3849999872 | tf_op jit(solution)/shard_map/received_rows/pallas_call | solution.py:380
  30.3 1.2 %collective-permute-start.12 = (bf16[128,768]{1,0:T(8,128)(2,1)S(1)}, bf16[128,768]{1,0:T(8,128)(2,1)S(1)}, u32[]{:S(2)}, u32[]{:S(2)}) collective-permute-start(bf16[128,768]{1,0:T(8,128)(2,1)S(1)} %collective-permute-done.8.rest_1_), channel_id=1, source_target_pairs={{0,2},{2,4},{4,6},{6,7},{7,5},{5,3},{3,1},{1,0},{8,10},{10,12},{12... | collective-permute-start | bytes 589832 | tf_op jit(solution)/shard_map/ppermute | solution.py:460
  32.1 2.4 %collective-permute-start.11 = (bf16[136,768]{1,0:T(8,128)(2,1)S(1)}, bf16[136,768]{1,0:T(8,128)(2,1)S(1)}, u32[]{:S(2)}, u32[]{:S(2)}) collective-permute-start(bf16[136,768]{1,0:T(8,128)(2,1)S(1)} %collective-permute-done.7.rest_0_), channel_id=1, source_target_pairs={{0,2},{2,4},{4,6},{6,7},{7,5},{5,3},{3,1},{1,0},{8,10},{10,12},{12... | collective-permute-start | bytes 626696 | tf_op jit(solution)/shard_map/ppermute | solution.py:460
  34.5 3.0 %received_rows.4.old_ref = f32[12,80,256]{2,1,0:T(8,128)S(1)} custom-call(bf16[12,128,256]{2,1,0:T(8,128)(2,1)S(1)} %get-tuple-element.26.queries_ref, bf16[768,768]{1,0:T(8,128)(2,1)S(1)} %get-tuple-element.25.refs_3_.wk_ref, bf16[768,768]{1,0:T(8,128)(2,1)S(1)} %get-tuple-element.24.refs_4_.wv_ref, f32[12,80,256]{2,1,0:T(8,128)S(1)} %received_rows.3.old_ref, ...), custom_call_target="tpu_custom_call" | custom-call | flops 3849999872 | tf_op jit(solution)/shard_map/received_rows/pallas_call | solution.py:380
  38.2 0.9 %collective-permute-start.16 = (bf16[128,768]{1,0:T(8,128)(2,1)S(1)}, bf16[128,768]{1,0:T(8,128)(2,1)S(1)}, u32[]{:S(2)}, u32[]{:S(2)}) collective-permute-start(bf16[128,768]{1,0:T(8,128)(2,1)S(1)} %collective-permute-done.14.rest_3_), channel_id=1, source_target_pairs={{2,0},{4,2},{6,4},{7,6},{5,7},{3,5},{1,3},{0,1},{10,8},{12,10},{14... | collective-permute-start | bytes 589832 | tf_op jit(solution)/shard_map/ppermute | solution.py:465
  39.1 1.1 %collective-permute-done.11.rest_0_ = bf16[136,768]{1,0:T(8,128)(2,1)S(1)} collective-permute-done((bf16[136,768]{1,0:T(8,128)(2,1)S(1)}, bf16[136,768]{1,0:T(8,128)(2,1)S(1)}, u32[]{:S(2)}, u32[]{:S(2)}) %collective-permute-start.11) | collective-permute-done | bytes 208928 | tf_op jit(solution)/shard_map/ppermute | solution.py:460
  40.2 1.8 %collective-permute-start.15 = (bf16[136,768]{1,0:T(8,128)(2,1)S(1)}, bf16[136,768]{1,0:T(8,128)(2,1)S(1)}, u32[]{:S(2)}, u32[]{:S(2)}) collective-permute-start(bf16[136,768]{1,0:T(8,128)(2,1)S(1)} %collective-permute-done.11.rest_0_), channel_id=1, source_target_pairs={{0,2},{2,4},{4,6},{6,7},{7,5},{5,3},{3,1},{1,0},{8,10},{10,12},{12... | collective-permute-start | bytes 626696 | tf_op jit(solution)/shard_map/ppermute | solution.py:464
  42.6 3.2 %received_rows.5.old_ref = f32[12,80,256]{2,1,0:T(8,128)S(1)} custom-call(bf16[12,128,256]{2,1,0:T(8,128)(2,1)S(1)} %get-tuple-element.26.queries_ref, bf16[768,768]{1,0:T(8,128)(2,1)S(1)} %get-tuple-element.25.refs_3_.wk_ref, bf16[768,768]{1,0:T(8,128)(2,1)S(1)} %get-tuple-element.24.refs_4_.wv_ref, f32[12,80,256]{2,1,0:T(8,128)S(1)} %received_rows.4.old_ref, ...), custom_call_target="tpu_custom_call" | custom-call | flops 3849999872 | tf_op jit(solution)/shard_map/received_rows/pallas_call | solution.py:380
  46.0 2.6 %last_rows.1 = (bf16[64,768]{1,0:T(8,128)(2,1)S(1)}, bf16[64,768]{1,0:T(8,128)(2,1)S(1)}, bf16[64,768]{1,0:T(8,128)(2,1)S(1)}, bf16[64,768]{1,0:T(8,128)(2,1)S(1)}) custom-call(bf16[12,128,256]{2,1,0:T(8,128)(2,1)S(1)} %get-tuple-element.26.queries_ref, bf16[768,768]{1,0:T(8,128)(2,1)S(1)} %get-tuple-element.25.refs_3_.wk_ref, ...), custom_call_target="tpu_custom_call" | custom-call | flops 3300000000 | tf_op jit(solution)/shard_map/last_rows/pallas_call | solution.py:394
  48.6 1.8 %collective-permute-start.18 = (bf16[64,768]{1,0:T(8,128)(2,1)S(1)}, bf16[64,768]{1,0:T(8,128)(2,1)S(1)}, u32[]{:S(2)}, u32[]{:S(2)}) collective-permute-start(bf16[64,768]{1,0:T(8,128)(2,1)S(1)} %get-tuple-element.31), channel_id=1, source_target_pairs={{0,16},{8,24},{16,0},{24,8},{1,17},{9,25},{17,1},{25,9},{2,18},{10... | collective-permute-start | bytes 294920 | tf_op jit(solution)/shard_map/ppermute | solution.py:431
  50.5 3.8 %collective-permute-done.18.refs_2_ = bf16[64,768]{1,0:T(8,128)(2,1)S(1)} collective-permute-done((bf16[64,768]{1,0:T(8,128)(2,1)S(1)}, bf16[64,768]{1,0:T(8,128)(2,1)S(1)}, u32[]{:S(2)}, u32[]{:S(2)}) %collective-permute-start.18) | collective-permute-done | bytes 98336 | tf_op jit(solution)/shard_map/ppermute | solution.py:431
  54.3 1.2 %collective-permute-done.19.refs_3_ = bf16[64,768]{1,0:T(8,128)(2,1)S(1)} collective-permute-done((bf16[64,768]{1,0:T(8,128)(2,1)S(1)}, bf16[64,768]{1,0:T(8,128)(2,1)S(1)}, u32[]{:S(2)}, u32[]{:S(2)}) %collective-permute-start.19) | collective-permute-done | bytes 98336 | tf_op jit(solution)/shard_map/ppermute | solution.py:431
  55.5 1.3 %arrange.1 = bf16[256,768]{1,0:T(8,128)(2,1)} custom-call(s32[4]{0:T(128)S(1)} %copy-done.8, bf16[64,768]{1,0:T(8,128)(2,1)S(1)} %get-tuple-element.29.refs_0_, bf16[64,768]{1,0:T(8,128)(2,1)S(1)} %collective-permute-done.17.refs_1_, bf16[64,768]{1,0:T(8,128)(2,1)S(1)} %collective-permute-done.18.refs_2_, bf16[64,768]{1,0:T(8,128)(2,1)S(1)} %collective-permute-done.19.refs_3_), custom_call_target="tpu_custom_call" | custom-call | flops 1430000000 | tf_op jit(solution)/shard_map/arrange/pallas_call | solution.py:417
  (45 shorter events, 8.9 us)
Async XLA Ops:
  0.0 5.8 %copy-start.4 = (bf16[768,768]{1,0:T(8,128)(2,1)S(1)}, bf16[768,768]{1,0:T(8,128)(2,1)}, u32[]{:S(2)}) copy-start(bf16[768,768]{1,0:T(8,128)(2,1)} %refs_0_.2) | copy-start | bytes 3538948
  0.0 5.8 %copy-start.5 = (bf16[768,768]{1,0:T(8,128)(2,1)S(1)}, bf16[768,768]{1,0:T(8,128)(2,1)}, u32[]{:S(2)}) copy-start(bf16[768,768]{1,0:T(8,128)(2,1)} %refs_1_.2) | copy-start | bytes 3538948
  2.7 4.6 %collective-permute-start = (bf16[64,768]{1,0:T(8,128)(2,1)}, bf16[64,768]{1,0:T(8,128)(2,1)S(1)}, u32[]{:S(2)}, u32[]{:S(2)}) collective-permute-start(bf16[64,768]{1,0:T(8,128)(2,1)} %get-tuple-element.20), channel_id=1, source_target_pairs={{0,8},{8,0},{16,24},{24,16},{1,9},{9,1},{17,25},{25,17},{2,10},{10... | collective-permute-start | bytes 294920 | tf_op jit(solution)/shard_map/ppermute | solution.py:431
  3.2 6.4 %collective-permute-start.1 = (bf16[64,768]{1,0:T(8,128)(2,1)}, bf16[64,768]{1,0:T(8,128)(2,1)S(1)}, u32[]{:S(2)}, u32[]{:S(2)}) collective-permute-start(bf16[64,768]{1,0:T(8,128)(2,1)} %get-tuple-element.22), channel_id=1, source_target_pairs={{0,16},{8,24},{16,0},{24,8},{1,17},{9,25},{17,1},{25,9},{2,18},{10... | collective-permute-start | bytes 294920 | tf_op jit(solution)/shard_map/ppermute | solution.py:431
  5.7 5.4 %collective-permute-start.2 = (bf16[64,768]{1,0:T(8,128)(2,1)}, bf16[64,768]{1,0:T(8,128)(2,1)S(1)}, u32[]{:S(2)}, u32[]{:S(2)}) collective-permute-start(bf16[64,768]{1,0:T(8,128)(2,1)} %get-tuple-element.23), channel_id=1, source_target_pairs={{0,24},{8,16},{16,8},{24,0},{1,25},{9,17},{17,9},{25,1},{2,26},{10... | collective-permute-start | bytes 294920 | tf_op jit(solution)/shard_map/ppermute | solution.py:431
  11.3 9.9 %collective-permute-start.4 = (bf16[128,768]{1,0:T(8,128)(2,1)S(1)}, bf16[128,768]{1,0:T(8,128)(2,1)S(1)}, u32[]{:S(2)}, u32[]{:S(2)}) collective-permute-start(bf16[128,768]{1,0:T(8,128)(2,1)S(1)} %norm.3.refs_1_), channel_id=1, source_target_pairs={{0,2},{2,4},{4,6},{6,7},{7,5},{5,3},{3,1},{1,0},{8,10},{10,12},{12... | collective-permute-start | bytes 589832 | tf_op jit(solution)/shard_map/ppermute | solution.py:460
  13.0 7.8 %collective-permute-start.6 = (bf16[128,768]{1,0:T(8,128)(2,1)S(1)}, bf16[128,768]{1,0:T(8,128)(2,1)S(1)}, u32[]{:S(2)}, u32[]{:S(2)}) collective-permute-start(bf16[128,768]{1,0:T(8,128)(2,1)S(1)} %norm.3.refs_1_), channel_id=1, source_target_pairs={{2,0},{4,2},{6,4},{7,6},{5,7},{3,5},{1,3},{0,1},{10,8},{12,10},{14... | collective-permute-start | bytes 589832 | tf_op jit(solution)/shard_map/ppermute | solution.py:461
  13.4 10.2 %collective-permute-start.3 = (bf16[136,768]{1,0:T(8,128)(2,1)S(1)}, bf16[136,768]{1,0:T(8,128)(2,1)S(1)}, u32[]{:S(2)}, u32[]{:S(2)}) collective-permute-start(bf16[136,768]{1,0:T(8,128)(2,1)S(1)} %norm.2.refs_2_.refs_3_.refs_0_), channel_id=1, source_target_pairs={{0,2},{2,4},{4,6},{6,7},{7,5},{5,3},{3,1},{1,0},{8,10},{10,12},{12... | collective-permute-start | bytes 626696 | tf_op jit(solution)/shard_map/ppermute | solution.py:460
  15.0 10.2 %collective-permute-start.5 = (bf16[136,768]{1,0:T(8,128)(2,1)S(1)}, bf16[136,768]{1,0:T(8,128)(2,1)S(1)}, u32[]{:S(2)}, u32[]{:S(2)}) collective-permute-start(bf16[136,768]{1,0:T(8,128)(2,1)S(1)} %norm.2.refs_2_.refs_3_.refs_0_), channel_id=1, source_target_pairs={{2,0},{4,2},{6,4},{7,6},{5,7},{3,5},{1,3},{0,1},{10,8},{12,10},{14... | collective-permute-start | bytes 626696 | tf_op jit(solution)/shard_map/ppermute | solution.py:461
  20.8 8.7 %collective-permute-start.10 = (bf16[128,768]{1,0:T(8,128)(2,1)S(1)}, bf16[128,768]{1,0:T(8,128)(2,1)S(1)}, u32[]{:S(2)}, u32[]{:S(2)}) collective-permute-start(bf16[128,768]{1,0:T(8,128)(2,1)S(1)} %collective-permute-done.6.rest_3_), channel_id=1, source_target_pairs={{2,0},{4,2},{6,4},{7,6},{5,7},{3,5},{1,3},{0,1},{10,8},{12,10},{14... | collective-permute-start | bytes 589832 | tf_op jit(solution)/shard_map/ppermute | solution.py:461
  21.2 9.1 %collective-permute-start.8 = (bf16[128,768]{1,0:T(8,128)(2,1)S(1)}, bf16[128,768]{1,0:T(8,128)(2,1)S(1)}, u32[]{:S(2)}, u32[]{:S(2)}) collective-permute-start(bf16[128,768]{1,0:T(8,128)(2,1)S(1)} %collective-permute-done.4.rest_1_), channel_id=1, source_target_pairs={{0,2},{2,4},{4,6},{6,7},{7,5},{5,3},{3,1},{1,0},{8,10},{10,12},{12... | collective-permute-start | bytes 589832 | tf_op jit(solution)/shard_map/ppermute | solution.py:460
  23.6 8.5 %collective-permute-start.7 = (bf16[136,768]{1,0:T(8,128)(2,1)S(1)}, bf16[136,768]{1,0:T(8,128)(2,1)S(1)}, u32[]{:S(2)}, u32[]{:S(2)}) collective-permute-start(bf16[136,768]{1,0:T(8,128)(2,1)S(1)} %collective-permute-done.3.rest_0_), channel_id=1, source_target_pairs={{0,2},{2,4},{4,6},{6,7},{7,5},{5,3},{3,1},{1,0},{8,10},{10,12},{12... | collective-permute-start | bytes 626696 | tf_op jit(solution)/shard_map/ppermute | solution.py:460
  25.3 9.2 %collective-permute-start.9 = (bf16[136,768]{1,0:T(8,128)(2,1)S(1)}, bf16[136,768]{1,0:T(8,128)(2,1)S(1)}, u32[]{:S(2)}, u32[]{:S(2)}) collective-permute-start(bf16[136,768]{1,0:T(8,128)(2,1)S(1)} %collective-permute-done.5.rest_2_), channel_id=1, source_target_pairs={{2,0},{4,2},{6,4},{7,6},{5,7},{3,5},{1,3},{0,1},{10,8},{12,10},{14... | collective-permute-start | bytes 626696 | tf_op jit(solution)/shard_map/ppermute | solution.py:461
  29.5 8.7 %collective-permute-start.14 = (bf16[128,768]{1,0:T(8,128)(2,1)S(1)}, bf16[128,768]{1,0:T(8,128)(2,1)S(1)}, u32[]{:S(2)}, u32[]{:S(2)}) collective-permute-start(bf16[128,768]{1,0:T(8,128)(2,1)S(1)} %collective-permute-done.10.rest_3_), channel_id=1, source_target_pairs={{2,0},{4,2},{6,4},{7,6},{5,7},{3,5},{1,3},{0,1},{10,8},{12,10},{14... | collective-permute-start | bytes 589832 | tf_op jit(solution)/shard_map/ppermute | solution.py:461
  30.3 11.7 %collective-permute-start.12 = (bf16[128,768]{1,0:T(8,128)(2,1)S(1)}, bf16[128,768]{1,0:T(8,128)(2,1)S(1)}, u32[]{:S(2)}, u32[]{:S(2)}) collective-permute-start(bf16[128,768]{1,0:T(8,128)(2,1)S(1)} %collective-permute-done.8.rest_1_), channel_id=1, source_target_pairs={{0,2},{2,4},{4,6},{6,7},{7,5},{5,3},{3,1},{1,0},{8,10},{10,12},{12... | collective-permute-start | bytes 589832 | tf_op jit(solution)/shard_map/ppermute | solution.py:460
  32.1 8.1 %collective-permute-start.11 = (bf16[136,768]{1,0:T(8,128)(2,1)S(1)}, bf16[136,768]{1,0:T(8,128)(2,1)S(1)}, u32[]{:S(2)}, u32[]{:S(2)}) collective-permute-start(bf16[136,768]{1,0:T(8,128)(2,1)S(1)} %collective-permute-done.7.rest_0_), channel_id=1, source_target_pairs={{0,2},{2,4},{4,6},{6,7},{7,5},{5,3},{3,1},{1,0},{8,10},{10,12},{12... | collective-permute-start | bytes 626696 | tf_op jit(solution)/shard_map/ppermute | solution.py:460
  34.5 8.2 %collective-permute-start.13 = (bf16[136,768]{1,0:T(8,128)(2,1)S(1)}, bf16[136,768]{1,0:T(8,128)(2,1)S(1)}, u32[]{:S(2)}, u32[]{:S(2)}) collective-permute-start(bf16[136,768]{1,0:T(8,128)(2,1)S(1)} %collective-permute-done.9.rest_2_), channel_id=1, source_target_pairs={{2,0},{4,2},{6,4},{7,6},{5,7},{3,5},{1,3},{0,1},{10,8},{12,10},{14... | collective-permute-start | bytes 626696 | tf_op jit(solution)/shard_map/ppermute | solution.py:461
  37.5 8.5 %copy-start.1 = (bf16[64,768]{1,0:T(8,128)(2,1)S(1)}, bf16[64,768]{1,0:T(8,128)(2,1)}, u32[]{:S(2)}) copy-start(bf16[64,768]{1,0:T(8,128)(2,1)} %get-tuple-element.19.refs_2_.refs_0_.rest_2_) | copy-start | bytes 294916
  38.2 7.7 %collective-permute-start.16 = (bf16[128,768]{1,0:T(8,128)(2,1)S(1)}, bf16[128,768]{1,0:T(8,128)(2,1)S(1)}, u32[]{:S(2)}, u32[]{:S(2)}) collective-permute-start(bf16[128,768]{1,0:T(8,128)(2,1)S(1)} %collective-permute-done.14.rest_3_), channel_id=1, source_target_pairs={{2,0},{4,2},{6,4},{7,6},{5,7},{3,5},{1,3},{0,1},{10,8},{12,10},{14... | collective-permute-start | bytes 589832 | tf_op jit(solution)/shard_map/ppermute | solution.py:465
  40.2 5.8 %collective-permute-start.15 = (bf16[136,768]{1,0:T(8,128)(2,1)S(1)}, bf16[136,768]{1,0:T(8,128)(2,1)S(1)}, u32[]{:S(2)}, u32[]{:S(2)}) collective-permute-start(bf16[136,768]{1,0:T(8,128)(2,1)S(1)} %collective-permute-done.11.rest_0_), channel_id=1, source_target_pairs={{0,2},{2,4},{4,6},{6,7},{7,5},{5,3},{3,1},{1,0},{8,10},{10,12},{12... | collective-permute-start | bytes 626696 | tf_op jit(solution)/shard_map/ppermute | solution.py:464
  46.0 9.5 %copy-start.8 = (s32[4]{0:T(128)S(1)}, s32[4]{0:T(128)}, u32[]{:S(2)}) copy-start(s32[4]{0:T(128)} %listing_ref.3) | copy-start | bytes 52
  48.5 1.9 %collective-permute-start.17 = (bf16[64,768]{1,0:T(8,128)(2,1)S(1)}, bf16[64,768]{1,0:T(8,128)(2,1)S(1)}, u32[]{:S(2)}, u32[]{:S(2)}) collective-permute-start(bf16[64,768]{1,0:T(8,128)(2,1)S(1)} %get-tuple-element.30), channel_id=1, source_target_pairs={{0,8},{8,0},{16,24},{24,16},{1,9},{9,1},{17,25},{25,17},{2,10},{10... | collective-permute-start | bytes 294920 | tf_op jit(solution)/shard_map/ppermute | solution.py:431
  48.6 5.6 %collective-permute-start.18 = (bf16[64,768]{1,0:T(8,128)(2,1)S(1)}, bf16[64,768]{1,0:T(8,128)(2,1)S(1)}, u32[]{:S(2)}, u32[]{:S(2)}) collective-permute-start(bf16[64,768]{1,0:T(8,128)(2,1)S(1)} %get-tuple-element.31), channel_id=1, source_target_pairs={{0,16},{8,24},{16,0},{24,8},{1,17},{9,25},{17,1},{25,9},{2,18},{10... | collective-permute-start | bytes 294920 | tf_op jit(solution)/shard_map/ppermute | solution.py:431
  50.4 5.1 %collective-permute-start.19 = (bf16[64,768]{1,0:T(8,128)(2,1)S(1)}, bf16[64,768]{1,0:T(8,128)(2,1)S(1)}, u32[]{:S(2)}, u32[]{:S(2)}) collective-permute-start(bf16[64,768]{1,0:T(8,128)(2,1)S(1)} %get-tuple-element.32), channel_id=1, source_target_pairs={{0,24},{8,16},{16,8},{24,0},{1,25},{9,17},{17,9},{25,1},{2,26},{10... | collective-permute-start | bytes 294920 | tf_op jit(solution)/shard_map/ppermute | solution.py:431
  (5 other events, 4.9 us)

commit v4 on v3

--- a/solution.py
+++ b/solution.py
@@ -16,14 +16,19 @@
 BIG = 3.3895313892515355e38
 LARGEST = 1e30
 LOG2E = 1.4426950408889634
+COST = 0.05 * 1.1e9
+LARGE = 56 * 1024 * 1024
 VMEM_LIMIT = 32 * 1024 * 1024
-LARGE = 56 * 1024 * 1024
 
 
 def vmem(count):
     return [pl.BlockSpec(memory_space=pltpu.VMEM)] * count
 
 
+def hbm(count):
+    return [pl.BlockSpec(memory_space=pltpu.HBM)] * count
+
+
 def anywhere(count):
     return [pl.BlockSpec(memory_space=pl.ANY)] * count
 
@@ -37,7 +42,7 @@
 
 
 def cost(us):
-    return pl.CostEstimate(flops=int(us * 1.1e9), bytes_accessed=0, transcendentals=0)
+    return pl.CostEstimate(flops=int(us * COST), bytes_accessed=0, transcendentals=0)
 
 
 def piece_of(listing_ref, group, groups):
@@ -47,63 +52,84 @@
     return place
 
 
-def route_kernel(groups, listing_ref, series_ref, mask_ref, token_ref, *rest):
-    out_refs, (held_ref, lines_ref, word_ref, column_ref, sems) = rest[:groups], rest[groups:]
-    piece, width = out_refs[0].shape
+def route_kernel(
+    groups, from_ref, series_ref, mask_ref, token_ref, gain_ref, docs_ref, *rest
+):
+    out_refs, masked_ref = rest[:groups], rest[groups]
+    listing_ref, held_ref, lines_ref, word_ref, scale_ref, numbers_ref, sems = rest[groups + 1 :]
+    rows, width = series_ref.shape
+    piece = rows // groups
     own = lax.axis_index("group")
     copies = [
-        pltpu.make_async_copy(mask_ref, lines_ref, sems.at[groups]),
-        pltpu.make_async_copy(token_ref, word_ref, sems.at[groups + 1]),
+        pltpu.make_async_copy(from_ref, listing_ref, sems.at[0]),
+        pltpu.make_async_copy(mask_ref, lines_ref, sems.at[1]),
+        pltpu.make_async_copy(token_ref, word_ref, sems.at[2]),
+        pltpu.make_async_copy(series_ref, held_ref, sems.at[3]),
+        pltpu.make_async_copy(gain_ref, scale_ref, sems.at[4]),
+        pltpu.make_async_copy(docs_ref, numbers_ref, sems.at[5]),
     ]
-    firsts = []
+    for copy in copies:
+        copy.start()
+    for copy in copies:
+        copy.wait()
+    token = word_ref[...].reshape(1, width)
+    for part in range(lines_ref.shape[0]):
+        line = lines_ref[part : part + 1, :].astype(jnp.float32)
+        hidden = jnp.broadcast_to(line, (128, 128)).T > 0.5
+        here = slice(part * 128, (part + 1) * 128)
+        for lane in range(0, width, 128):
+            masked_ref[here, lane : lane + 128] = jnp.where(
+                hidden,
+                token[:, lane : lane + 128].astype(jnp.float32),
+                held_ref[here, lane : lane + 128].astype(jnp.float32),
+            ).astype(jnp.bfloat16)
+    gain = scale_ref[...].astype(jnp.float32).reshape(1, width)
     for r in range(groups):
         place = piece_of(listing_ref, lax.bitwise_xor(own, jnp.int32(r)), groups)
-        first = pl.multiple_of(place * piece, piece)
-        firsts.append(first)
-        copies.append(
-            pltpu.make_async_copy(
-                series_ref.at[pl.ds(first, piece), :],
-                held_ref.at[r * piece : (r + 1) * piece, :],
-                sems.at[r],
-            )
-        )
-    for copy in copies:
-        copy.start()
-    copies[0].wait()
-    for part in range(lines_ref.shape[0]):
-        line = lines_ref[part : part + 1, :].astype(jnp.float32)
-        column_ref[part * 128 : (part + 1) * 128, :] = jnp.broadcast_to(line, (128, 128)).T
-    copies[1].wait()
-    token = word_ref[...].astype(jnp.float32).reshape(1, width)
-    for r in range(groups):
-        copies[2 + r].wait()
-        hidden = column_ref[pl.ds(firsts[r], piece), :] > 0.5
-        arrived = held_ref[r * piece : (r + 1) * piece, :].astype(jnp.float32)
-        for lane in range(0, width, 128):
-            out_refs[r][:, lane : lane + 128] = jnp.where(
-                hidden, token[:, lane : lane + 128], arrived[:, lane : lane + 128]
-            ).astype(jnp.bfloat16)
-
-
-def route(packing_list, series, recon_mask, mask_token, groups):
+        widened = masked_ref[pl.ds(pl.multiple_of(place * piece, piece), piece), :].astype(jnp.float32)
+        factor = lax.rsqrt(jnp.mean(widened * widened, axis=-1, keepdims=True) + 1e-06)
+        out_refs[r][:piece, :] = (widened * factor * gain).astype(jnp.bfloat16)
+    row = lax.broadcasted_iota(jnp.int32, (8, width), 0)
+    lines = jnp.zeros((8, width), jnp.float32)
+    for d in (1, 2, 3):
+        below = jnp.sum(jnp.where(numbers_ref[...] < d, 1.0, 0.0), axis=-1, keepdims=True)
+        lines = jnp.where(row == d, below, lines)
+    out_refs[0][piece:, :] = lines.astype(jnp.bfloat16)
+
+
+def route(packing_list, series, recon_mask, mask_token, norm_gain, doc_ids, groups):
     rows, width = series.shape
     piece = rows // groups
-    return pl.pallas_call(
+    *pieces, masked = pl.pallas_call(
         functools.partial(route_kernel, groups),
-        out_shape=[jax.ShapeDtypeStruct((piece, width), jnp.bfloat16)] * groups,
-        in_specs=[smem()] + anywhere(3),
-        out_specs=vmem(groups),
+        out_shape=[
+            jax.ShapeDtypeStruct((piece + 8 if r == 0 else piece, width), jnp.bfloat16)
+            for r in range(groups)
+        ]
+        + [jax.ShapeDtypeStruct((rows, width), jnp.bfloat16)],
+        in_specs=anywhere(6),
+        out_specs=vmem(groups + 1),
         scratch_shapes=[
+            pltpu.SMEM((groups,), jnp.int32),
             pltpu.VMEM((rows, width), jnp.bfloat16),
             pltpu.VMEM((rows // 128, 128), jnp.int32),
             pltpu.VMEM((width,), jnp.bfloat16),
-            pltpu.VMEM((rows, 128), jnp.float32),
-            pltpu.SemaphoreType.DMA((groups + 2,)),
+            pltpu.VMEM((width,), jnp.bfloat16),
+            pltpu.VMEM(doc_ids.shape, jnp.int32),
+            pltpu.SemaphoreType.DMA((6,)),
         ],
         compiler_params=params(LARGE),
-        cost_estimate=cost(1.5),
+        cost_estimate=cost(100.0),
         name="route",
-    )(packing_list, series, recon_mask.reshape(rows // 128, 128), mask_token)
+    )(
+        packing_list,
+        series,
+        recon_mask.reshape(rows // 128, 128),
+        mask_token,
+        norm_gain,
+        doc_ids,
+    )
+    return pieces, masked
 
 
 def stage_kernel(count, turned, *refs):
@@ -131,7 +157,7 @@
     return pl.pallas_call(
         functools.partial(stage_kernel, count, turned),
         out_shape=[jax.ShapeDtypeStruct(member.shape, member.dtype) for member in weights],
-        in_specs=anywhere(count + 1),
+        in_specs=hbm(count) + anywhere(1),
         out_specs=vmem(count),
         scratch_shapes=scratch + [pltpu.SemaphoreType.DMA((count,))],
         compiler_params=params(),
@@ -140,39 +166,24 @@
     )(*weights, behind)
 
 
-def norm_kernel(count, with_borders, *refs):
-    piece_refs, gain_ref = refs[:count], refs[count]
-    out_ref = refs[-1]
-    piece, width = piece_refs[0].shape
-    gain = gain_ref[...].astype(jnp.float32).reshape(1, width)
-    for i, ref in enumerate(piece_refs):
-        widened = ref[...].astype(jnp.float32)
-        factor = lax.rsqrt(jnp.mean(widened * widened, axis=-1, keepdims=True) + 1e-06)
-        out_ref[i * piece : (i + 1) * piece, :] = (widened * factor * gain).astype(jnp.bfloat16)
-    if with_borders:
-        docs = refs[count + 1][...]
-        row = lax.broadcasted_iota(jnp.int32, (8, width), 0)
-        lines = jnp.zeros((8, width), jnp.float32)
-        for d in (1, 2, 3):
-            below = jnp.sum(jnp.where(docs < d, 1.0, 0.0), axis=-1, keepdims=True)
-            lines = jnp.where(row == d, below, lines)
-        out_ref[count * piece :, :] = lines.astype(jnp.bfloat16)
-
-
-def norm(pieces, gain, docs=None, behind=()):
-    piece, width = pieces[0].shape
-    count = len(pieces)
-    rows = count * piece + (8 if docs is not None else 0)
-    operands = list(pieces) + [gain] + ([docs] if docs is not None else [])
+def join_kernel(spans, *refs):
+    out_ref, at = refs[-1], 0
+    for i, first, count in spans:
+        out_ref[at : at + count, :] = refs[i][first : first + count, :]
+        at += count
+
+
+def join(members, spans, behind=()):
+    rows, width = sum(count for _, _, count in spans), members[0].shape[1]
     return pl.pallas_call(
-        functools.partial(norm_kernel, count, docs is not None),
+        functools.partial(join_kernel, spans),
         out_shape=jax.ShapeDtypeStruct((rows, width), jnp.bfloat16),
-        in_specs=vmem(len(operands)) + anywhere(len(behind)),
+        in_specs=vmem(len(members)) + anywhere(len(behind)),
         out_specs=vmem(1)[0],
         compiler_params=params(),
-        cost_estimate=cost(0.3),
-        name="norm",
-    )(*operands, *behind)
+        cost_estimate=cost(0.2),
+        name="join",
+    )(*members, *behind)
 
 
 def borders_of(ref, first):
@@ -344,8 +355,7 @@
 
 
 def last_kernel(groups, piece, layout, queries_ref, wk_ref, wv_ref, old_ref, wo_ref, *rest):
-    row_refs = rest[: -2 * groups - 1]
-    piece_refs, out_refs = rest[-2 * groups - 1 : -groups - 1], rest[-groups - 1 : -1]
+    row_refs, out_refs = rest[: -groups - 1], rest[-groups - 1 : -1]
     attended_ref = rest[-1]
 
     def finish(head, sums, top):
@@ -355,9 +365,7 @@
     attended = attended_ref[...].T.astype(jnp.bfloat16)
     mixed = jnp.dot(attended, wo_ref[...], preferred_element_type=jnp.float32)
     for r in range(groups):
-        out_refs[r][...] = (
-            piece_refs[r][...].astype(jnp.float32) + mixed[r * piece : (r + 1) * piece]
-        ).astype(jnp.bfloat16)
+        out_refs[r][...] = mixed[r * piece : (r + 1) * piece].astype(jnp.bfloat16)
 
 
 def own_call(members, layout, w_query, w_key, w_value, piece, rows):
@@ -388,41 +396,64 @@
     )(queries, w_key, w_value, state, *members)
 
 
-def last_call(queries, w_key, w_value, state, w_out, members, layout, pieces, piece):
-    groups, width = len(pieces), w_key.shape[0]
+def last_call(queries, w_key, w_value, state, w_out, members, layout, groups, piece):
+    width = w_key.shape[0]
     rows = queries.shape[2]
     return pl.pallas_call(
         functools.partial(last_kernel, groups, piece, layout),
         out_shape=[jax.ShapeDtypeStruct((piece, width), jnp.bfloat16)] * groups,
-        in_specs=vmem(5 + len(members) + groups),
+        in_specs=vmem(5 + len(members)),
         out_specs=vmem(groups),
         scratch_shapes=[pltpu.VMEM((HEADS * HD, rows), jnp.float32)],
         compiler_params=params(),
         cost_estimate=cost(3.0),
         name="last_rows",
-    )(queries, w_key, w_value, state, w_out, *members, *pieces)
-
-
-def arrange_kernel(groups, listing_ref, *refs):
+    )(queries, w_key, w_value, state, w_out, *members)
+
+
+def arrange_kernel(groups, listing_ref, masked_ref, *refs):
     piece_refs, out_ref = refs[:groups], refs[groups]
     piece = piece_refs[0].shape[0]
     own = lax.axis_index("group")
     for r in range(groups):
         place = piece_of(listing_ref, lax.bitwise_xor(own, jnp.int32(r)), groups)
-        out_ref[pl.ds(pl.multiple_of(place * piece, piece), piece), :] = piece_refs[r][...]
-
-
-def arrange(packing_list, pieces):
+        here = pl.ds(pl.multiple_of(place * piece, piece), piece)
+        out_ref[here, :] = (
+            masked_ref[here, :].astype(jnp.float32) + piece_refs[r][...].astype(jnp.float32)
+        ).astype(jnp.bfloat16)
+
+
+def arrange(packing_list, masked, pieces):
     groups, (piece, width) = len(pieces), pieces[0].shape
     return pl.pallas_call(
         functools.partial(arrange_kernel, groups),
         out_shape=jax.ShapeDtypeStruct((groups * piece, width), jnp.bfloat16),
-        in_specs=[smem()] + vmem(groups),
+        in_specs=[smem()] + vmem(groups + 1),
         out_specs=vmem(1)[0],
         compiler_params=params(),
         cost_estimate=cost(1.3),
         name="arrange",
-    )(packing_list, *pieces)
+    )(packing_list, masked, *pieces)
+
+
+def hold_kernel(*refs):
+    pass
+
+
+def hold(members, *behind):
+    count = len(members)
+    return tuple(
+        pl.pallas_call(
+            hold_kernel,
+            out_shape=[jax.ShapeDtypeStruct(member.shape, member.dtype) for member in members],
+            in_specs=anywhere(count + len(behind)),
+            out_specs=anywhere(count),
+            input_output_aliases={i: i for i in range(count)},
+            compiler_params=params(),
+            cost_estimate=cost(0.1),
+            name="hold",
+        )(*members, *behind)
+    )
 
 
 def exchange(pieces):
@@ -444,28 +475,35 @@
     backward = [(there, here) for here, there in onward]
 
     half = rows // 2
-    sent = route(packing_list, series, recon_mask, mask_token, groups)
-    w_query, w_key = stage((w_query, w_key), None, sent[0], 2.0)
+    sent, masked = route(
+        packing_list, series, recon_mask, mask_token, norm_gain, doc_ids, groups
+    )
+    w_query, w_key, w_value = stage((w_query, w_key, w_value), 2, sent[0], 0.01)
     pieces = exchange(sent)
-    a = norm(pieces[: groups // 2], norm_gain, doc_ids, (w_query,))
-    w_value, w_out = stage((w_value, w_out), 0, a, 2.0)
-    b = norm(pieces[groups // 2 :], norm_gain, None, (a, w_value))
-    own = (a, b)
+    low = groups // 2
+    spans = [(r, 0, piece) for r in range(low)]
+    a = join(pieces[:low], spans + [(0, piece, 8)])
+    b = join(pieces[low:], spans, (a, w_value))
+
+    def onto(member):
+        return lax.ppermute(member, "ctx", onward)
+
+    def back(member):
+        return lax.ppermute(member, "ctx", backward)
+
     own_layout = ([(0, 0, half), (1, 0, half)], (0, half))
     pair_layout = (own_layout, ([(2, 0, half), (3, 0, half)], (2, half)))
     far_layout = (own_layout,)
-    queries, state = own_call(own, own_layout, w_query, w_key, w_value, piece, rows)
-    before, after = own, own
+    queries, state = own_call((a, b), own_layout, w_query, w_key, w_value, piece, rows)
+    a_before, a_after, b_before, b_after = a, a, b, b
     for step in range(1, shards // 2):
-        before = tuple(lax.ppermute(member, "ctx", onward) for member in before)
-        after = tuple(lax.ppermute(member, "ctx", backward) for member in after)
-        state = chunk_call(queries, w_key, w_value, state, before + after, pair_layout, piece)
-    far = (
-        lax.ppermute(before[0], "ctx", onward),
-        lax.ppermute(after[1], "ctx", backward),
-    )
-    done = last_call(queries, w_key, w_value, state, w_out, far, far_layout, pieces, piece)
-    return arrange(packing_list, exchange(done))
+        a_before, a_after = hold((onto(a_before), back(a_after)))
+        b_before, b_after = hold((onto(b_before), back(b_after)), state)
+        received = (a_before, b_before, a_after, b_after)
+        state = chunk_call(queries, w_key, w_value, state, received, pair_layout, piece)
+    far = (onto(a_before), back(b_after))
+    done = last_call(queries, w_key, w_value, state, w_out, far, far_layout, groups, piece)
+    return arrange(packing_list, masked, exchange(done))
 
 
 def solution(mesh):

time: 57.1 us -> 55.2 us (0.967)
  local copies, waits for them, and re-layouts: 2.12 us -> 0.92 us
  waiting for transfers between devices: 14.2 us -> 15.2 us
  starting transfers between devices: 20.3 us -> 19.5 us
  Pallas kernels: 20 us -> 19.3 us
    ppermute x14, waiting for transfers between devices: 7.49 us -> 8.93 us  [the longest x7 6.83 us: back(): return lax.ppermute(member, 'ctx', backward)]
    unnamed x18 -> x14, local copies, waits for them, and re-layouts: 2.12 us -> 0.92 us
    ppermute x14, starting transfers between devices: 15.3 us -> 14.4 us  [the longest x7 11.4 us: onto(): return lax.ppermute(member, 'ctx', onward)]
    pallas_call x2 -> x1, Pallas kernels: 1.37 us -> 1.12 us  [stage(): pl.pallas_call(functools.partial(stage_kernel, count, turned), out_shape=...]
  transfers between devices with their start and end apart: 20 -> 20, of which waited for: 12 -> 10; matrix products, arithmetic and copies ran while one was open for 0% -> 0% of each run, Pallas kernels for 23% -> 24%
where the time goes in v4:
time: 55.2 us; the launch traced here: 55.1 us
  starting transfers between devices  19.5 us (35%)
  Pallas kernels  19.3 us (35%)
  waiting for transfers between devices  15.2 us (28%)
  local copies, waits for them, and re-layouts  0.92 us (2%)
    ppermute x7, starting transfers between devices, onto(): return lax.ppermute(member, 'ctx', onward)  11.4 us
    pallas_call x3, Pallas kernels, chunk_call(): pl.pallas_call(functools.partial(chunk_kernel, piece, layout), out_shape=...  9.1 us
    ppermute x7, waiting for transfers between devices, back(): return lax.ppermute(member, 'ctx', backward)  6.83 us
    ppermute x6, waiting for transfers between devices, exchange(): lax.ppermute(pieces[r], 'group', [(i, i ^ r) for i in range(groups)])  6.23 us
    ppermute x6, starting transfers between devices, exchange(): lax.ppermute(pieces[r], 'group', [(i, i ^ r) for i in range(groups)])  5.09 us
    ppermute x7, starting transfers between devices, back(): return lax.ppermute(member, 'ctx', backward)  2.99 us
    pallas_call x1, Pallas kernels, own_call(): pl.pallas_call(functools.partial(own_kernel, piece, parts, borders_at), o...  2.71 us
    pallas_call x1, Pallas kernels, last_call(): pl.pallas_call(functools.partial(last_kernel, groups, piece, layout), out...  2.55 us
  transfers between devices with their start and end apart: 20, of which 10 were waited for; matrix products, arithmetic and copies ran while one was open for 0% of the time, Pallas kernels for 24%

profile of v4, /device:TPU:0, one launch (start us, length us, event | category | flops | bytes accessed | tf_op | source)
XLA Modules:
  0.0 55.1 jit_solution(2544182531526527928)
XLA Ops:
  0.0 2.4 %route.1 = (bf16[72,768]{1,0:T(8,128)(2,1)}, bf16[64,768]{1,0:T(8,128)(2,1)}, bf16[64,768]{1,0:T(8,128)(2,1)}, bf16[64,768]{1,0:T(8,128)(2,1)}, bf16[256,768]{1,0:T(8,128)(2,1)}) custom-call(s32[4]{0:T(128)} %listing_ref.1, bf16[256,768]{1,0:T(8,128)(2,1)} %series_ref.1, s32[2,128]{1,0:T(2,128)} %bitcast.1, bf16[768]{0:T(1024)(128)(2,1)} %token_ref.1, ...), custom_call_target="tpu_custom_call" | custom-call | flops 5500000256 | tf_op jit(solution)/shard_map/route/pallas_call | solution.py:103
  3.0 2.6 %collective-permute-start.1 = (bf16[64,768]{1,0:T(8,128)(2,1)}, bf16[64,768]{1,0:T(8,128)(2,1)S(1)}, u32[]{:S(2)}, u32[]{:S(2)}) collective-permute-start(bf16[64,768]{1,0:T(8,128)(2,1)} %get-tuple-element.34), channel_id=1, source_target_pairs={{0,16},{8,24},{16,0},{24,8},{1,17},{9,25},{17,1},{25,9},{2,18},{10... | collective-permute-start | bytes 294920 | tf_op jit(solution)/shard_map/ppermute | solution.py:462
  6.5 1.9 %collective-permute-start.3 = (bf16[136,768]{1,0:T(8,128)(2,1)S(1)}, bf16[136,768]{1,0:T(8,128)(2,1)S(1)}, u32[]{:S(2)}, u32[]{:S(2)}) collective-permute-start(bf16[136,768]{1,0:T(8,128)(2,1)S(1)} %join.2.refs_2_.refs_0_), channel_id=1, source_target_pairs={{0,2},{2,4},{4,6},{6,7},{7,5},{5,3},{3,1},{1,0},{8,10},{10,12},{12... | collective-permute-start | bytes 626696 | tf_op jit(solution)/shard_map/ppermute | solution.py:489
  9.7 1.2 %collective-permute-done.2.refs_1_ = bf16[64,768]{1,0:T(8,128)(2,1)S(1)} collective-permute-done((bf16[64,768]{1,0:T(8,128)(2,1)}, bf16[64,768]{1,0:T(8,128)(2,1)S(1)}, u32[]{:S(2)}, u32[]{:S(2)}) %collective-permute-start.2) | collective-permute-done | bytes 98336 | tf_op jit(solution)/shard_map/ppermute | solution.py:462
  11.0 1.7 %collective-permute-start.5 = (bf16[128,768]{1,0:T(8,128)(2,1)S(1)}, bf16[128,768]{1,0:T(8,128)(2,1)S(1)}, u32[]{:S(2)}, u32[]{:S(2)}) collective-permute-start(bf16[128,768]{1,0:T(8,128)(2,1)S(1)} %join.3.refs_1_), channel_id=1, source_target_pairs={{0,2},{2,4},{4,6},{6,7},{7,5},{5,3},{3,1},{1,0},{8,10},{10,12},{12... | collective-permute-start | bytes 589832 | tf_op jit(solution)/shard_map/ppermute | solution.py:489
  14.0 1.5 %collective-permute-done.4.refs_1_ = bf16[136,768]{1,0:T(8,128)(2,1)S(1)} collective-permute-done((bf16[136,768]{1,0:T(8,128)(2,1)S(1)}, bf16[136,768]{1,0:T(8,128)(2,1)S(1)}, u32[]{:S(2)}, u32[]{:S(2)}) %collective-permute-start.4) | collective-permute-done | bytes 208928 | tf_op jit(solution)/shard_map/ppermute | solution.py:492
  15.5 1.6 %collective-permute-start.7 = (bf16[136,768]{1,0:T(8,128)(2,1)S(1)}, bf16[136,768]{1,0:T(8,128)(2,1)S(1)}, u32[]{:S(2)}, u32[]{:S(2)}) collective-permute-start(bf16[136,768]{1,0:T(8,128)(2,1)S(1)} %get-tuple-element.41.rest_0_), channel_id=1, source_target_pairs={{0,2},{2,4},{4,6},{6,7},{7,5},{5,3},{3,1},{1,0},{8,10},{10,12},{12... | collective-permute-start | bytes 626696 | tf_op jit(solution)/shard_map/ppermute | solution.py:489
  17.5 2.7 %own_rows.1 = (bf16[12,128,256]{2,1,0:T(8,128)(2,1)S(1)}, f32[12,80,256]{2,1,0:T(8,128)S(1)}) custom-call(bf16[136,768]{1,0:T(8,128)(2,1)S(1)} %join.2.refs_2_.refs_0_, bf16[128,768]{1,0:T(8,128)(2,1)S(1)} %join.3.refs_1_, bf16[768,768]{1,0:T(8,128)(2,1)S(1)} %get-tuple-element.37.refs_2_, bf16[768,768]{1,0:T(8,128)(2,1)S(1)} %get-tuple-element.38.refs_3_.wk_ref, ...), custom_call_target="tpu_custom_call" | custom-call | flops 165000000 | tf_op jit(solution)/shard_map/own_rows/pallas_call | solution.py:373
  20.4 1.6 %collective-permute-start.9 = (bf16[128,768]{1,0:T(8,128)(2,1)S(1)}, bf16[128,768]{1,0:T(8,128)(2,1)S(1)}, u32[]{:S(2)}, u32[]{:S(2)}) collective-permute-start(bf16[128,768]{1,0:T(8,128)(2,1)S(1)} %get-tuple-element.42.rest_1_), channel_id=1, source_target_pairs={{0,2},{2,4},{4,6},{6,7},{7,5},{5,3},{3,1},{1,0},{8,10},{10,12},{12... | collective-permute-start | bytes 589832 | tf_op jit(solution)/shard_map/ppermute | solution.py:489
  22.4 1.2 %collective-permute-done.7.refs_0_ = bf16[136,768]{1,0:T(8,128)(2,1)S(1)} collective-permute-done((bf16[136,768]{1,0:T(8,128)(2,1)S(1)}, bf16[136,768]{1,0:T(8,128)(2,1)S(1)}, u32[]{:S(2)}, u32[]{:S(2)}) %collective-permute-start.7) | collective-permute-done | bytes 208928 | tf_op jit(solution)/shard_map/ppermute | solution.py:489
  23.6 1.6 %collective-permute-done.8.refs_1_ = bf16[136,768]{1,0:T(8,128)(2,1)S(1)} collective-permute-done((bf16[136,768]{1,0:T(8,128)(2,1)S(1)}, bf16[136,768]{1,0:T(8,128)(2,1)S(1)}, u32[]{:S(2)}, u32[]{:S(2)}) %collective-permute-start.8) | collective-permute-done | bytes 208928 | tf_op jit(solution)/shard_map/ppermute | solution.py:492
  25.2 1.6 %collective-permute-start.11 = (bf16[136,768]{1,0:T(8,128)(2,1)S(1)}, bf16[136,768]{1,0:T(8,128)(2,1)S(1)}, u32[]{:S(2)}, u32[]{:S(2)}) collective-permute-start(bf16[136,768]{1,0:T(8,128)(2,1)S(1)} %get-tuple-element.45.rest_0_), channel_id=1, source_target_pairs={{0,2},{2,4},{4,6},{6,7},{7,5},{5,3},{3,1},{1,0},{8,10},{10,12},{12... | collective-permute-start | bytes 626696 | tf_op jit(solution)/shard_map/ppermute | solution.py:489
  27.2 3.0 %received_rows.3.refs_2_.old_ref = f32[12,80,256]{2,1,0:T(8,128)S(1)} custom-call(bf16[12,128,256]{2,1,0:T(8,128)(2,1)S(1)} %get-tuple-element.39.queries_ref, bf16[768,768]{1,0:T(8,128)(2,1)S(1)} %get-tuple-element.38.refs_3_.wk_ref, bf16[768,768]{1,0:T(8,128)(2,1)S(1)} %get-tuple-element.36.refs_3_.refs_4_.wv_ref, ...), custom_call_target="tpu_custom_call" | custom-call | flops 192500000 | tf_op jit(solution)/shard_map/received_rows/pallas_call | solution.py:388
  30.2 1.6 %collective-permute-start.13 = (bf16[128,768]{1,0:T(8,128)(2,1)S(1)}, bf16[128,768]{1,0:T(8,128)(2,1)S(1)}, u32[]{:S(2)}, u32[]{:S(2)}) collective-permute-start(bf16[128,768]{1,0:T(8,128)(2,1)S(1)} %get-tuple-element.46.rest_1_), channel_id=1, source_target_pairs={{0,2},{2,4},{4,6},{6,7},{7,5},{5,3},{3,1},{1,0},{8,10},{10,12},{12... | collective-permute-start | bytes 589832 | tf_op jit(solution)/shard_map/ppermute | solution.py:489
  32.3 1.7 %collective-permute-done.12.refs_1_ = bf16[136,768]{1,0:T(8,128)(2,1)S(1)} collective-permute-done((bf16[136,768]{1,0:T(8,128)(2,1)S(1)}, bf16[136,768]{1,0:T(8,128)(2,1)S(1)}, u32[]{:S(2)}, u32[]{:S(2)}) %collective-permute-start.12) | collective-permute-done | bytes 208928 | tf_op jit(solution)/shard_map/ppermute | solution.py:492
  34.0 1.5 %collective-permute-start.15 = (bf16[136,768]{1,0:T(8,128)(2,1)S(1)}, bf16[136,768]{1,0:T(8,128)(2,1)S(1)}, u32[]{:S(2)}, u32[]{:S(2)}) collective-permute-start(bf16[136,768]{1,0:T(8,128)(2,1)S(1)} %get-tuple-element.49.rest_0_), channel_id=1, source_target_pairs={{0,2},{2,4},{4,6},{6,7},{7,5},{5,3},{3,1},{1,0},{8,10},{10,12},{12... | collective-permute-start | bytes 626696 | tf_op jit(solution)/shard_map/ppermute | solution.py:489
  35.5 3.0 %received_rows.4.refs_2_.old_ref = f32[12,80,256]{2,1,0:T(8,128)S(1)} custom-call(bf16[12,128,256]{2,1,0:T(8,128)(2,1)S(1)} %get-tuple-element.39.queries_ref, bf16[768,768]{1,0:T(8,128)(2,1)S(1)} %get-tuple-element.38.refs_3_.wk_ref, bf16[768,768]{1,0:T(8,128)(2,1)S(1)} %get-tuple-element.36.refs_3_.refs_4_.wv_ref, ...), custom_call_target="tpu_custom_call" | custom-call | flops 192500000 | tf_op jit(solution)/shard_map/received_rows/pallas_call | solution.py:388
  39.0 3.2 %received_rows.5.old_ref = f32[12,80,256]{2,1,0:T(8,128)S(1)} custom-call(bf16[12,128,256]{2,1,0:T(8,128)(2,1)S(1)} %get-tuple-element.39.queries_ref, bf16[768,768]{1,0:T(8,128)(2,1)S(1)} %get-tuple-element.38.refs_3_.wk_ref, bf16[768,768]{1,0:T(8,128)(2,1)S(1)} %get-tuple-element.36.refs_3_.refs_4_.wv_ref, ...), custom_call_target="tpu_custom_call" | custom-call | flops 192500000 | tf_op jit(solution)/shard_map/received_rows/pallas_call | solution.py:388
  42.3 1.9 %collective-permute-done.16.rest_1_ = bf16[128,768]{1,0:T(8,128)(2,1)S(1)} collective-permute-done((bf16[128,768]{1,0:T(8,128)(2,1)S(1)}, bf16[128,768]{1,0:T(8,128)(2,1)S(1)}, u32[]{:S(2)}, u32[]{:S(2)}) %collective-permute-start.16) | collective-permute-done | bytes 196640 | tf_op jit(solution)/shard_map/ppermute | solution.py:492
  44.2 2.6 %last_rows.1 = (bf16[64,768]{1,0:T(8,128)(2,1)S(1)}, bf16[64,768]{1,0:T(8,128)(2,1)S(1)}, bf16[64,768]{1,0:T(8,128)(2,1)S(1)}, bf16[64,768]{1,0:T(8,128)(2,1)S(1)}) custom-call(bf16[12,128,256]{2,1,0:T(8,128)(2,1)S(1)} %get-tuple-element.39.queries_ref, bf16[768,768]{1,0:T(8,128)(2,1)S(1)} %get-tuple-element.38.refs_3_.wk_ref, ...), custom_call_target="tpu_custom_call" | custom-call | flops 165000000 | tf_op jit(solution)/shard_map/last_rows/pallas_call | solution.py:402
  46.8 1.6 %collective-permute-start.18 = (bf16[64,768]{1,0:T(8,128)(2,1)S(1)}, bf16[64,768]{1,0:T(8,128)(2,1)S(1)}, u32[]{:S(2)}, u32[]{:S(2)}) collective-permute-start(bf16[64,768]{1,0:T(8,128)(2,1)S(1)} %get-tuple-element.55), channel_id=1, source_target_pairs={{0,16},{8,24},{16,0},{24,8},{1,17},{9,25},{17,1},{25,9},{2,18},{10... | collective-permute-start | bytes 294920 | tf_op jit(solution)/shard_map/ppermute | solution.py:462
  48.7 3.8 %collective-permute-done.18.refs_2_ = bf16[64,768]{1,0:T(8,128)(2,1)S(1)} collective-permute-done((bf16[64,768]{1,0:T(8,128)(2,1)S(1)}, bf16[64,768]{1,0:T(8,128)(2,1)S(1)}, u32[]{:S(2)}, u32[]{:S(2)}) %collective-permute-start.18) | collective-permute-done | bytes 98336 | tf_op jit(solution)/shard_map/ppermute | solution.py:462
  52.5 1.2 %collective-permute-done.19.refs_3_ = bf16[64,768]{1,0:T(8,128)(2,1)S(1)} collective-permute-done((bf16[64,768]{1,0:T(8,128)(2,1)S(1)}, bf16[64,768]{1,0:T(8,128)(2,1)S(1)}, u32[]{:S(2)}, u32[]{:S(2)}) %collective-permute-start.19) | collective-permute-done | bytes 98336 | tf_op jit(solution)/shard_map/ppermute | solution.py:462
  53.7 1.4 %arrange.1 = bf16[256,768]{1,0:T(8,128)(2,1)} custom-call(s32[4]{0:T(128)S(1)} %copy-done.6, bf16[256,768]{1,0:T(8,128)(2,1)S(1)} %copy-done.5, bf16[64,768]{1,0:T(8,128)(2,1)S(1)} %get-tuple-element.53.refs_0_, bf16[64,768]{1,0:T(8,128)(2,1)S(1)} %collective-permute-done.17.refs_1_, bf16[64,768]{1,0:T(8,128)(2,1)S(1)} %collective-permute-done.18.refs_2_, ...), custom_call_target="tpu_custom_call" | custom-call | flops 71500000 | tf_op jit(solution)/shard_map/arrange/pallas_call | solution.py:428
  (46 shorter events, 7.1 us)
Async XLA Ops:
  0.0 8.6 %copy-start.1 = (bf16[768,768]{1,0:T(8,128)(2,1)S(1)}, bf16[768,768]{1,0:T(8,128)(2,1)}, u32[]{:S(2)}) copy-start(bf16[768,768]{1,0:T(8,128)(2,1)} %refs_1_.1) | copy-start | bytes 3538948
  0.0 8.6 %copy-start.2 = (bf16[768,768]{1,0:T(8,128)(2,1)S(1)}, bf16[768,768]{1,0:T(8,128)(2,1)}, u32[]{:S(2)}) copy-start(bf16[768,768]{1,0:T(8,128)(2,1)} %refs_2_.1) | copy-start | bytes 3538948
  2.4 3.2 %collective-permute-start = (bf16[64,768]{1,0:T(8,128)(2,1)}, bf16[64,768]{1,0:T(8,128)(2,1)S(1)}, u32[]{:S(2)}, u32[]{:S(2)}) collective-permute-start(bf16[64,768]{1,0:T(8,128)(2,1)} %get-tuple-element.33), channel_id=1, source_target_pairs={{0,8},{8,0},{16,24},{24,16},{1,9},{9,1},{17,25},{25,17},{2,10},{10... | collective-permute-start | bytes 294920 | tf_op jit(solution)/shard_map/ppermute | solution.py:462
  3.0 6.8 %collective-permute-start.1 = (bf16[64,768]{1,0:T(8,128)(2,1)}, bf16[64,768]{1,0:T(8,128)(2,1)S(1)}, u32[]{:S(2)}, u32[]{:S(2)}) collective-permute-start(bf16[64,768]{1,0:T(8,128)(2,1)} %get-tuple-element.34), channel_id=1, source_target_pairs={{0,16},{8,24},{16,0},{24,8},{1,17},{9,25},{17,1},{25,9},{2,18},{10... | collective-permute-start | bytes 294920 | tf_op jit(solution)/shard_map/ppermute | solution.py:462
  5.5 5.4 %collective-permute-start.2 = (bf16[64,768]{1,0:T(8,128)(2,1)}, bf16[64,768]{1,0:T(8,128)(2,1)S(1)}, u32[]{:S(2)}, u32[]{:S(2)}) collective-permute-start(bf16[64,768]{1,0:T(8,128)(2,1)} %get-tuple-element.35), channel_id=1, source_target_pairs={{0,24},{8,16},{16,8},{24,0},{1,25},{9,17},{17,9},{25,1},{2,26},{10... | collective-permute-start | bytes 294920 | tf_op jit(solution)/shard_map/ppermute | solution.py:462
  6.5 7.5 %collective-permute-start.3 = (bf16[136,768]{1,0:T(8,128)(2,1)S(1)}, bf16[136,768]{1,0:T(8,128)(2,1)S(1)}, u32[]{:S(2)}, u32[]{:S(2)}) collective-permute-start(bf16[136,768]{1,0:T(8,128)(2,1)S(1)} %join.2.refs_2_.refs_0_), channel_id=1, source_target_pairs={{0,2},{2,4},{4,6},{6,7},{7,5},{5,3},{3,1},{1,0},{8,10},{10,12},{12... | collective-permute-start | bytes 626696 | tf_op jit(solution)/shard_map/ppermute | solution.py:489
  8.4 7.1 %collective-permute-start.4 = (bf16[136,768]{1,0:T(8,128)(2,1)S(1)}, bf16[136,768]{1,0:T(8,128)(2,1)S(1)}, u32[]{:S(2)}, u32[]{:S(2)}) collective-permute-start(bf16[136,768]{1,0:T(8,128)(2,1)S(1)} %join.2.refs_2_.refs_0_), channel_id=1, source_target_pairs={{2,0},{4,2},{6,4},{7,6},{5,7},{3,5},{1,3},{0,1},{10,8},{12,10},{14... | collective-permute-start | bytes 626696 | tf_op jit(solution)/shard_map/ppermute | solution.py:492
  11.0 9.3 %collective-permute-start.5 = (bf16[128,768]{1,0:T(8,128)(2,1)S(1)}, bf16[128,768]{1,0:T(8,128)(2,1)S(1)}, u32[]{:S(2)}, u32[]{:S(2)}) collective-permute-start(bf16[128,768]{1,0:T(8,128)(2,1)S(1)} %join.3.refs_1_), channel_id=1, source_target_pairs={{0,2},{2,4},{4,6},{6,7},{7,5},{5,3},{3,1},{1,0},{8,10},{10,12},{12... | collective-permute-start | bytes 589832 | tf_op jit(solution)/shard_map/ppermute | solution.py:489
  12.7 7.7 %collective-permute-start.6 = (bf16[128,768]{1,0:T(8,128)(2,1)S(1)}, bf16[128,768]{1,0:T(8,128)(2,1)S(1)}, u32[]{:S(2)}, u32[]{:S(2)}) collective-permute-start(bf16[128,768]{1,0:T(8,128)(2,1)S(1)} %join.3.refs_1_), channel_id=1, source_target_pairs={{2,0},{4,2},{6,4},{7,6},{5,7},{3,5},{1,3},{0,1},{10,8},{12,10},{14... | collective-permute-start | bytes 589832 | tf_op jit(solution)/shard_map/ppermute | solution.py:492
  15.5 8.1 %collective-permute-start.7 = (bf16[136,768]{1,0:T(8,128)(2,1)S(1)}, bf16[136,768]{1,0:T(8,128)(2,1)S(1)}, u32[]{:S(2)}, u32[]{:S(2)}) collective-permute-start(bf16[136,768]{1,0:T(8,128)(2,1)S(1)} %get-tuple-element.41.rest_0_), channel_id=1, source_target_pairs={{0,2},{2,4},{4,6},{6,7},{7,5},{5,3},{3,1},{1,0},{8,10},{10,12},{12... | collective-permute-start | bytes 626696 | tf_op jit(solution)/shard_map/ppermute | solution.py:489
  17.1 8.1 %collective-permute-start.8 = (bf16[136,768]{1,0:T(8,128)(2,1)S(1)}, bf16[136,768]{1,0:T(8,128)(2,1)S(1)}, u32[]{:S(2)}, u32[]{:S(2)}) collective-permute-start(bf16[136,768]{1,0:T(8,128)(2,1)S(1)} %get-tuple-element.43.rest_2_), channel_id=1, source_target_pairs={{2,0},{4,2},{6,4},{7,6},{5,7},{3,5},{1,3},{0,1},{10,8},{12,10},{14... | collective-permute-start | bytes 626696 | tf_op jit(solution)/shard_map/ppermute | solution.py:492
  20.4 9.8 %collective-permute-start.9 = (bf16[128,768]{1,0:T(8,128)(2,1)S(1)}, bf16[128,768]{1,0:T(8,128)(2,1)S(1)}, u32[]{:S(2)}, u32[]{:S(2)}) collective-permute-start(bf16[128,768]{1,0:T(8,128)(2,1)S(1)} %get-tuple-element.42.rest_1_), channel_id=1, source_target_pairs={{0,2},{2,4},{4,6},{6,7},{7,5},{5,3},{3,1},{1,0},{8,10},{10,12},{12... | collective-permute-start | bytes 589832 | tf_op jit(solution)/shard_map/ppermute | solution.py:489
  22.0 8.2 %collective-permute-start.10 = (bf16[128,768]{1,0:T(8,128)(2,1)S(1)}, bf16[128,768]{1,0:T(8,128)(2,1)S(1)}, u32[]{:S(2)}, u32[]{:S(2)}) collective-permute-start(bf16[128,768]{1,0:T(8,128)(2,1)S(1)} %get-tuple-element.44.rest_3_), channel_id=1, source_target_pairs={{2,0},{4,2},{6,4},{7,6},{5,7},{3,5},{1,3},{0,1},{10,8},{12,10},{14... | collective-permute-start | bytes 589832 | tf_op jit(solution)/shard_map/ppermute | solution.py:492
  25.2 7.1 %collective-permute-start.11 = (bf16[136,768]{1,0:T(8,128)(2,1)S(1)}, bf16[136,768]{1,0:T(8,128)(2,1)S(1)}, u32[]{:S(2)}, u32[]{:S(2)}) collective-permute-start(bf16[136,768]{1,0:T(8,128)(2,1)S(1)} %get-tuple-element.45.rest_0_), channel_id=1, source_target_pairs={{0,2},{2,4},{4,6},{6,7},{7,5},{5,3},{3,1},{1,0},{8,10},{10,12},{12... | collective-permute-start | bytes 626696 | tf_op jit(solution)/shard_map/ppermute | solution.py:489
  26.8 7.2 %collective-permute-start.12 = (bf16[136,768]{1,0:T(8,128)(2,1)S(1)}, bf16[136,768]{1,0:T(8,128)(2,1)S(1)}, u32[]{:S(2)}, u32[]{:S(2)}) collective-permute-start(bf16[136,768]{1,0:T(8,128)(2,1)S(1)} %get-tuple-element.47.rest_2_), channel_id=1, source_target_pairs={{2,0},{4,2},{6,4},{7,6},{5,7},{3,5},{1,3},{0,1},{10,8},{12,10},{14... | collective-permute-start | bytes 626696 | tf_op jit(solution)/shard_map/ppermute | solution.py:492
  30.2 8.2 %collective-permute-start.13 = (bf16[128,768]{1,0:T(8,128)(2,1)S(1)}, bf16[128,768]{1,0:T(8,128)(2,1)S(1)}, u32[]{:S(2)}, u32[]{:S(2)}) collective-permute-start(bf16[128,768]{1,0:T(8,128)(2,1)S(1)} %get-tuple-element.46.rest_1_), channel_id=1, source_target_pairs={{0,2},{2,4},{4,6},{6,7},{7,5},{5,3},{3,1},{1,0},{8,10},{10,12},{12... | collective-permute-start | bytes 589832 | tf_op jit(solution)/shard_map/ppermute | solution.py:489
  31.9 6.6 %collective-permute-start.14 = (bf16[128,768]{1,0:T(8,128)(2,1)S(1)}, bf16[128,768]{1,0:T(8,128)(2,1)S(1)}, u32[]{:S(2)}, u32[]{:S(2)}) collective-permute-start(bf16[128,768]{1,0:T(8,128)(2,1)S(1)} %get-tuple-element.48.rest_3_), channel_id=1, source_target_pairs={{2,0},{4,2},{6,4},{7,6},{5,7},{3,5},{1,3},{0,1},{10,8},{12,10},{14... | collective-permute-start | bytes 589832 | tf_op jit(solution)/shard_map/ppermute | solution.py:492
  34.0 10.2 %collective-permute-start.15 = (bf16[136,768]{1,0:T(8,128)(2,1)S(1)}, bf16[136,768]{1,0:T(8,128)(2,1)S(1)}, u32[]{:S(2)}, u32[]{:S(2)}) collective-permute-start(bf16[136,768]{1,0:T(8,128)(2,1)S(1)} %get-tuple-element.49.rest_0_), channel_id=1, source_target_pairs={{0,2},{2,4},{4,6},{6,7},{7,5},{5,3},{3,1},{1,0},{8,10},{10,12},{12... | collective-permute-start | bytes 626696 | tf_op jit(solution)/shard_map/ppermute | solution.py:489
  38.5 5.7 %collective-permute-start.16 = (bf16[128,768]{1,0:T(8,128)(2,1)S(1)}, bf16[128,768]{1,0:T(8,128)(2,1)S(1)}, u32[]{:S(2)}, u32[]{:S(2)}) collective-permute-start(bf16[128,768]{1,0:T(8,128)(2,1)S(1)} %get-tuple-element.52.rest_3_), channel_id=1, source_target_pairs={{2,0},{4,2},{6,4},{7,6},{5,7},{3,5},{1,3},{0,1},{10,8},{12,10},{14... | collective-permute-start | bytes 589832 | tf_op jit(solution)/shard_map/ppermute | solution.py:492
  42.2 11.5 %copy-start.5 = (bf16[256,768]{1,0:T(8,128)(2,1)S(1)}, bf16[256,768]{1,0:T(8,128)(2,1)}, u32[]{:S(2)}) copy-start(bf16[256,768]{1,0:T(8,128)(2,1)} %get-tuple-element.31.masked_ref) | copy-start | bytes 1179652
  42.2 11.4 %copy-start.6 = (s32[4]{0:T(128)S(1)}, s32[4]{0:T(128)}, u32[]{:S(2)}) copy-start(s32[4]{0:T(128)} %listing_ref.1) | copy-start | bytes 52
  46.7 1.9 %collective-permute-start.17 = (bf16[64,768]{1,0:T(8,128)(2,1)S(1)}, bf16[64,768]{1,0:T(8,128)(2,1)S(1)}, u32[]{:S(2)}, u32[]{:S(2)}) collective-permute-start(bf16[64,768]{1,0:T(8,128)(2,1)S(1)} %get-tuple-element.54), channel_id=1, source_target_pairs={{0,8},{8,0},{16,24},{24,16},{1,9},{9,1},{17,25},{25,17},{2,10},{10... | collective-permute-start | bytes 294920 | tf_op jit(solution)/shard_map/ppermute | solution.py:462
  46.8 5.7 %collective-permute-start.18 = (bf16[64,768]{1,0:T(8,128)(2,1)S(1)}, bf16[64,768]{1,0:T(8,128)(2,1)S(1)}, u32[]{:S(2)}, u32[]{:S(2)}) collective-permute-start(bf16[64,768]{1,0:T(8,128)(2,1)S(1)} %get-tuple-element.55), channel_id=1, source_target_pairs={{0,16},{8,24},{16,0},{24,8},{1,17},{9,25},{17,1},{25,9},{2,18},{10... | collective-permute-start | bytes 294920 | tf_op jit(solution)/shard_map/ppermute | solution.py:462
  48.4 5.3 %collective-permute-start.19 = (bf16[64,768]{1,0:T(8,128)(2,1)S(1)}, bf16[64,768]{1,0:T(8,128)(2,1)S(1)}, u32[]{:S(2)}, u32[]{:S(2)}) collective-permute-start(bf16[64,768]{1,0:T(8,128)(2,1)S(1)} %get-tuple-element.56), channel_id=1, source_target_pairs={{0,24},{8,16},{16,8},{24,0},{1,25},{9,17},{17,9},{25,1},{2,26},{10... | collective-permute-start | bytes 294920 | tf_op jit(solution)/shard_map/ppermute | solution.py:462
  (3 other events, 14.6 us)

commit v5 on v4

--- a/solution.py
+++ b/solution.py
@@ -9,6 +9,8 @@
 from jax.sharding import PartitionSpec as P
 
 HEADS = 12
+AH = 0.1
+BH = 0.1
 HD = 64
 STEP_HEADS = 4
 STEP_COLS = STEP_HEADS * HD
@@ -412,35 +414,46 @@
 
 
 def arrange_kernel(groups, listing_ref, masked_ref, *refs):
-    piece_refs, out_ref = refs[:groups], refs[groups]
+    piece_refs, out_ref, sums_ref, sems = refs[:groups], refs[-3], refs[-2], refs[-1]
     piece = piece_refs[0].shape[0]
     own = lax.axis_index("group")
-    for r in range(groups):
-        place = piece_of(listing_ref, lax.bitwise_xor(own, jnp.int32(r)), groups)
-        here = pl.ds(pl.multiple_of(place * piece, piece), piece)
-        out_ref[here, :] = (
-            masked_ref[here, :].astype(jnp.float32) + piece_refs[r][...].astype(jnp.float32)
-        ).astype(jnp.bfloat16)
+    copies = []
+    for k in range(groups):
+        group = listing_ref[0:1, k : k + 1]
+        here = slice(k * piece, (k + 1) * piece)
+        back = piece_refs[0][...].astype(jnp.float32)
+        for r in range(1, groups):
+            mine = group == lax.bitwise_xor(own, jnp.int32(r))
+            back = jnp.where(mine, piece_refs[r][...].astype(jnp.float32), back)
+        sums_ref[here, :] = (masked_ref[here, :].astype(jnp.float32) + back).astype(jnp.bfloat16)
+        copies.append(pltpu.make_async_copy(sums_ref.at[here, :], out_ref.at[here, :], sems.at[k]))
+        copies[-1].start()
+    for copy in copies:
+        copy.wait()
 
 
 def arrange(packing_list, masked, pieces):
-    groups, (piece, width) = len(pieces), pieces[0].shape
+    groups = len(pieces)
     return pl.pallas_call(
         functools.partial(arrange_kernel, groups),
-        out_shape=jax.ShapeDtypeStruct((groups * piece, width), jnp.bfloat16),
-        in_specs=[smem()] + vmem(groups + 1),
-        out_specs=vmem(1)[0],
+        out_shape=jax.ShapeDtypeStruct(masked.shape, jnp.bfloat16),
+        in_specs=vmem(groups + 2),
+        out_specs=anywhere(1)[0],
+        scratch_shapes=[
+            pltpu.VMEM(masked.shape, jnp.bfloat16),
+            pltpu.SemaphoreType.DMA((groups,)),
+        ],
         compiler_params=params(),
-        cost_estimate=cost(1.3),
+        cost_estimate=cost(0.5),
         name="arrange",
-    )(packing_list, masked, *pieces)
+    )(packing_list.reshape(1, groups), masked, *pieces)
 
 
 def hold_kernel(*refs):
     pass
 
 
-def hold(members, *behind):
+def hold(members, *behind, us=0.1):
     count = len(members)
     return tuple(
         pl.pallas_call(
@@ -450,7 +463,7 @@
             out_specs=anywhere(count),
             input_output_aliases={i: i for i in range(count)},
             compiler_params=params(),
-            cost_estimate=cost(0.1),
+            cost_estimate=cost(us),
             name="hold",
         )(*members, *behind)
     )
@@ -497,8 +510,8 @@
     queries, state = own_call((a, b), own_layout, w_query, w_key, w_value, piece, rows)
     a_before, a_after, b_before, b_after = a, a, b, b
     for step in range(1, shards // 2):
-        a_before, a_after = hold((onto(a_before), back(a_after)))
-        b_before, b_after = hold((onto(b_before), back(b_after)), state)
+        a_before, a_after = hold((onto(a_before), back(a_after)), state, us=AH)
+        b_before, b_after = hold((onto(b_before), back(b_after)), us=BH)
         received = (a_before, b_before, a_after, b_after)
         state = chunk_call(queries, w_key, w_value, state, received, pair_layout, piece)
     far = (onto(a_before), back(b_after))

time: 55.2 us -> 53.7 us (0.973)
  waiting for transfers between devices: 15.2 us -> 13.1 us
  starting transfers between devices: 19.5 us -> 20.2 us
    ppermute x7, waiting for transfers between devices: 6.83 us -> 5.71 us  [back(): return lax.ppermute(member, 'ctx', backward)]
    ppermute x7, waiting for transfers between devices: 2.11 us -> 1.19 us  [onto(): return lax.ppermute(member, 'ctx', onward)]
  transfers between devices with their start and end apart: 20 -> 20, of which waited for: 10 -> 12; matrix products, arithmetic and copies ran while one was open for 0% -> 0% of each run, Pallas kernels for 24% -> 24%
where the time goes in v5:
time: 53.7 us; the launch traced here: 53.6 us
  starting transfers between devices  20.2 us (38%)
  Pallas kernels  19 us (35%)
  waiting for transfers between devices  13.1 us (24%)
  local copies, waits for them, and re-layouts  0.92 us (2%)
    ppermute x7, starting transfers between devices, onto(): return lax.ppermute(member, 'ctx', onward)  11.6 us
    pallas_call x3, Pallas kernels, chunk_call(): pl.pallas_call(functools.partial(chunk_kernel, piece, layout), out_shape=...  9.11 us
    ppermute x6, waiting for transfers between devices, exchange(): lax.ppermute(pieces[r], 'group', [(i, i ^ r) for i in range(groups)])  6.23 us
    ppermute x7, waiting for transfers between devices, back(): return lax.ppermute(member, 'ctx', backward)  5.71 us
    ppermute x6, starting transfers between devices, exchange(): lax.ppermute(pieces[r], 'group', [(i, i ^ r) for i in range(groups)])  5.09 us
    ppermute x7, starting transfers between devices, back(): return lax.ppermute(member, 'ctx', backward)  3.52 us
    pallas_call x1, Pallas kernels, own_call(): pl.pallas_call(functools.partial(own_kernel, piece, parts, borders_at), o...  2.71 us
    pallas_call x1, Pallas kernels, last_call(): pl.pallas_call(functools.partial(last_kernel, groups, piece, layout), out...  2.54 us
  transfers between devices with their start and end apart: 20, of which 12 were waited for; matrix products, arithmetic and copies ran while one was open for 0% of the time, Pallas kernels for 24%

profile of v5, /device:TPU:0, one launch (start us, length us, event | category | flops | bytes accessed | tf_op | source)
XLA Modules:
  0.0 53.6 jit_solution(798412015753702218)
XLA Ops:
  0.0 2.4 %route.1 = (bf16[72,768]{1,0:T(8,128)(2,1)}, bf16[64,768]{1,0:T(8,128)(2,1)}, bf16[64,768]{1,0:T(8,128)(2,1)}, bf16[64,768]{1,0:T(8,128)(2,1)}, bf16[256,768]{1,0:T(8,128)(2,1)}) custom-call(s32[4]{0:T(128)} %from_ref.1, bf16[256,768]{1,0:T(8,128)(2,1)} %series_ref.1, s32[2,128]{1,0:T(2,128)} %bitcast.3, bf16[768]{0:T(1024)(128)(2,1)} %token_ref.1, ...), custom_call_target="tpu_custom_call" | custom-call | flops 5500000256 | tf_op jit(solution)/shard_map/route/pallas_call | solution.py:105
  3.0 2.6 %collective-permute-start.1 = (bf16[64,768]{1,0:T(8,128)(2,1)}, bf16[64,768]{1,0:T(8,128)(2,1)S(1)}, u32[]{:S(2)}, u32[]{:S(2)}) collective-permute-start(bf16[64,768]{1,0:T(8,128)(2,1)} %get-tuple-element.34), channel_id=1, source_target_pairs={{0,16},{8,24},{16,0},{24,8},{1,17},{9,25},{17,1},{25,9},{2,18},{10... | collective-permute-start | bytes 294920 | tf_op jit(solution)/shard_map/ppermute | solution.py:475
  6.5 1.9 %collective-permute-start.3 = (bf16[136,768]{1,0:T(8,128)(2,1)S(1)}, bf16[136,768]{1,0:T(8,128)(2,1)S(1)}, u32[]{:S(2)}, u32[]{:S(2)}) collective-permute-start(bf16[136,768]{1,0:T(8,128)(2,1)S(1)} %join.2.refs_2_.refs_0_), channel_id=1, source_target_pairs={{0,2},{2,4},{4,6},{6,7},{7,5},{5,3},{3,1},{1,0},{8,10},{10,12},{12... | collective-permute-start | bytes 626696 | tf_op jit(solution)/shard_map/ppermute | solution.py:502
  8.6 1.1 %stage.1 = (bf16[768,768]{1,0:T(8,128)(2,1)S(1)}, bf16[768,768]{1,0:T(8,128)(2,1)S(1)}, bf16[768,768]{1,0:T(8,128)(2,1)S(1)}) custom-call(bf16[768,768]{1,0:T(8,128)(2,1)S(1)} %copy-done, bf16[768,768]{1,0:T(8,128)(2,1)S(1)} %copy-done.1, bf16[768,768]{1,0:T(8,128)(2,1)S(1)} %copy-done.2, bf16[72,768]{1,0:T(8,128)(2,1)S(1)} %copy-done.4), custom_call_target="tpu_custom_call" | custom-call | flops 550000 | tf_op jit(solution)/shard_map/stage/pallas_call | solution.py:159
  9.7 1.2 %collective-permute-done.2.refs_1_ = bf16[64,768]{1,0:T(8,128)(2,1)S(1)} collective-permute-done((bf16[64,768]{1,0:T(8,128)(2,1)}, bf16[64,768]{1,0:T(8,128)(2,1)S(1)}, u32[]{:S(2)}, u32[]{:S(2)}) %collective-permute-start.2) | collective-permute-done | bytes 98336 | tf_op jit(solution)/shard_map/ppermute | solution.py:475
  11.0 1.7 %collective-permute-start.5 = (bf16[128,768]{1,0:T(8,128)(2,1)S(1)}, bf16[128,768]{1,0:T(8,128)(2,1)S(1)}, u32[]{:S(2)}, u32[]{:S(2)}) collective-permute-start(bf16[128,768]{1,0:T(8,128)(2,1)S(1)} %join.3.refs_1_), channel_id=1, source_target_pairs={{0,2},{2,4},{4,6},{6,7},{7,5},{5,3},{3,1},{1,0},{8,10},{10,12},{12... | collective-permute-start | bytes 589832 | tf_op jit(solution)/shard_map/ppermute | solution.py:502
  13.1 2.7 %own_rows.1 = (bf16[12,128,256]{2,1,0:T(8,128)(2,1)S(1)}, f32[12,80,256]{2,1,0:T(8,128)S(1)}) custom-call(bf16[136,768]{1,0:T(8,128)(2,1)S(1)} %join.2.refs_2_.refs_0_, bf16[128,768]{1,0:T(8,128)(2,1)S(1)} %join.3.refs_1_, bf16[768,768]{1,0:T(8,128)(2,1)S(1)} %get-tuple-element.37.refs_2_, bf16[768,768]{1,0:T(8,128)(2,1)S(1)} %get-tuple-element.38.refs_3_.wk_ref, ...), custom_call_target="tpu_custom_call" | custom-call | flops 165000000 | tf_op jit(solution)/shard_map/own_rows/pallas_call | solution.py:375
  15.8 1.7 %collective-permute-start.7 = (bf16[136,768]{1,0:T(8,128)(2,1)S(1)}, bf16[136,768]{1,0:T(8,128)(2,1)S(1)}, u32[]{:S(2)}, u32[]{:S(2)}) collective-permute-start(bf16[136,768]{1,0:T(8,128)(2,1)S(1)} %get-tuple-element.41.rest_0_), channel_id=1, source_target_pairs={{0,2},{2,4},{4,6},{6,7},{7,5},{5,3},{3,1},{1,0},{8,10},{10,12},{12... | collective-permute-start | bytes 626696 | tf_op jit(solution)/shard_map/ppermute | solution.py:502
  18.3 1.5 %collective-permute-done.6.refs_1_ = bf16[128,768]{1,0:T(8,128)(2,1)S(1)} collective-permute-done((bf16[128,768]{1,0:T(8,128)(2,1)S(1)}, bf16[128,768]{1,0:T(8,128)(2,1)S(1)}, u32[]{:S(2)}, u32[]{:S(2)}) %collective-permute-start.6) | collective-permute-done | bytes 196640 | tf_op jit(solution)/shard_map/ppermute | solution.py:505
  19.8 1.6 %collective-permute-start.9 = (bf16[128,768]{1,0:T(8,128)(2,1)S(1)}, bf16[128,768]{1,0:T(8,128)(2,1)S(1)}, u32[]{:S(2)}, u32[]{:S(2)}) collective-permute-start(bf16[128,768]{1,0:T(8,128)(2,1)S(1)} %get-tuple-element.42.rest_1_), channel_id=1, source_target_pairs={{0,2},{2,4},{4,6},{6,7},{7,5},{5,3},{3,1},{1,0},{8,10},{10,12},{12... | collective-permute-start | bytes 589832 | tf_op jit(solution)/shard_map/ppermute | solution.py:502
  21.8 3.0 %received_rows.3.refs_2_.old_ref = f32[12,80,256]{2,1,0:T(8,128)S(1)} custom-call(bf16[12,128,256]{2,1,0:T(8,128)(2,1)S(1)} %get-tuple-element.39.queries_ref, bf16[768,768]{1,0:T(8,128)(2,1)S(1)} %get-tuple-element.38.refs_3_.wk_ref, bf16[768,768]{1,0:T(8,128)(2,1)S(1)} %get-tuple-element.36.refs_3_.refs_4_.wv_ref, ...), custom_call_target="tpu_custom_call" | custom-call | flops 192500000 | tf_op jit(solution)/shard_map/received_rows/pallas_call | solution.py:390
  25.4 1.6 %collective-permute-start.11 = (bf16[136,768]{1,0:T(8,128)(2,1)S(1)}, bf16[136,768]{1,0:T(8,128)(2,1)S(1)}, u32[]{:S(2)}, u32[]{:S(2)}) collective-permute-start(bf16[136,768]{1,0:T(8,128)(2,1)S(1)} %get-tuple-element.45.rest_0_), channel_id=1, source_target_pairs={{0,2},{2,4},{4,6},{6,7},{7,5},{5,3},{3,1},{1,0},{8,10},{10,12},{12... | collective-permute-start | bytes 626696 | tf_op jit(solution)/shard_map/ppermute | solution.py:502
  27.7 1.6 %collective-permute-done.10.refs_1_ = bf16[128,768]{1,0:T(8,128)(2,1)S(1)} collective-permute-done((bf16[128,768]{1,0:T(8,128)(2,1)S(1)}, bf16[128,768]{1,0:T(8,128)(2,1)S(1)}, u32[]{:S(2)}, u32[]{:S(2)}) %collective-permute-start.10) | collective-permute-done | bytes 196640 | tf_op jit(solution)/shard_map/ppermute | solution.py:505
  29.3 1.6 %collective-permute-start.13 = (bf16[128,768]{1,0:T(8,128)(2,1)S(1)}, bf16[128,768]{1,0:T(8,128)(2,1)S(1)}, u32[]{:S(2)}, u32[]{:S(2)}) collective-permute-start(bf16[128,768]{1,0:T(8,128)(2,1)S(1)} %get-tuple-element.46.rest_1_), channel_id=1, source_target_pairs={{0,2},{2,4},{4,6},{6,7},{7,5},{5,3},{3,1},{1,0},{8,10},{10,12},{12... | collective-permute-start | bytes 589832 | tf_op jit(solution)/shard_map/ppermute | solution.py:502
  31.3 3.0 %received_rows.4.refs_2_.old_ref = f32[12,80,256]{2,1,0:T(8,128)S(1)} custom-call(bf16[12,128,256]{2,1,0:T(8,128)(2,1)S(1)} %get-tuple-element.39.queries_ref, bf16[768,768]{1,0:T(8,128)(2,1)S(1)} %get-tuple-element.38.refs_3_.wk_ref, bf16[768,768]{1,0:T(8,128)(2,1)S(1)} %get-tuple-element.36.refs_3_.refs_4_.wv_ref, ...), custom_call_target="tpu_custom_call" | custom-call | flops 192500000 | tf_op jit(solution)/shard_map/received_rows/pallas_call | solution.py:390
  34.6 1.6 %collective-permute-start.15 = (bf16[136,768]{1,0:T(8,128)(2,1)S(1)}, bf16[136,768]{1,0:T(8,128)(2,1)S(1)}, u32[]{:S(2)}, u32[]{:S(2)}) collective-permute-start(bf16[136,768]{1,0:T(8,128)(2,1)S(1)} %get-tuple-element.49.rest_0_), channel_id=1, source_target_pairs={{0,2},{2,4},{4,6},{6,7},{7,5},{5,3},{3,1},{1,0},{8,10},{10,12},{12... | collective-permute-start | bytes 626696 | tf_op jit(solution)/shard_map/ppermute | solution.py:502
  37.2 1.2 %collective-permute-start.16 = (bf16[128,768]{1,0:T(8,128)(2,1)S(1)}, bf16[128,768]{1,0:T(8,128)(2,1)S(1)}, u32[]{:S(2)}, u32[]{:S(2)}) collective-permute-start(bf16[128,768]{1,0:T(8,128)(2,1)S(1)} %get-tuple-element.52.rest_3_), channel_id=1, source_target_pairs={{2,0},{4,2},{6,4},{7,6},{5,7},{3,5},{1,3},{0,1},{10,8},{12,10},{14... | collective-permute-start | bytes 589832 | tf_op jit(solution)/shard_map/ppermute | solution.py:505
  38.4 3.2 %received_rows.5.old_ref = f32[12,80,256]{2,1,0:T(8,128)S(1)} custom-call(bf16[12,128,256]{2,1,0:T(8,128)(2,1)S(1)} %get-tuple-element.39.queries_ref, bf16[768,768]{1,0:T(8,128)(2,1)S(1)} %get-tuple-element.38.refs_3_.wk_ref, bf16[768,768]{1,0:T(8,128)(2,1)S(1)} %get-tuple-element.36.refs_3_.refs_4_.wv_ref, ...), custom_call_target="tpu_custom_call" | custom-call | flops 192500000 | tf_op jit(solution)/shard_map/received_rows/pallas_call | solution.py:390
  41.6 1.3 %collective-permute-done.16.rest_1_ = bf16[128,768]{1,0:T(8,128)(2,1)S(1)} collective-permute-done((bf16[128,768]{1,0:T(8,128)(2,1)S(1)}, bf16[128,768]{1,0:T(8,128)(2,1)S(1)}, u32[]{:S(2)}, u32[]{:S(2)}) %collective-permute-start.16) | collective-permute-done | bytes 196640 | tf_op jit(solution)/shard_map/ppermute | solution.py:505
  42.9 2.5 %last_rows.1 = (bf16[64,768]{1,0:T(8,128)(2,1)S(1)}, bf16[64,768]{1,0:T(8,128)(2,1)S(1)}, bf16[64,768]{1,0:T(8,128)(2,1)S(1)}, bf16[64,768]{1,0:T(8,128)(2,1)S(1)}) custom-call(bf16[12,128,256]{2,1,0:T(8,128)(2,1)S(1)} %get-tuple-element.39.queries_ref, bf16[768,768]{1,0:T(8,128)(2,1)S(1)} %get-tuple-element.38.refs_3_.wk_ref, ...), custom_call_target="tpu_custom_call" | custom-call | flops 165000000 | tf_op jit(solution)/shard_map/last_rows/pallas_call | solution.py:404
  45.5 1.6 %collective-permute-start.18 = (bf16[64,768]{1,0:T(8,128)(2,1)S(1)}, bf16[64,768]{1,0:T(8,128)(2,1)S(1)}, u32[]{:S(2)}, u32[]{:S(2)}) collective-permute-start(bf16[64,768]{1,0:T(8,128)(2,1)S(1)} %get-tuple-element.55), channel_id=1, source_target_pairs={{0,16},{8,24},{16,0},{24,8},{1,17},{9,25},{17,1},{25,9},{2,18},{10... | collective-permute-start | bytes 294920 | tf_op jit(solution)/shard_map/ppermute | solution.py:475
  47.4 3.8 %collective-permute-done.18.refs_2_ = bf16[64,768]{1,0:T(8,128)(2,1)S(1)} collective-permute-done((bf16[64,768]{1,0:T(8,128)(2,1)S(1)}, bf16[64,768]{1,0:T(8,128)(2,1)S(1)}, u32[]{:S(2)}, u32[]{:S(2)}) %collective-permute-start.18) | collective-permute-done | bytes 98336 | tf_op jit(solution)/shard_map/ppermute | solution.py:475
  51.2 1.2 %collective-permute-done.19.refs_3_ = bf16[64,768]{1,0:T(8,128)(2,1)S(1)} collective-permute-done((bf16[64,768]{1,0:T(8,128)(2,1)S(1)}, bf16[64,768]{1,0:T(8,128)(2,1)S(1)}, u32[]{:S(2)}, u32[]{:S(2)}) %collective-permute-start.19) | collective-permute-done | bytes 98336 | tf_op jit(solution)/shard_map/ppermute | solution.py:475
  52.4 1.0 %arrange.1 = bf16[256,768]{1,0:T(8,128)(2,1)} custom-call(s32[1,4]{1,0:T(1,128)S(1)} %bitcast.2, bf16[256,768]{1,0:T(8,128)(2,1)S(1)} %copy-done.5, bf16[64,768]{1,0:T(8,128)(2,1)S(1)} %get-tuple-element.53.refs_0_, bf16[64,768]{1,0:T(8,128)(2,1)S(1)} %collective-permute-done.17.refs_1_, bf16[64,768]{1,0:T(8,128)(2,1)S(1)} %collective-permute-done.18.refs_2_, ...), custom_call_target="tpu_custom_call" | custom-call | flops 27500000 | tf_op jit(solution)/shard_map/arrange/pallas_call | solution.py:437
  (46 shorter events, 6.8 us)
Async XLA Ops:
  0.0 8.6 %copy-start.1 = (bf16[768,768]{1,0:T(8,128)(2,1)S(1)}, bf16[768,768]{1,0:T(8,128)(2,1)}, u32[]{:S(2)}) copy-start(bf16[768,768]{1,0:T(8,128)(2,1)} %refs_1_.1) | copy-start | bytes 3538948
  0.0 8.6 %copy-start.2 = (bf16[768,768]{1,0:T(8,128)(2,1)S(1)}, bf16[768,768]{1,0:T(8,128)(2,1)}, u32[]{:S(2)}) copy-start(bf16[768,768]{1,0:T(8,128)(2,1)} %refs_2_.1) | copy-start | bytes 3538948
  2.4 3.2 %collective-permute-start = (bf16[64,768]{1,0:T(8,128)(2,1)}, bf16[64,768]{1,0:T(8,128)(2,1)S(1)}, u32[]{:S(2)}, u32[]{:S(2)}) collective-permute-start(bf16[64,768]{1,0:T(8,128)(2,1)} %get-tuple-element.33), channel_id=1, source_target_pairs={{0,8},{8,0},{16,24},{24,16},{1,9},{9,1},{17,25},{25,17},{2,10},{10... | collective-permute-start | bytes 294920 | tf_op jit(solution)/shard_map/ppermute | solution.py:475
  3.0 6.8 %collective-permute-start.1 = (bf16[64,768]{1,0:T(8,128)(2,1)}, bf16[64,768]{1,0:T(8,128)(2,1)S(1)}, u32[]{:S(2)}, u32[]{:S(2)}) collective-permute-start(bf16[64,768]{1,0:T(8,128)(2,1)} %get-tuple-element.34), channel_id=1, source_target_pairs={{0,16},{8,24},{16,0},{24,8},{1,17},{9,25},{17,1},{25,9},{2,18},{10... | collective-permute-start | bytes 294920 | tf_op jit(solution)/shard_map/ppermute | solution.py:475
  5.5 5.4 %collective-permute-start.2 = (bf16[64,768]{1,0:T(8,128)(2,1)}, bf16[64,768]{1,0:T(8,128)(2,1)S(1)}, u32[]{:S(2)}, u32[]{:S(2)}) collective-permute-start(bf16[64,768]{1,0:T(8,128)(2,1)} %get-tuple-element.35), channel_id=1, source_target_pairs={{0,24},{8,16},{16,8},{24,0},{1,25},{9,17},{17,9},{25,1},{2,26},{10... | collective-permute-start | bytes 294920 | tf_op jit(solution)/shard_map/ppermute | solution.py:475
  6.5 9.3 %collective-permute-start.3 = (bf16[136,768]{1,0:T(8,128)(2,1)S(1)}, bf16[136,768]{1,0:T(8,128)(2,1)S(1)}, u32[]{:S(2)}, u32[]{:S(2)}) collective-permute-start(bf16[136,768]{1,0:T(8,128)(2,1)S(1)} %join.2.refs_2_.refs_0_), channel_id=1, source_target_pairs={{0,2},{2,4},{4,6},{6,7},{7,5},{5,3},{3,1},{1,0},{8,10},{10,12},{12... | collective-permute-start | bytes 626696 | tf_op jit(solution)/shard_map/ppermute | solution.py:502
  8.4 7.4 %collective-permute-start.4 = (bf16[136,768]{1,0:T(8,128)(2,1)S(1)}, bf16[136,768]{1,0:T(8,128)(2,1)S(1)}, u32[]{:S(2)}, u32[]{:S(2)}) collective-permute-start(bf16[136,768]{1,0:T(8,128)(2,1)S(1)} %join.2.refs_2_.refs_0_), channel_id=1, source_target_pairs={{2,0},{4,2},{6,4},{7,6},{5,7},{3,5},{1,3},{0,1},{10,8},{12,10},{14... | collective-permute-start | bytes 626696 | tf_op jit(solution)/shard_map/ppermute | solution.py:505
  11.0 7.3 %collective-permute-start.5 = (bf16[128,768]{1,0:T(8,128)(2,1)S(1)}, bf16[128,768]{1,0:T(8,128)(2,1)S(1)}, u32[]{:S(2)}, u32[]{:S(2)}) collective-permute-start(bf16[128,768]{1,0:T(8,128)(2,1)S(1)} %join.3.refs_1_), channel_id=1, source_target_pairs={{0,2},{2,4},{4,6},{6,7},{7,5},{5,3},{3,1},{1,0},{8,10},{10,12},{12... | collective-permute-start | bytes 589832 | tf_op jit(solution)/shard_map/ppermute | solution.py:502
  12.7 7.1 %collective-permute-start.6 = (bf16[128,768]{1,0:T(8,128)(2,1)S(1)}, bf16[128,768]{1,0:T(8,128)(2,1)S(1)}, u32[]{:S(2)}, u32[]{:S(2)}) collective-permute-start(bf16[128,768]{1,0:T(8,128)(2,1)S(1)} %join.3.refs_1_), channel_id=1, source_target_pairs={{2,0},{4,2},{6,4},{7,6},{5,7},{3,5},{1,3},{0,1},{10,8},{12,10},{14... | collective-permute-start | bytes 589832 | tf_op jit(solution)/shard_map/ppermute | solution.py:505
  15.8 9.0 %collective-permute-start.7 = (bf16[136,768]{1,0:T(8,128)(2,1)S(1)}, bf16[136,768]{1,0:T(8,128)(2,1)S(1)}, u32[]{:S(2)}, u32[]{:S(2)}) collective-permute-start(bf16[136,768]{1,0:T(8,128)(2,1)S(1)} %get-tuple-element.41.rest_0_), channel_id=1, source_target_pairs={{0,2},{2,4},{4,6},{6,7},{7,5},{5,3},{3,1},{1,0},{8,10},{10,12},{12... | collective-permute-start | bytes 626696 | tf_op jit(solution)/shard_map/ppermute | solution.py:502
  17.5 7.9 %collective-permute-start.8 = (bf16[136,768]{1,0:T(8,128)(2,1)S(1)}, bf16[136,768]{1,0:T(8,128)(2,1)S(1)}, u32[]{:S(2)}, u32[]{:S(2)}) collective-permute-start(bf16[136,768]{1,0:T(8,128)(2,1)S(1)} %get-tuple-element.43.rest_2_), channel_id=1, source_target_pairs={{2,0},{4,2},{6,4},{7,6},{5,7},{3,5},{1,3},{0,1},{10,8},{12,10},{14... | collective-permute-start | bytes 626696 | tf_op jit(solution)/shard_map/ppermute | solution.py:505
  19.8 7.9 %collective-permute-start.9 = (bf16[128,768]{1,0:T(8,128)(2,1)S(1)}, bf16[128,768]{1,0:T(8,128)(2,1)S(1)}, u32[]{:S(2)}, u32[]{:S(2)}) collective-permute-start(bf16[128,768]{1,0:T(8,128)(2,1)S(1)} %get-tuple-element.42.rest_1_), channel_id=1, source_target_pairs={{0,2},{2,4},{4,6},{6,7},{7,5},{5,3},{3,1},{1,0},{8,10},{10,12},{12... | collective-permute-start | bytes 589832 | tf_op jit(solution)/shard_map/ppermute | solution.py:502
  21.4 7.9 %collective-permute-start.10 = (bf16[128,768]{1,0:T(8,128)(2,1)S(1)}, bf16[128,768]{1,0:T(8,128)(2,1)S(1)}, u32[]{:S(2)}, u32[]{:S(2)}) collective-permute-start(bf16[128,768]{1,0:T(8,128)(2,1)S(1)} %get-tuple-element.44.rest_3_), channel_id=1, source_target_pairs={{2,0},{4,2},{6,4},{7,6},{5,7},{3,5},{1,3},{0,1},{10,8},{12,10},{14... | collective-permute-start | bytes 589832 | tf_op jit(solution)/shard_map/ppermute | solution.py:505
  25.4 8.9 %collective-permute-start.11 = (bf16[136,768]{1,0:T(8,128)(2,1)S(1)}, bf16[136,768]{1,0:T(8,128)(2,1)S(1)}, u32[]{:S(2)}, u32[]{:S(2)}) collective-permute-start(bf16[136,768]{1,0:T(8,128)(2,1)S(1)} %get-tuple-element.45.rest_0_), channel_id=1, source_target_pairs={{0,2},{2,4},{4,6},{6,7},{7,5},{5,3},{3,1},{1,0},{8,10},{10,12},{12... | collective-permute-start | bytes 626696 | tf_op jit(solution)/shard_map/ppermute | solution.py:502
  27.0 7.6 %collective-permute-start.12 = (bf16[136,768]{1,0:T(8,128)(2,1)S(1)}, bf16[136,768]{1,0:T(8,128)(2,1)S(1)}, u32[]{:S(2)}, u32[]{:S(2)}) collective-permute-start(bf16[136,768]{1,0:T(8,128)(2,1)S(1)} %get-tuple-element.47.rest_2_), channel_id=1, source_target_pairs={{2,0},{4,2},{6,4},{7,6},{5,7},{3,5},{1,3},{0,1},{10,8},{12,10},{14... | collective-permute-start | bytes 626696 | tf_op jit(solution)/shard_map/ppermute | solution.py:505
  29.3 7.5 %collective-permute-start.13 = (bf16[128,768]{1,0:T(8,128)(2,1)S(1)}, bf16[128,768]{1,0:T(8,128)(2,1)S(1)}, u32[]{:S(2)}, u32[]{:S(2)}) collective-permute-start(bf16[128,768]{1,0:T(8,128)(2,1)S(1)} %get-tuple-element.46.rest_1_), channel_id=1, source_target_pairs={{0,2},{2,4},{4,6},{6,7},{7,5},{5,3},{3,1},{1,0},{8,10},{10,12},{12... | collective-permute-start | bytes 589832 | tf_op jit(solution)/shard_map/ppermute | solution.py:502
  30.9 6.3 %collective-permute-start.14 = (bf16[128,768]{1,0:T(8,128)(2,1)S(1)}, bf16[128,768]{1,0:T(8,128)(2,1)S(1)}, u32[]{:S(2)}, u32[]{:S(2)}) collective-permute-start(bf16[128,768]{1,0:T(8,128)(2,1)S(1)} %get-tuple-element.48.rest_3_), channel_id=1, source_target_pairs={{2,0},{4,2},{6,4},{7,6},{5,7},{3,5},{1,3},{0,1},{10,8},{12,10},{14... | collective-permute-start | bytes 589832 | tf_op jit(solution)/shard_map/ppermute | solution.py:505
  34.6 8.3 %collective-permute-start.15 = (bf16[136,768]{1,0:T(8,128)(2,1)S(1)}, bf16[136,768]{1,0:T(8,128)(2,1)S(1)}, u32[]{:S(2)}, u32[]{:S(2)}) collective-permute-start(bf16[136,768]{1,0:T(8,128)(2,1)S(1)} %get-tuple-element.49.rest_0_), channel_id=1, source_target_pairs={{0,2},{2,4},{4,6},{6,7},{7,5},{5,3},{3,1},{1,0},{8,10},{10,12},{12... | collective-permute-start | bytes 626696 | tf_op jit(solution)/shard_map/ppermute | solution.py:502
  37.2 5.7 %collective-permute-start.16 = (bf16[128,768]{1,0:T(8,128)(2,1)S(1)}, bf16[128,768]{1,0:T(8,128)(2,1)S(1)}, u32[]{:S(2)}, u32[]{:S(2)}) collective-permute-start(bf16[128,768]{1,0:T(8,128)(2,1)S(1)} %get-tuple-element.52.rest_3_), channel_id=1, source_target_pairs={{2,0},{4,2},{6,4},{7,6},{5,7},{3,5},{1,3},{0,1},{10,8},{12,10},{14... | collective-permute-start | bytes 589832 | tf_op jit(solution)/shard_map/ppermute | solution.py:505
  41.6 10.8 %copy-start.5 = (bf16[256,768]{1,0:T(8,128)(2,1)S(1)}, bf16[256,768]{1,0:T(8,128)(2,1)}, u32[]{:S(2)}) copy-start(bf16[256,768]{1,0:T(8,128)(2,1)} %get-tuple-element.31.masked_ref) | copy-start | bytes 1179652
  41.6 10.8 %copy-start.6 = (s32[4]{0:T(128)S(1)}, s32[4]{0:T(128)}, u32[]{:S(2)}) copy-start(s32[4]{0:T(128)} %from_ref.1) | copy-start | bytes 52
  45.4 1.9 %collective-permute-start.17 = (bf16[64,768]{1,0:T(8,128)(2,1)S(1)}, bf16[64,768]{1,0:T(8,128)(2,1)S(1)}, u32[]{:S(2)}, u32[]{:S(2)}) collective-permute-start(bf16[64,768]{1,0:T(8,128)(2,1)S(1)} %get-tuple-element.54), channel_id=1, source_target_pairs={{0,8},{8,0},{16,24},{24,16},{1,9},{9,1},{17,25},{25,17},{2,10},{10... | collective-permute-start | bytes 294920 | tf_op jit(solution)/shard_map/ppermute | solution.py:475
  45.5 5.7 %collective-permute-start.18 = (bf16[64,768]{1,0:T(8,128)(2,1)S(1)}, bf16[64,768]{1,0:T(8,128)(2,1)S(1)}, u32[]{:S(2)}, u32[]{:S(2)}) collective-permute-start(bf16[64,768]{1,0:T(8,128)(2,1)S(1)} %get-tuple-element.55), channel_id=1, source_target_pairs={{0,16},{8,24},{16,0},{24,8},{1,17},{9,25},{17,1},{25,9},{2,18},{10... | collective-permute-start | bytes 294920 | tf_op jit(solution)/shard_map/ppermute | solution.py:475
  47.1 5.3 %collective-permute-start.19 = (bf16[64,768]{1,0:T(8,128)(2,1)S(1)}, bf16[64,768]{1,0:T(8,128)(2,1)S(1)}, u32[]{:S(2)}, u32[]{:S(2)}) collective-permute-start(bf16[64,768]{1,0:T(8,128)(2,1)S(1)} %get-tuple-element.56), channel_id=1, source_target_pairs={{0,24},{8,16},{16,8},{24,0},{1,25},{9,17},{17,9},{25,1},{2,26},{10... | collective-permute-start | bytes 294920 | tf_op jit(solution)/shard_map/ppermute | solution.py:475
  (3 other events, 14.0 us)

commit v6 on v5

--- a/solution.py
+++ b/solution.py
@@ -54,11 +54,45 @@
     return place
 
 
+def fill_masked(mask_ref, token_ref, series_ref, masked_ref):
+    width = series_ref.shape[1]
+    token = token_ref[...].reshape(1, width)
+    for part in range(mask_ref.shape[0]):
+        line = mask_ref[part : part + 1, :].astype(jnp.float32)
+        hidden = jnp.broadcast_to(line, (128, 128)).T > 0.5
+        here = slice(part * 128, (part + 1) * 128)
+        for lane in range(0, width, 128):
+            masked_ref[here, lane : lane + 128] = jnp.where(
+                hidden,
+                token[:, lane : lane + 128].astype(jnp.float32),
+                series_ref[here, lane : lane + 128].astype(jnp.float32),
+            ).astype(jnp.bfloat16)
+
+
+def masked_kernel(mask_ref, token_ref, series_ref, behind_ref, masked_ref):
+    fill_masked(mask_ref, token_ref, series_ref, masked_ref)
+
+
+def masked_rows(series, recon_mask, mask_token, behind):
+    rows = series.shape[0]
+    return pl.pallas_call(
+        masked_kernel,
+        out_shape=jax.ShapeDtypeStruct(series.shape, jnp.bfloat16),
+        in_specs=vmem(3) + anywhere(1),
+        out_specs=vmem(1)[0],
+        compiler_params=params(),
+        cost_estimate=cost(0.1),
+        name="masked_rows",
+    )(recon_mask.reshape(rows // 128, 128), mask_token, series, behind)
+
+
 def route_kernel(
     groups, from_ref, series_ref, mask_ref, token_ref, gain_ref, docs_ref, *rest
 ):
-    out_refs, masked_ref = rest[:groups], rest[groups]
-    listing_ref, held_ref, lines_ref, word_ref, scale_ref, numbers_ref, sems = rest[groups + 1 :]
+    out_refs = rest[:groups]
+    listing_ref, held_ref, lines_ref, word_ref, scale_ref, numbers_ref, masked_ref, sems = rest[
+        groups:
+    ]
     rows, width = series_ref.shape
     piece = rows // groups
     own = lax.axis_index("group")
@@ -74,17 +108,7 @@
         copy.start()
     for copy in copies:
         copy.wait()
-    token = word_ref[...].reshape(1, width)
-    for part in range(lines_ref.shape[0]):
-        line = lines_ref[part : part + 1, :].astype(jnp.float32)
-        hidden = jnp.broadcast_to(line, (128, 128)).T > 0.5
-        here = slice(part * 128, (part + 1) * 128)
-        for lane in range(0, width, 128):
-            masked_ref[here, lane : lane + 128] = jnp.where(
-                hidden,
-                token[:, lane : lane + 128].astype(jnp.float32),
-                held_ref[here, lane : lane + 128].astype(jnp.float32),
-            ).astype(jnp.bfloat16)
+    fill_masked(lines_ref, word_ref, held_ref, masked_ref)
     gain = scale_ref[...].astype(jnp.float32).reshape(1, width)
     for r in range(groups):
         place = piece_of(listing_ref, lax.bitwise_xor(own, jnp.int32(r)), groups)
@@ -102,15 +126,14 @@
 def route(packing_list, series, recon_mask, mask_token, norm_gain, doc_ids, groups):
     rows, width = series.shape
     piece = rows // groups
-    *pieces, masked = pl.pallas_call(
+    return pl.pallas_call(
         functools.partial(route_kernel, groups),
         out_shape=[
             jax.ShapeDtypeStruct((piece + 8 if r == 0 else piece, width), jnp.bfloat16)
             for r in range(groups)
-        ]
-        + [jax.ShapeDtypeStruct((rows, width), jnp.bfloat16)],
+        ],
         in_specs=anywhere(6),
-        out_specs=vmem(groups + 1),
+        out_specs=vmem(groups),
         scratch_shapes=[
             pltpu.SMEM((groups,), jnp.int32),
             pltpu.VMEM((rows, width), jnp.bfloat16),
@@ -118,6 +141,7 @@
             pltpu.VMEM((width,), jnp.bfloat16),
             pltpu.VMEM((width,), jnp.bfloat16),
             pltpu.VMEM(doc_ids.shape, jnp.int32),
+            pltpu.VMEM((rows, width), jnp.bfloat16),
             pltpu.SemaphoreType.DMA((6,)),
         ],
         compiler_params=params(LARGE),
@@ -131,7 +155,6 @@
         norm_gain,
         doc_ids,
     )
-    return pieces, masked
 
 
 def stage_kernel(count, turned, *refs):
@@ -195,8 +218,7 @@
 def places_of(count, piece, shape, axis):
     own = lax.axis_index("group")
     held = lax.broadcasted_iota(jnp.int32, shape, axis)
-    source = lax.bitwise_xor(held // piece, own)
-    return (source * piece + held % piece).astype(jnp.float32)
+    return lax.bitwise_xor(held, own * piece).astype(jnp.float32)
 
 
 def doc_numbers(borders, place):
@@ -208,7 +230,7 @@
 
 def key_extras(borders, rows, piece):
     docs = doc_numbers(borders, places_of(rows, piece, (rows, 128), 0))
-    column = lax.rem(lax.broadcasted_iota(jnp.int32, (rows, 128), 1), HD)
+    column = lax.bitwise_and(lax.broadcasted_iota(jnp.int32, (rows, 128), 1), HD - 1)
     named = jnp.where(docs == column.astype(jnp.float32), 1.0, 0.0)
     flags = jnp.where(column < 7, 1.0, 0.0)
     return jnp.where(column < 4, named, flags).astype(jnp.bfloat16)
@@ -488,7 +510,7 @@
     backward = [(there, here) for here, there in onward]
 
     half = rows // 2
-    sent, masked = route(
+    sent = route(
         packing_list, series, recon_mask, mask_token, norm_gain, doc_ids, groups
     )
     w_query, w_key, w_value = stage((w_query, w_key, w_value), 2, sent[0], 0.01)
@@ -496,7 +518,8 @@
     low = groups // 2
     spans = [(r, 0, piece) for r in range(low)]
     a = join(pieces[:low], spans + [(0, piece, 8)])
-    b = join(pieces[low:], spans, (a, w_value))
+    masked = masked_rows(series, recon_mask, mask_token, w_value)
+    b = join(pieces[low:], spans, (a, w_value, masked))
 
     def onto(member):
         return lax.ppermute(member, "ctx", onward)

time: 53.7 us -> 53.6 us (level)
  transfers between devices with their start and end apart: 20 -> 20, of which waited for: 12 -> 12; matrix products, arithmetic and copies ran while one was open for 0% -> 0% of each run, Pallas kernels for 24% -> 25%
where the time goes in v6:
time: 53.6 us; the launch traced here: 53.5 us
  starting transfers between devices  20.3 us (38%)
  Pallas kernels  19 us (35%)
  waiting for transfers between devices  12.9 us (24%)
  local copies, waits for them, and re-layouts  0.94 us (2%)
    ppermute x7, starting transfers between devices, onto(): return lax.ppermute(member, 'ctx', onward)  11.6 us
    pallas_call x3, Pallas kernels, chunk_call(): pl.pallas_call(functools.partial(chunk_kernel, piece, layout), out_shape=...  9.11 us
    ppermute x6, waiting for transfers between devices, exchange(): lax.ppermute(pieces[r], 'group', [(i, i ^ r) for i in range(groups)])  6 us
    ppermute x7, waiting for transfers between devices, back(): return lax.ppermute(member, 'ctx', backward)  5.72 us
    ppermute x6, starting transfers between devices, exchange(): lax.ppermute(pieces[r], 'group', [(i, i ^ r) for i in range(groups)])  5.09 us
    ppermute x7, starting transfers between devices, back(): return lax.ppermute(member, 'ctx', backward)  3.52 us
    pallas_call x1, Pallas kernels, own_call(): pl.pallas_call(functools.partial(own_kernel, piece, parts, borders_at), o...  2.71 us
    pallas_call x1, Pallas kernels, last_call(): pl.pallas_call(functools.partial(last_kernel, groups, piece, layout), out...  2.54 us
  transfers between devices with their start and end apart: 20, of which 12 were waited for; matrix products, arithmetic and copies ran while one was open for 0% of the time, Pallas kernels for 25%

profile of v6, /device:TPU:0, one launch (start us, length us, event | category | flops | bytes accessed | tf_op | source)
XLA Modules:
  0.0 53.5 jit_solution(15626464178839471381)
XLA Ops:
  0.0 2.3 %route.1 = (bf16[72,768]{1,0:T(8,128)(2,1)}, bf16[64,768]{1,0:T(8,128)(2,1)}, bf16[64,768]{1,0:T(8,128)(2,1)}, bf16[64,768]{1,0:T(8,128)(2,1)}) custom-call(s32[4]{0:T(128)} %from_ref.1, bf16[256,768]{1,0:T(8,128)(2,1)} %series_ref.3, s32[2,128]{1,0:T(2,128)} %bitcast.2, bf16[768]{0:T(1024)(128)(2,1)} %token_ref.3, bf16[768]{0:T(1024)(128)(2,1)} %gain_ref.1, ...), custom_call_target="tpu_custom_call" | custom-call | flops 5500000256 | tf_op jit(solution)/shard_map/route/pallas_call | solution.py:129
  2.8 2.6 %collective-permute-start.1 = (bf16[64,768]{1,0:T(8,128)(2,1)}, bf16[64,768]{1,0:T(8,128)(2,1)S(1)}, u32[]{:S(2)}, u32[]{:S(2)}) collective-permute-start(bf16[64,768]{1,0:T(8,128)(2,1)} %get-tuple-element.33), channel_id=1, source_target_pairs={{0,16},{8,24},{16,0},{24,8},{1,17},{9,25},{17,1},{25,9},{2,18},{10... | collective-permute-start | bytes 294920 | tf_op jit(solution)/shard_map/ppermute | solution.py:497
  6.4 1.9 %collective-permute-start.3 = (bf16[136,768]{1,0:T(8,128)(2,1)S(1)}, bf16[136,768]{1,0:T(8,128)(2,1)S(1)}, u32[]{:S(2)}, u32[]{:S(2)}) collective-permute-start(bf16[136,768]{1,0:T(8,128)(2,1)S(1)} %join.2.refs_2_.refs_0_), channel_id=1, source_target_pairs={{0,2},{2,4},{4,6},{6,7},{7,5},{5,3},{3,1},{1,0},{8,10},{10,12},{12... | collective-permute-start | bytes 626696 | tf_op jit(solution)/shard_map/ppermute | solution.py:525
  8.5 1.1 %stage.1 = (bf16[768,768]{1,0:T(8,128)(2,1)S(1)}, bf16[768,768]{1,0:T(8,128)(2,1)S(1)}, bf16[768,768]{1,0:T(8,128)(2,1)S(1)}) custom-call(bf16[768,768]{1,0:T(8,128)(2,1)S(1)} %copy-done, bf16[768,768]{1,0:T(8,128)(2,1)S(1)} %copy-done.1, bf16[768,768]{1,0:T(8,128)(2,1)S(1)} %copy-done.2, bf16[72,768]{1,0:T(8,128)(2,1)S(1)} %copy-done.4), custom_call_target="tpu_custom_call" | custom-call | flops 550000 | tf_op jit(solution)/shard_map/stage/pallas_call | solution.py:182
  9.8 1.0 %collective-permute-done.2.refs_1_ = bf16[64,768]{1,0:T(8,128)(2,1)S(1)} collective-permute-done((bf16[64,768]{1,0:T(8,128)(2,1)}, bf16[64,768]{1,0:T(8,128)(2,1)S(1)}, u32[]{:S(2)}, u32[]{:S(2)}) %collective-permute-start.2) | collective-permute-done | bytes 98336 | tf_op jit(solution)/shard_map/ppermute | solution.py:497
  10.9 1.7 %collective-permute-start.5 = (bf16[128,768]{1,0:T(8,128)(2,1)S(1)}, bf16[128,768]{1,0:T(8,128)(2,1)S(1)}, u32[]{:S(2)}, u32[]{:S(2)}) collective-permute-start(bf16[128,768]{1,0:T(8,128)(2,1)S(1)} %join.3.refs_1_), channel_id=1, source_target_pairs={{0,2},{2,4},{4,6},{6,7},{7,5},{5,3},{3,1},{1,0},{8,10},{10,12},{12... | collective-permute-start | bytes 589832 | tf_op jit(solution)/shard_map/ppermute | solution.py:525
  13.0 2.7 %own_rows.1 = (bf16[12,128,256]{2,1,0:T(8,128)(2,1)S(1)}, f32[12,80,256]{2,1,0:T(8,128)S(1)}) custom-call(bf16[136,768]{1,0:T(8,128)(2,1)S(1)} %join.2.refs_2_.refs_0_, bf16[128,768]{1,0:T(8,128)(2,1)S(1)} %join.3.refs_1_, bf16[768,768]{1,0:T(8,128)(2,1)S(1)} %get-tuple-element.35.refs_2_, bf16[768,768]{1,0:T(8,128)(2,1)S(1)} %get-tuple-element.36.refs_3_.wk_ref, ...), custom_call_target="tpu_custom_call" | custom-call | flops 165000000 | tf_op jit(solution)/shard_map/own_rows/pallas_call | solution.py:397
  15.7 1.7 %collective-permute-start.7 = (bf16[136,768]{1,0:T(8,128)(2,1)S(1)}, bf16[136,768]{1,0:T(8,128)(2,1)S(1)}, u32[]{:S(2)}, u32[]{:S(2)}) collective-permute-start(bf16[136,768]{1,0:T(8,128)(2,1)S(1)} %get-tuple-element.39.rest_0_), channel_id=1, source_target_pairs={{0,2},{2,4},{4,6},{6,7},{7,5},{5,3},{3,1},{1,0},{8,10},{10,12},{12... | collective-permute-start | bytes 626696 | tf_op jit(solution)/shard_map/ppermute | solution.py:525
  18.1 1.5 %collective-permute-done.6.refs_1_ = bf16[128,768]{1,0:T(8,128)(2,1)S(1)} collective-permute-done((bf16[128,768]{1,0:T(8,128)(2,1)S(1)}, bf16[128,768]{1,0:T(8,128)(2,1)S(1)}, u32[]{:S(2)}, u32[]{:S(2)}) %collective-permute-start.6) | collective-permute-done | bytes 196640 | tf_op jit(solution)/shard_map/ppermute | solution.py:528
  19.7 1.6 %collective-permute-start.9 = (bf16[128,768]{1,0:T(8,128)(2,1)S(1)}, bf16[128,768]{1,0:T(8,128)(2,1)S(1)}, u32[]{:S(2)}, u32[]{:S(2)}) collective-permute-start(bf16[128,768]{1,0:T(8,128)(2,1)S(1)} %get-tuple-element.40.rest_1_), channel_id=1, source_target_pairs={{0,2},{2,4},{4,6},{6,7},{7,5},{5,3},{3,1},{1,0},{8,10},{10,12},{12... | collective-permute-start | bytes 589832 | tf_op jit(solution)/shard_map/ppermute | solution.py:525
  21.7 3.0 %received_rows.3.refs_2_.old_ref = f32[12,80,256]{2,1,0:T(8,128)S(1)} custom-call(bf16[12,128,256]{2,1,0:T(8,128)(2,1)S(1)} %get-tuple-element.37.queries_ref, bf16[768,768]{1,0:T(8,128)(2,1)S(1)} %get-tuple-element.36.refs_3_.wk_ref, bf16[768,768]{1,0:T(8,128)(2,1)S(1)} %get-tuple-element.31.behind_ref.refs_3_.refs_4_.wv_ref, ...), custom_call_target="tpu_custom_call" | custom-call | flops 192500000 | tf_op jit(solution)/shard_map/received_rows/pallas_call | solution.py:412
  25.3 1.6 %collective-permute-start.11 = (bf16[136,768]{1,0:T(8,128)(2,1)S(1)}, bf16[136,768]{1,0:T(8,128)(2,1)S(1)}, u32[]{:S(2)}, u32[]{:S(2)}) collective-permute-start(bf16[136,768]{1,0:T(8,128)(2,1)S(1)} %get-tuple-element.43.rest_0_), channel_id=1, source_target_pairs={{0,2},{2,4},{4,6},{6,7},{7,5},{5,3},{3,1},{1,0},{8,10},{10,12},{12... | collective-permute-start | bytes 626696 | tf_op jit(solution)/shard_map/ppermute | solution.py:525
  27.6 1.6 %collective-permute-done.10.refs_1_ = bf16[128,768]{1,0:T(8,128)(2,1)S(1)} collective-permute-done((bf16[128,768]{1,0:T(8,128)(2,1)S(1)}, bf16[128,768]{1,0:T(8,128)(2,1)S(1)}, u32[]{:S(2)}, u32[]{:S(2)}) %collective-permute-start.10) | collective-permute-done | bytes 196640 | tf_op jit(solution)/shard_map/ppermute | solution.py:528
  29.2 1.6 %collective-permute-start.13 = (bf16[128,768]{1,0:T(8,128)(2,1)S(1)}, bf16[128,768]{1,0:T(8,128)(2,1)S(1)}, u32[]{:S(2)}, u32[]{:S(2)}) collective-permute-start(bf16[128,768]{1,0:T(8,128)(2,1)S(1)} %get-tuple-element.44.rest_1_), channel_id=1, source_target_pairs={{0,2},{2,4},{4,6},{6,7},{7,5},{5,3},{3,1},{1,0},{8,10},{10,12},{12... | collective-permute-start | bytes 589832 | tf_op jit(solution)/shard_map/ppermute | solution.py:525
  31.2 3.0 %received_rows.4.refs_2_.old_ref = f32[12,80,256]{2,1,0:T(8,128)S(1)} custom-call(bf16[12,128,256]{2,1,0:T(8,128)(2,1)S(1)} %get-tuple-element.37.queries_ref, bf16[768,768]{1,0:T(8,128)(2,1)S(1)} %get-tuple-element.36.refs_3_.wk_ref, bf16[768,768]{1,0:T(8,128)(2,1)S(1)} %get-tuple-element.31.behind_ref.refs_3_.refs_4_.wv_ref, ...), custom_call_target="tpu_custom_call" | custom-call | flops 192500000 | tf_op jit(solution)/shard_map/received_rows/pallas_call | solution.py:412
  34.5 1.6 %collective-permute-start.15 = (bf16[136,768]{1,0:T(8,128)(2,1)S(1)}, bf16[136,768]{1,0:T(8,128)(2,1)S(1)}, u32[]{:S(2)}, u32[]{:S(2)}) collective-permute-start(bf16[136,768]{1,0:T(8,128)(2,1)S(1)} %get-tuple-element.47.rest_0_), channel_id=1, source_target_pairs={{0,2},{2,4},{4,6},{6,7},{7,5},{5,3},{3,1},{1,0},{8,10},{10,12},{12... | collective-permute-start | bytes 626696 | tf_op jit(solution)/shard_map/ppermute | solution.py:525
  37.1 1.2 %collective-permute-start.16 = (bf16[128,768]{1,0:T(8,128)(2,1)S(1)}, bf16[128,768]{1,0:T(8,128)(2,1)S(1)}, u32[]{:S(2)}, u32[]{:S(2)}) collective-permute-start(bf16[128,768]{1,0:T(8,128)(2,1)S(1)} %get-tuple-element.50.rest_3_), channel_id=1, source_target_pairs={{2,0},{4,2},{6,4},{7,6},{5,7},{3,5},{1,3},{0,1},{10,8},{12,10},{14... | collective-permute-start | bytes 589832 | tf_op jit(solution)/shard_map/ppermute | solution.py:528
  38.3 3.2 %received_rows.5.old_ref = f32[12,80,256]{2,1,0:T(8,128)S(1)} custom-call(bf16[12,128,256]{2,1,0:T(8,128)(2,1)S(1)} %get-tuple-element.37.queries_ref, bf16[768,768]{1,0:T(8,128)(2,1)S(1)} %get-tuple-element.36.refs_3_.wk_ref, bf16[768,768]{1,0:T(8,128)(2,1)S(1)} %get-tuple-element.31.behind_ref.refs_3_.refs_4_.wv_ref, ...), custom_call_target="tpu_custom_call" | custom-call | flops 192500000 | tf_op jit(solution)/shard_map/received_rows/pallas_call | solution.py:412
  41.5 1.3 %collective-permute-done.16.rest_1_ = bf16[128,768]{1,0:T(8,128)(2,1)S(1)} collective-permute-done((bf16[128,768]{1,0:T(8,128)(2,1)S(1)}, bf16[128,768]{1,0:T(8,128)(2,1)S(1)}, u32[]{:S(2)}, u32[]{:S(2)}) %collective-permute-start.16) | collective-permute-done | bytes 196640 | tf_op jit(solution)/shard_map/ppermute | solution.py:528
  42.8 2.5 %last_rows.1 = (bf16[64,768]{1,0:T(8,128)(2,1)S(1)}, bf16[64,768]{1,0:T(8,128)(2,1)S(1)}, bf16[64,768]{1,0:T(8,128)(2,1)S(1)}, bf16[64,768]{1,0:T(8,128)(2,1)S(1)}) custom-call(bf16[12,128,256]{2,1,0:T(8,128)(2,1)S(1)} %get-tuple-element.37.queries_ref, bf16[768,768]{1,0:T(8,128)(2,1)S(1)} %get-tuple-element.36.refs_3_.wk_ref, ...), custom_call_target="tpu_custom_call" | custom-call | flops 165000000 | tf_op jit(solution)/shard_map/last_rows/pallas_call | solution.py:426
  45.4 1.6 %collective-permute-start.18 = (bf16[64,768]{1,0:T(8,128)(2,1)S(1)}, bf16[64,768]{1,0:T(8,128)(2,1)S(1)}, u32[]{:S(2)}, u32[]{:S(2)}) collective-permute-start(bf16[64,768]{1,0:T(8,128)(2,1)S(1)} %get-tuple-element.53), channel_id=1, source_target_pairs={{0,16},{8,24},{16,0},{24,8},{1,17},{9,25},{17,1},{25,9},{2,18},{10... | collective-permute-start | bytes 294920 | tf_op jit(solution)/shard_map/ppermute | solution.py:497
  47.3 3.8 %collective-permute-done.18.refs_2_ = bf16[64,768]{1,0:T(8,128)(2,1)S(1)} collective-permute-done((bf16[64,768]{1,0:T(8,128)(2,1)S(1)}, bf16[64,768]{1,0:T(8,128)(2,1)S(1)}, u32[]{:S(2)}, u32[]{:S(2)}) %collective-permute-start.18) | collective-permute-done | bytes 98336 | tf_op jit(solution)/shard_map/ppermute | solution.py:497
  51.1 1.2 %collective-permute-done.19.refs_3_ = bf16[64,768]{1,0:T(8,128)(2,1)S(1)} collective-permute-done((bf16[64,768]{1,0:T(8,128)(2,1)S(1)}, bf16[64,768]{1,0:T(8,128)(2,1)S(1)}, u32[]{:S(2)}, u32[]{:S(2)}) %collective-permute-start.19) | collective-permute-done | bytes 98336 | tf_op jit(solution)/shard_map/ppermute | solution.py:497
  52.3 1.0 %arrange.1 = bf16[256,768]{1,0:T(8,128)(2,1)} custom-call(s32[1,4]{1,0:T(1,128)S(1)} %bitcast.4, bf16[256,768]{1,0:T(8,128)(2,1)S(1)} %masked_rows.1.refs_4_.masked_ref, bf16[64,768]{1,0:T(8,128)(2,1)S(1)} %get-tuple-element.51.refs_0_, bf16[64,768]{1,0:T(8,128)(2,1)S(1)} %collective-permute-done.17.refs_1_, ...), custom_call_target="tpu_custom_call" | custom-call | flops 27500000 | tf_op jit(solution)/shard_map/arrange/pallas_call | solution.py:459
  (51 shorter events, 6.9 us)
Async XLA Ops:
  0.0 8.5 %copy-start = (bf16[768,768]{1,0:T(8,128)(2,1)S(1)}, bf16[768,768]{1,0:T(8,128)(2,1)}, u32[]{:S(2)}) copy-start(bf16[768,768]{1,0:T(8,128)(2,1)} %refs_0_.1) | copy-start | bytes 3538948
  0.0 8.5 %copy-start.1 = (bf16[768,768]{1,0:T(8,128)(2,1)S(1)}, bf16[768,768]{1,0:T(8,128)(2,1)}, u32[]{:S(2)}) copy-start(bf16[768,768]{1,0:T(8,128)(2,1)} %refs_1_.1) | copy-start | bytes 3538948
  0.0 8.5 %copy-start.2 = (bf16[768,768]{1,0:T(8,128)(2,1)S(1)}, bf16[768,768]{1,0:T(8,128)(2,1)}, u32[]{:S(2)}) copy-start(bf16[768,768]{1,0:T(8,128)(2,1)} %refs_2_.1) | copy-start | bytes 3538948
  2.3 3.2 %collective-permute-start = (bf16[64,768]{1,0:T(8,128)(2,1)}, bf16[64,768]{1,0:T(8,128)(2,1)S(1)}, u32[]{:S(2)}, u32[]{:S(2)}) collective-permute-start(bf16[64,768]{1,0:T(8,128)(2,1)} %get-tuple-element.32), channel_id=1, source_target_pairs={{0,8},{8,0},{16,24},{24,16},{1,9},{9,1},{17,25},{25,17},{2,10},{10... | collective-permute-start | bytes 294920 | tf_op jit(solution)/shard_map/ppermute | solution.py:497
  2.8 7.0 %collective-permute-start.1 = (bf16[64,768]{1,0:T(8,128)(2,1)}, bf16[64,768]{1,0:T(8,128)(2,1)S(1)}, u32[]{:S(2)}, u32[]{:S(2)}) collective-permute-start(bf16[64,768]{1,0:T(8,128)(2,1)} %get-tuple-element.33), channel_id=1, source_target_pairs={{0,16},{8,24},{16,0},{24,8},{1,17},{9,25},{17,1},{25,9},{2,18},{10... | collective-permute-start | bytes 294920 | tf_op jit(solution)/shard_map/ppermute | solution.py:497
  5.4 5.4 %collective-permute-start.2 = (bf16[64,768]{1,0:T(8,128)(2,1)}, bf16[64,768]{1,0:T(8,128)(2,1)S(1)}, u32[]{:S(2)}, u32[]{:S(2)}) collective-permute-start(bf16[64,768]{1,0:T(8,128)(2,1)} %get-tuple-element.34), channel_id=1, source_target_pairs={{0,24},{8,16},{16,8},{24,0},{1,25},{9,17},{17,9},{25,1},{2,26},{10... | collective-permute-start | bytes 294920 | tf_op jit(solution)/shard_map/ppermute | solution.py:497
  6.4 9.2 %collective-permute-start.3 = (bf16[136,768]{1,0:T(8,128)(2,1)S(1)}, bf16[136,768]{1,0:T(8,128)(2,1)S(1)}, u32[]{:S(2)}, u32[]{:S(2)}) collective-permute-start(bf16[136,768]{1,0:T(8,128)(2,1)S(1)} %join.2.refs_2_.refs_0_), channel_id=1, source_target_pairs={{0,2},{2,4},{4,6},{6,7},{7,5},{5,3},{3,1},{1,0},{8,10},{10,12},{12... | collective-permute-start | bytes 626696 | tf_op jit(solution)/shard_map/ppermute | solution.py:525
  8.3 7.4 %collective-permute-start.4 = (bf16[136,768]{1,0:T(8,128)(2,1)S(1)}, bf16[136,768]{1,0:T(8,128)(2,1)S(1)}, u32[]{:S(2)}, u32[]{:S(2)}) collective-permute-start(bf16[136,768]{1,0:T(8,128)(2,1)S(1)} %join.2.refs_2_.refs_0_), channel_id=1, source_target_pairs={{2,0},{4,2},{6,4},{7,6},{5,7},{3,5},{1,3},{0,1},{10,8},{12,10},{14... | collective-permute-start | bytes 626696 | tf_op jit(solution)/shard_map/ppermute | solution.py:528
  10.9 7.3 %collective-permute-start.5 = (bf16[128,768]{1,0:T(8,128)(2,1)S(1)}, bf16[128,768]{1,0:T(8,128)(2,1)S(1)}, u32[]{:S(2)}, u32[]{:S(2)}) collective-permute-start(bf16[128,768]{1,0:T(8,128)(2,1)S(1)} %join.3.refs_1_), channel_id=1, source_target_pairs={{0,2},{2,4},{4,6},{6,7},{7,5},{5,3},{3,1},{1,0},{8,10},{10,12},{12... | collective-permute-start | bytes 589832 | tf_op jit(solution)/shard_map/ppermute | solution.py:525
  12.6 7.1 %collective-permute-start.6 = (bf16[128,768]{1,0:T(8,128)(2,1)S(1)}, bf16[128,768]{1,0:T(8,128)(2,1)S(1)}, u32[]{:S(2)}, u32[]{:S(2)}) collective-permute-start(bf16[128,768]{1,0:T(8,128)(2,1)S(1)} %join.3.refs_1_), channel_id=1, source_target_pairs={{2,0},{4,2},{6,4},{7,6},{5,7},{3,5},{1,3},{0,1},{10,8},{12,10},{14... | collective-permute-start | bytes 589832 | tf_op jit(solution)/shard_map/ppermute | solution.py:528
  15.7 9.0 %collective-permute-start.7 = (bf16[136,768]{1,0:T(8,128)(2,1)S(1)}, bf16[136,768]{1,0:T(8,128)(2,1)S(1)}, u32[]{:S(2)}, u32[]{:S(2)}) collective-permute-start(bf16[136,768]{1,0:T(8,128)(2,1)S(1)} %get-tuple-element.39.rest_0_), channel_id=1, source_target_pairs={{0,2},{2,4},{4,6},{6,7},{7,5},{5,3},{3,1},{1,0},{8,10},{10,12},{12... | collective-permute-start | bytes 626696 | tf_op jit(solution)/shard_map/ppermute | solution.py:525
  17.4 7.9 %collective-permute-start.8 = (bf16[136,768]{1,0:T(8,128)(2,1)S(1)}, bf16[136,768]{1,0:T(8,128)(2,1)S(1)}, u32[]{:S(2)}, u32[]{:S(2)}) collective-permute-start(bf16[136,768]{1,0:T(8,128)(2,1)S(1)} %get-tuple-element.41.rest_2_), channel_id=1, source_target_pairs={{2,0},{4,2},{6,4},{7,6},{5,7},{3,5},{1,3},{0,1},{10,8},{12,10},{14... | collective-permute-start | bytes 626696 | tf_op jit(solution)/shard_map/ppermute | solution.py:528
  19.7 7.9 %collective-permute-start.9 = (bf16[128,768]{1,0:T(8,128)(2,1)S(1)}, bf16[128,768]{1,0:T(8,128)(2,1)S(1)}, u32[]{:S(2)}, u32[]{:S(2)}) collective-permute-start(bf16[128,768]{1,0:T(8,128)(2,1)S(1)} %get-tuple-element.40.rest_1_), channel_id=1, source_target_pairs={{0,2},{2,4},{4,6},{6,7},{7,5},{5,3},{3,1},{1,0},{8,10},{10,12},{12... | collective-permute-start | bytes 589832 | tf_op jit(solution)/shard_map/ppermute | solution.py:525
  21.2 7.9 %collective-permute-start.10 = (bf16[128,768]{1,0:T(8,128)(2,1)S(1)}, bf16[128,768]{1,0:T(8,128)(2,1)S(1)}, u32[]{:S(2)}, u32[]{:S(2)}) collective-permute-start(bf16[128,768]{1,0:T(8,128)(2,1)S(1)} %get-tuple-element.42.rest_3_), channel_id=1, source_target_pairs={{2,0},{4,2},{6,4},{7,6},{5,7},{3,5},{1,3},{0,1},{10,8},{12,10},{14... | collective-permute-start | bytes 589832 | tf_op jit(solution)/shard_map/ppermute | solution.py:528
  25.3 8.9 %collective-permute-start.11 = (bf16[136,768]{1,0:T(8,128)(2,1)S(1)}, bf16[136,768]{1,0:T(8,128)(2,1)S(1)}, u32[]{:S(2)}, u32[]{:S(2)}) collective-permute-start(bf16[136,768]{1,0:T(8,128)(2,1)S(1)} %get-tuple-element.43.rest_0_), channel_id=1, source_target_pairs={{0,2},{2,4},{4,6},{6,7},{7,5},{5,3},{3,1},{1,0},{8,10},{10,12},{12... | collective-permute-start | bytes 626696 | tf_op jit(solution)/shard_map/ppermute | solution.py:525
  26.9 7.6 %collective-permute-start.12 = (bf16[136,768]{1,0:T(8,128)(2,1)S(1)}, bf16[136,768]{1,0:T(8,128)(2,1)S(1)}, u32[]{:S(2)}, u32[]{:S(2)}) collective-permute-start(bf16[136,768]{1,0:T(8,128)(2,1)S(1)} %get-tuple-element.45.rest_2_), channel_id=1, source_target_pairs={{2,0},{4,2},{6,4},{7,6},{5,7},{3,5},{1,3},{0,1},{10,8},{12,10},{14... | collective-permute-start | bytes 626696 | tf_op jit(solution)/shard_map/ppermute | solution.py:528
  29.2 7.5 %collective-permute-start.13 = (bf16[128,768]{1,0:T(8,128)(2,1)S(1)}, bf16[128,768]{1,0:T(8,128)(2,1)S(1)}, u32[]{:S(2)}, u32[]{:S(2)}) collective-permute-start(bf16[128,768]{1,0:T(8,128)(2,1)S(1)} %get-tuple-element.44.rest_1_), channel_id=1, source_target_pairs={{0,2},{2,4},{4,6},{6,7},{7,5},{5,3},{3,1},{1,0},{8,10},{10,12},{12... | collective-permute-start | bytes 589832 | tf_op jit(solution)/shard_map/ppermute | solution.py:525
  30.8 6.3 %collective-permute-start.14 = (bf16[128,768]{1,0:T(8,128)(2,1)S(1)}, bf16[128,768]{1,0:T(8,128)(2,1)S(1)}, u32[]{:S(2)}, u32[]{:S(2)}) collective-permute-start(bf16[128,768]{1,0:T(8,128)(2,1)S(1)} %get-tuple-element.46.rest_3_), channel_id=1, source_target_pairs={{2,0},{4,2},{6,4},{7,6},{5,7},{3,5},{1,3},{0,1},{10,8},{12,10},{14... | collective-permute-start | bytes 589832 | tf_op jit(solution)/shard_map/ppermute | solution.py:528
  34.5 8.3 %collective-permute-start.15 = (bf16[136,768]{1,0:T(8,128)(2,1)S(1)}, bf16[136,768]{1,0:T(8,128)(2,1)S(1)}, u32[]{:S(2)}, u32[]{:S(2)}) collective-permute-start(bf16[136,768]{1,0:T(8,128)(2,1)S(1)} %get-tuple-element.47.rest_0_), channel_id=1, source_target_pairs={{0,2},{2,4},{4,6},{6,7},{7,5},{5,3},{3,1},{1,0},{8,10},{10,12},{12... | collective-permute-start | bytes 626696 | tf_op jit(solution)/shard_map/ppermute | solution.py:525
  37.1 5.7 %collective-permute-start.16 = (bf16[128,768]{1,0:T(8,128)(2,1)S(1)}, bf16[128,768]{1,0:T(8,128)(2,1)S(1)}, u32[]{:S(2)}, u32[]{:S(2)}) collective-permute-start(bf16[128,768]{1,0:T(8,128)(2,1)S(1)} %get-tuple-element.50.rest_3_), channel_id=1, source_target_pairs={{2,0},{4,2},{6,4},{7,6},{5,7},{3,5},{1,3},{0,1},{10,8},{12,10},{14... | collective-permute-start | bytes 589832 | tf_op jit(solution)/shard_map/ppermute | solution.py:528
  41.5 10.8 %copy-start.8 = (s32[4]{0:T(128)S(1)}, s32[4]{0:T(128)}, u32[]{:S(2)}) copy-start(s32[4]{0:T(128)} %from_ref.1) | copy-start | bytes 52
  45.3 1.9 %collective-permute-start.17 = (bf16[64,768]{1,0:T(8,128)(2,1)S(1)}, bf16[64,768]{1,0:T(8,128)(2,1)S(1)}, u32[]{:S(2)}, u32[]{:S(2)}) collective-permute-start(bf16[64,768]{1,0:T(8,128)(2,1)S(1)} %get-tuple-element.52), channel_id=1, source_target_pairs={{0,8},{8,0},{16,24},{24,16},{1,9},{9,1},{17,25},{25,17},{2,10},{10... | collective-permute-start | bytes 294920 | tf_op jit(solution)/shard_map/ppermute | solution.py:497
  45.4 5.7 %collective-permute-start.18 = (bf16[64,768]{1,0:T(8,128)(2,1)S(1)}, bf16[64,768]{1,0:T(8,128)(2,1)S(1)}, u32[]{:S(2)}, u32[]{:S(2)}) collective-permute-start(bf16[64,768]{1,0:T(8,128)(2,1)S(1)} %get-tuple-element.53), channel_id=1, source_target_pairs={{0,16},{8,24},{16,0},{24,8},{1,17},{9,25},{17,1},{25,9},{2,18},{10... | collective-permute-start | bytes 294920 | tf_op jit(solution)/shard_map/ppermute | solution.py:497
  47.0 5.3 %collective-permute-start.19 = (bf16[64,768]{1,0:T(8,128)(2,1)S(1)}, bf16[64,768]{1,0:T(8,128)(2,1)S(1)}, u32[]{:S(2)}, u32[]{:S(2)}) collective-permute-start(bf16[64,768]{1,0:T(8,128)(2,1)S(1)} %get-tuple-element.54), channel_id=1, source_target_pairs={{0,24},{8,16},{16,8},{24,0},{1,25},{9,17},{17,9},{25,1},{2,26},{10... | collective-permute-start | bytes 294920 | tf_op jit(solution)/shard_map/ppermute | solution.py:497
  (5 other events, 15.2 us)
